TPU v7x, 32 devices: a whole 2x2x4 slice. The times are simulated.
32 devices in a mesh: group: 2 (over y), view: 4 (over z), depth: 2 (over x), row: 2 (over core).
Axes of the slice: x: 2, y: 2, z: 4, core: 2. Of those that a mesh axis runs over, the one named last changes fastest.
Arguments:
- features: float32 [4, 32, 8, 512], P('view', None, ('group', 'row')), parts along dimension 2, may hold values from -6 to 6
- cotangent: float32 [8, 32, 8, 512], P('depth', 'view', ('group', 'row')), parts along dimension 2, may hold values from -6 to 6
- src_row: int32 [4, 8, 8, 512], P('view', 'depth', ('group', 'row')), parts along dimension 2, may hold values from -2 to 4, as said below
- src_col: int32 [4, 8, 8, 512], P('view', 'depth', ('group', 'row')), parts along dimension 2, may hold values from 0 to 510
- fractions: int32 [2, 4, 8, 8, 512], P(None, 'view', 'depth', ('group', 'row')), parts along dimension 3, may hold values from 0 to 256
Outputs:
- grad_features: float32 [4, 32, 8, 512], P('view', None, ('group', 'row'), 'depth'), parts along dimension 2
There are 2 independent parts, one for each index of `group`. A program takes and returns all parts, laid end to end along the dimension named above; each array names one. Nothing has to cross between parts.
Inputs may be any that keep to these rules, and one draw needn't show every extreme that they name: src_row[v, d, y, x] lies between y - 2 and y + 1.
All inputs are finite; a program needn't handle non-finite values.
Results may differ from a plain program's by a relative error of at most 0.0003.
Values sent between devices are 32-bit elements; how exact they have to be, the bound alone decides.
No kernel may reach another device: no remote copies, remote signals or barrier semaphores. Data moves between devices by JAX's collectives and lax.ppermute only.
A program may use at most 64 MiB of HBM per device.

v0:
```python
import jax
import jax.numpy as jnp
from jax import lax
from jax.sharding import PartitionSpec as P

HALO = 2


def partner(shard, axis, apart):
    return lax.ppermute(shard, axis, [(i, i ^ 1 << apart) for i in range(lax.axis_size(axis))])


def with_halo(block, sides, width):
    for axis, dim in sides:
        count = lax.axis_size(axis)
        forward = [(i, i + 1) for i in range(count - 1)]
        backward = [(target, source) for source, target in forward]
        low = lax.ppermute(
            lax.slice_in_dim(block, block.shape[dim] - width, None, axis=dim), axis, forward
        )
        high = lax.ppermute(lax.slice_in_dim(block, 0, width, axis=dim), axis, backward)
        block = jnp.concatenate([low, block, high], axis=dim)
    return block


def sample(flattened, flat_index, frac_row, frac_col, width):

    def corner(shift_by):
        return jnp.take(flattened, flat_index + shift_by, axis=1)

    upper_mix = (1.0 - frac_col) * corner(0) + frac_col * corner(1)
    lower_mix = (1.0 - frac_col) * corner(width) + frac_col * corner(width + 1)
    mixed = (1.0 - frac_row) * upper_mix + frac_row * lower_mix
    return jnp.transpose(mixed, (1, 0, 2, 3))


def spread(grad_warp, flat_index, frac_row, frac_col, width, length):
    moved = jnp.transpose(grad_warp, (1, 0, 2, 3))
    channels = moved.shape[0]
    upper_part = (1.0 - frac_row) * moved
    lower_part = frac_row * moved
    result = jnp.zeros((channels, length), jnp.float32)
    result = result.at[:, flat_index].add((1.0 - frac_col) * upper_part)
    result = result.at[:, flat_index + 1].add(frac_col * upper_part)
    result = result.at[:, flat_index + width].add((1.0 - frac_col) * lower_part)
    result = result.at[:, flat_index + width + 1].add(frac_col * lower_part)
    return result


def fold_rims(grad_pad):
    upper_rim = grad_pad[:, :HALO]
    lower_rim = grad_pad[:, grad_pad.shape[1] - HALO :]
    interior = grad_pad[:, HALO : grad_pad.shape[1] - HALO]
    is_first = lax.axis_index("row") == 0
    outgoing = jnp.where(is_first, lower_rim, upper_rim)
    incoming = partner(outgoing, "row", 0)
    add_upper = jnp.where(is_first, 0.0, incoming)
    add_lower = jnp.where(is_first, incoming, 0.0)
    interior = interior.at[:, :HALO].add(add_upper)
    interior = interior.at[:, interior.shape[1] - HALO :].add(add_lower)
    return interior


def depth_reduce(partial_grad):
    return lax.psum_scatter(partial_grad, "depth", scatter_dimension=2, tiled=True)


def per_device(features, cotangent, src_row, src_col, fractions):
    channels = features.shape[1]
    row_count = features.shape[2]
    col_count = features.shape[3]
    padded = with_halo(features[0], (("row", 1),), HALO)
    padded_rows = row_count + 2 * HALO
    flattened = padded.reshape(channels, padded_rows * col_count)
    row_offset = lax.axis_index("row") * row_count
    flat_index = (src_row[0] - row_offset + HALO) * col_count + src_col[0]
    weights = fractions[:, 0].astype(jnp.float32) / 256.0
    warped = sample(flattened, flat_index, weights[0], weights[1], col_count)
    view_count = lax.axis_size("view") * features.shape[0]
    factor = 2.0 / view_count
    full_cotangent = lax.all_gather(cotangent, "view", axis=1, tiled=True)
    view_sum = lax.psum(warped, "view")
    average = view_sum / view_count
    grad_warp = factor * full_cotangent * (warped - average)
    spread_out = spread(
        grad_warp, flat_index, weights[0], weights[1], col_count, padded_rows * col_count
    )
    grad_pad = spread_out.reshape(channels, padded_rows, col_count)
    result = fold_rims(depth_reduce(grad_pad))
    return result[None]


def solution(mesh):
    in_specs = (
        P("view", None, ("group", "row"), None),
        P("depth", "view", ("group", "row"), None),
        P("view", "depth", ("group", "row"), None),
        P("view", "depth", ("group", "row"), None),
        P(None, "view", "depth", ("group", "row"), None),
    )
    out_specs = P("view", None, ("group", "row"), "depth")
    return jax.shard_map(
        per_device, mesh=mesh, in_specs=in_specs, out_specs=out_specs, check_vma=False
    )
```

profile of v0, /device:TPU:0, one launch (start us, length us, event | category | flops | bytes accessed | tf_op | source)
XLA Modules:
  0.0 254.7 jit_solution(4598418391159267502)
XLA Ops:
  6.5 2.4 collective-permute-start
  13.9 14.1 %gather_fusion = f32[4096,32]{1,0:T(8,128)} fusion(f32[32,3072]{0,1:T(8,128)S(1)} %bitcast.135, s32[4096]{0:T(1024)S(1)} %broadcast_clamp_fusion.3), kind=kCustom, calls=%fused_computation.clone | custom fusion | bytes 1064960 | tf_op jit(solution)/shard_map/jit(_take)/gather | solution.py:29
  28.0 1.9 copy.13
  29.9 14.1 %gather_fusion.1 = f32[4096,32]{1,0:T(8,128)} fusion(f32[32,3072]{0,1:T(8,128)S(1)} %bitcast.136, s32[4096]{0:T(1024)S(1)} %broadcast_clamp_fusion.2), kind=kCustom, calls=%fused_computation.1.clone | custom fusion | bytes 1064960 | tf_op jit(solution)/shard_map/jit(_take)/gather | solution.py:29
  44.0 1.9 copy.14
  45.9 14.1 %gather_fusion.2 = f32[4096,32]{1,0:T(8,128)} fusion(f32[32,3072]{0,1:T(8,128)S(1)} %bitcast.137, s32[4096]{0:T(1024)S(1)} %broadcast_clamp_fusion.1), kind=kCustom, calls=%fused_computation.2.clone | custom fusion | bytes 1064960 | tf_op jit(solution)/shard_map/jit(_take)/gather | solution.py:29
  60.0 1.9 copy.15
  61.9 14.1 %gather_fusion.3 = f32[4096,32]{1,0:T(8,128)} fusion(f32[32,3072]{0,1:T(8,128)S(1)} %bitcast.138, s32[4096]{0:T(1024)S(1)} %broadcast_clamp_fusion), kind=kCustom, calls=%fused_computation.3.clone | custom fusion | bytes 1064960 | tf_op jit(solution)/shard_map/jit(_take)/gather | solution.py:29
  76.0 1.9 copy.16
  77.9 1.7 fusion.5
  79.8 22.7 %all_gather.3 = f32[4,32,2,512]{3,2,1,0:T(2,128)S(1)} all-gather(f32[4,8,2,512]{3,2,1,0:T(2,128)S(1)} %copy-done), channel_id=1, replica_groups=mesh['group'=2,'view'=4,'depth'=2,'row'=2] {'view'}, dimensions={1}, use_global_device_ids=true | all-gather | bytes 655360 | tf_op jit(solution)/shard_map/all_gather | solution.py:81
  102.5 22.7 %all-reduce.2.cloned.1.call-done = f32[4,32,2,512]{3,2,1,0:T(2,128)} async-done(((f32[4,32,2,512]{3,2,1,0:T(2,128)}), f32[4,32,2,512]{3,2,1,0:T(2,128)}) %all-reduce.2.cloned.1.call-update) | async-done | bytes 524304 | tf_op jit(solution)/shard_map/psum | solution.py:82
  125.2 1.8 multiply_bitcast_fusion
  127.6 1.8 copy.26
  129.4 1.7 copy.27
  131.1 1.8 copy.28
  132.9 1.7 copy.29
  134.6 23.0 %scatter_custom_fusion = f32[32,3072]{0,1:T(8,128)S(1)} fusion(s32[4096]{0:T(1024)S(1)} %bitcast.158, f32[4096,32]{1,0:T(8,128)} %bitcast.147, f32[]{:T(128)} %constant.99.clone.1), kind=kCustom, calls=%fused_computation.8 | custom fusion | flops 131072 | bytes 393728 | tf_op jit(solution)/shard_map/scatter-add | solution.py:43
  157.6 23.3 %scatter_fusion = f32[32,3072]{0,1:T(8,128)S(1)} fusion(f32[32,3072]{0,1:T(8,128)S(1)} %scatter_custom_fusion, s32[4096]{0:T(1024)S(1)} %bitcast.153, f32[4096,32]{1,0:T(8,128)} %bitcast.142), kind=kCustom, calls=%fused_computation.5 | custom fusion | flops 131072 | bytes 1589248 | tf_op jit(solution)/shard_map/scatter-add | solution.py:44
  180.9 23.3 %scatter_fusion.1 = f32[32,3072]{0,1:T(8,128)S(1)} fusion(f32[32,3072]{0,1:T(8,128)S(1)} %scatter_fusion, s32[4096]{0:T(1024)S(1)} %bitcast.152, f32[4096,32]{1,0:T(8,128)} %bitcast.141), kind=kCustom, calls=%fused_computation.6 | custom fusion | flops 131072 | bytes 1589248 | tf_op jit(solution)/shard_map/scatter-add | solution.py:45
  204.2 23.4 %scatter_fusion.2 = f32[32,3072]{0,1:T(8,128)S(1)} fusion(f32[32,3072]{0,1:T(8,128)S(1)} %scatter_fusion.1, s32[4096]{0:T(1024)S(1)} %bitcast.151, f32[4096,32]{1,0:T(8,128)} %bitcast.140), kind=kCustom, calls=%fused_computation.7 | custom fusion | flops 131072 | bytes 1589248 | tf_op jit(solution)/shard_map/scatter-add | solution.py:46
  227.6 1.5 copy.25
  229.1 14.7 %reduce-scatter.2.cloned.1.call-done = f32[32,6,256]{2,1,0:T(8,128)} async-done(((f32[32,6,512]{2,1,0:T(8,128)}), f32[32,6,256]{2,1,0:T(8,128)}) %reduce-scatter.2.cloned.1.call-update) | async-done | bytes 196624 | tf_op jit(solution)/shard_map/reduce_scatter | solution.py:65
  246.2 1.6 fusion.9
  (33 shorter events, 8.1 us)
Async XLA Ops:
  6.5 118.6 %all-reduce.2.cloned.1.call-start = ((), (), s32[]{:S(2)}) async-start(), calls=%async_computation.1 | async-start | bytes 1048576 | tf_op jit(solution)/shard_map/psum | solution.py:82
  6.5 5.5 %collective-permute-start = (f32[32,2,512]{2,1,0:T(2,128)}, f32[32,2,512]{2,1,0:T(2,128)S(1)}, u32[]{:S(2)}, u32[]{:S(2)}) collective-permute-start(f32[32,2,512]{2,1,0:T(2,128)} %bitcast.148), channel_id=1, source_target_pairs={{0,1},{2,3},{4,5},{6,7},{8,9},{10,11},{12,13},{14,15},{16,17},{18,... | collective-permute-start | bytes 393224 | tf_op jit(solution)/shard_map/ppermute | solution.py:18
  8.9 3.5 %collective-permute-start.1 = (f32[32,2,512]{2,1,0:T(2,128)}, f32[32,2,512]{2,1,0:T(2,128)S(1)}, u32[]{:S(2)}, u32[]{:S(2)}) collective-permute-start(f32[32,2,512]{2,1,0:T(2,128)} %bitcast.149), channel_id=1, source_target_pairs={{1,0},{3,2},{5,4},{7,6},{9,8},{11,10},{13,12},{15,14},{17,16},{19,... | collective-permute-start | bytes 393224 | tf_op jit(solution)/shard_map/ppermute | solution.py:21
  77.9 1.9 copy-start
  79.7 164.1 %reduce-scatter.2.cloned.1.call-start = ((), (), s32[]{:S(2)}) async-start(), calls=%async_computation.2 | async-start | bytes 786432 | tf_op jit(solution)/shard_map/reduce_scatter | solution.py:65
  244.9 1.3 collective-permute-start.2
Sparse Core Ops, SparseCore 0:
  79.8 45.3 all-reduce.1
  229.2 14.5 reduce-scatter.1
where the time goes:
time: 255 us
  other arithmetic  103 us (40%)
  local copies, waits for them, and re-layouts  72.9 us (29%)
  waiting for transfers between devices  38.9 us (15%)
  blocking collectives  22.7 us (9%)
  between operations  13.7 us (5%)
  starting transfers between devices  3.76 us (1%)
    gather x8, local copies, waits for them, and re-layouts, corner(): return jnp.take(flattened, flat_index + shift_by, axis=1)  63.9 us
    scatter-add x1, other arithmetic, spread(): result = result.at[:, flat_index + width + 1].add(frac_col * lower_part)  23.4 us
    scatter-add x1, other arithmetic, spread(): result = result.at[:, flat_index + 1].add(frac_col * upper_part)  23.3 us
    scatter-add x1, other arithmetic, spread(): result = result.at[:, flat_index + width].add((1.0 - frac_col) * lower_part)  23.3 us
    scatter-add x1, other arithmetic, spread(): result = result.at[:, flat_index].add((1.0 - frac_col) * upper_part)  23 us
    all_gather x1, blocking collectives, per_device(): full_cotangent = lax.all_gather(cotangent, 'view', axis=1, tiled=True)  22.7 us
    psum x1, waiting for transfers between devices, per_device(): view_sum = lax.psum(warped, 'view')  22.7 us
    reduce_scatter x1, waiting for transfers between devices, depth_reduce(): lax.psum_scatter(partial_grad, 'depth', scatter_dimension=2, tiled=True)  14.7 us
  transfers between devices with their start and end apart: 5, of which 4 were waited for; matrix products, arithmetic and copies ran while one was open for 1% of the time, Pallas kernels for 0%

commit v1 on v0

v1 whole, which is shorter than its diff:
```python
import functools

import jax
import jax.numpy as jnp
from jax import lax
from jax.experimental import pallas as pl
from jax.experimental.pallas import tpu as pltpu
from jax.sharding import PartitionSpec as P

HALO = 2
BF = jnp.bfloat16
F32 = jnp.float32
VMEM = pl.BlockSpec(memory_space=pltpu.VMEM)


def peer(me, k, count):
    if count & (count - 1) == 0:
        return lax.bitwise_xor(me, jnp.int32(k))
    return lax.rem(me + k, jnp.int32(count))


def pairs_of(count, k):
    if count & (count - 1) == 0:
        return [(i, i ^ k) for i in range(count)]
    return [(i, (i + k) % count) for i in range(count)]


def to_peer(block, axis, k):
    return lax.ppermute(block, axis, pairs_of(lax.axis_size(axis), k))


def to_origin(block, axis, k):
    return lax.ppermute(block, axis, [(b, a) for a, b in pairs_of(lax.axis_size(axis), k)])


def call(body, out_shape, *args, scratch=(), flops=0):
    moved = sum(a.size * 4 for a in args)
    many = isinstance(out_shape, (tuple, list))
    return pl.pallas_call(
        body,
        out_shape=out_shape,
        in_specs=[VMEM] * len(args),
        out_specs=[VMEM] * len(out_shape) if many else VMEM,
        scratch_shapes=scratch,
        cost_estimate=pl.CostEstimate(flops=flops, bytes_accessed=moved, transcendentals=0),
        compiler_params=pltpu.CompilerParams(vmem_limit_bytes=48 << 20),
    )(*args)


def pack_kernel(views, share, feat_ref, row_ref, col_ref, frac_ref, *outs):
    me = lax.axis_index("view")
    planes, rows = row_ref.shape[1:3]
    first = lax.axis_index("row") * rows
    width = feat_ref.shape[3]
    lanes = outs[0].shape[1]
    for k in range(views):
        base = peer(me, k, views) * share
        for y in range(rows):
            if share % 8:
                outs[k][y] = jnp.zeros((lanes, width), F32)
            for c in range(share):
                outs[k][y, c : c + 1, :] = feat_ref[0, base + c, y : y + 1, :]
        for d in range(planes):
            for y in range(rows):
                at = d * rows + y
                page, line = divmod(at, lanes)
                pages = -(-planes * rows // lanes)
                top = (row_ref[0, d, y : y + 1, :] - (first + y - HALO)).astype(F32)
                col = col_ref[0, d, y : y + 1, :].astype(F32)
                fy = frac_ref[0, 0, d, y : y + 1, :].astype(F32) / 256.0
                fx = frac_ref[1, 0, d, y : y + 1, :].astype(F32) / 256.0
                for kind, value in enumerate((top, col, fy, fx)):
                    outs[k][rows + kind * pages + page, line : line + 1, :] = value


def split(x):
    high = x.astype(BF)
    return high, (x - high.astype(F32)).astype(BF)


def main_kernel(views, planes, rows, share, *refs):
    packets, halo_ref, cot_ref = refs[:views], refs[views], refs[views + 1]
    own_ref, rim_ref, grad_ref, w_ref, f_ref = refs[views + 2 :]
    lanes, width = packets[0].shape[1:]
    pages = -(-planes * rows // lanes)
    padded = rows + 2 * HALO
    window = 2 * HALO + 1
    is_first = lax.axis_index("row") == 0
    for v in range(views):
        for r in range(padded):
            if r < HALO:
                x = jnp.where(is_first, 0.0, halo_ref[v, rows - HALO + r])
            elif r < HALO + rows:
                x = packets[v][r - HALO]
            else:
                x = jnp.where(is_first, halo_ref[v, r - HALO - rows], 0.0)
            f_ref[v, 2 * lanes * r : 2 * lanes * (r + 1)] = jnp.concatenate(split(x), axis=0)
    grad_ref[...] = jnp.zeros_like(grad_ref)
    block = 256

    def plane(d, carry):
        for y in range(rows):
            page, line = (d * rows + y) // lanes, (d * rows + y) % lanes
            warped, row_weights = [], []
            for v in range(views):
                top, col, fy, fx = (
                    packets[v][rows + kind * pages + page, pl.ds(line, 1), :] for kind in range(4)
                )
                left, right = (1.0 - fx).astype(BF), fx.astype(BF)
                for start in range(0, width, block):
                    it = lax.broadcasted_iota(jnp.int32, (block, width), 0).astype(F32).astype(BF)
                    here = jnp.clip(col - start, -2.0, float(block)).astype(BF)
                    after = jnp.clip(col - (start - 1), -2.0, float(block)).astype(BF)
                    w_ref[v, start : start + block, :] = jnp.where(
                        it == here, left, jnp.where(it == after, right, jnp.zeros((), BF))
                    )
                a = f_ref[v, 2 * lanes * y : 2 * lanes * (y + window)]
                p = jnp.dot(a, w_ref[v], preferred_element_type=F32)
                rw = [
                    jnp.where(top == i, 1.0 - fy, jnp.where(top == i - 1, fy, 0.0))
                    for i in range(window)
                ]
                total = 0.0
                for i in range(window):
                    at = 2 * lanes * i
                    total = total + rw[i] * (p[at : at + lanes] + p[at + lanes : at + 2 * lanes])
                warped.append(total)
                row_weights.append(rw)
            average = sum(warped) / views
            cot = cot_ref[d, :, y, :]
            if share % 8:
                cot = jnp.broadcast_to(cot, (lanes, width)) if share == 1 else jnp.pad(cot, ((0, lanes - share), (0, 0)))
            for v in range(views):
                g = (2.0 / views) * cot * (warped[v] - average)
                parts = []
                for i in range(window):
                    parts += split(row_weights[v][i] * g)
                p = lax.dot_general(
                    jnp.concatenate(parts, axis=0),
                    w_ref[v],
                    (((1,), (1,)), ((), ())),
                    preferred_element_type=F32,
                )
                for i in range(window):
                    at = 2 * lanes * i
                    grad_ref[v, y + i] += p[at : at + lanes] + p[at + lanes : at + 2 * lanes]
        return carry

    lax.fori_loop(0, planes, plane, 0, unroll=views <= 8)
    for v in range(views):
        for r in range(rows):
            own_ref[v, r] = grad_ref[v, HALO + r]
        for r in range(HALO):
            rim_ref[v, r] = jnp.where(is_first, grad_ref[v, HALO + rows + r], grad_ref[v, r])


def fold_kernel(depths, own_ref, rim_ref, *outs):
    views, rows, lanes, width = own_ref.shape
    part = width // depths
    me = lax.axis_index("depth")
    for k in range(depths):
        at = pl.multiple_of(peer(me, k, depths) * part, part)
        for v in range(views):
            for r in range(rows):
                outs[k][v, r] = own_ref[v, r, :, pl.ds(at, part)]
    is_first = lax.axis_index("row") == 0
    for k in range(depths):
        at = pl.multiple_of(peer(me, k, depths) * part, part)
        for v in range(views):
            for r in range(HALO):
                upper, lower = r, rows - HALO + r
                value = rim_ref[v, r, :, pl.ds(at, part)]
                outs[k][v, upper] += jnp.where(is_first, 0.0, value)
                outs[k][v, lower] += jnp.where(is_first, value, 0.0)


def sum_kernel(depths, views, *refs):
    for v in range(views):
        total = refs[0][v]
        for k in range(1, depths):
            total = total + refs[k][v]
        refs[depths + v][...] = total


def place_kernel(views, share, *refs):
    out_ref = refs[views]
    me = lax.axis_index("view")
    rows = out_ref.shape[2]
    for k in range(views):
        base = peer(me, k, views) * share
        for c in range(share):
            for r in range(rows):
                out_ref[0, base + c, r : r + 1, :] = refs[k][r, c : c + 1, :]


def per_device(features, cotangent, src_row, src_col, fractions):
    views = lax.axis_size("view")
    depths = lax.axis_size("depth")
    channels, rows, width = features.shape[1:]
    planes, share = cotangent.shape[:2]
    lanes = -(-share // 8) * 8
    pages = -(-planes * rows // lanes)
    packet = jax.ShapeDtypeStruct((rows + 4 * pages, lanes, width), F32)
    packets = call(
        functools.partial(pack_kernel, views, share),
        [packet] * views,
        features, src_row, src_col, fractions,
    )
    packets = [packets[0]] + [to_peer(packets[k], "view", k) for k in range(1, views)]
    halo = to_peer(jnp.stack([p[:rows] for p in packets]), "row", 1)
    volume = (views, rows, lanes, width)
    own, rim = call(
        functools.partial(main_kernel, views, planes, rows, share),
        [
            jax.ShapeDtypeStruct(volume, F32),
            jax.ShapeDtypeStruct((views, HALO, lanes, width), F32),
        ],
        *packets, halo, cotangent,
        scratch=[
            pltpu.VMEM((views, rows + 2 * HALO, lanes, width), F32),
            pltpu.VMEM((views, width, width), BF),
            pltpu.VMEM((views, 2 * lanes * (rows + 2 * HALO), width), BF),
        ],
        flops=8 * views * planes * rows * width * width * 5 * lanes,
    )
    rim = to_peer(rim, "row", 1)
    part = width // depths
    halves = call(
        functools.partial(fold_kernel, depths),
        [jax.ShapeDtypeStruct((views, rows, lanes, part), F32)] * depths,
        own, rim,
    )
    halves = [halves[0]] + [to_peer(halves[k], "depth", k) for k in range(1, depths)]
    pieces = call(
        functools.partial(sum_kernel, depths, views),
        [jax.ShapeDtypeStruct((rows, lanes, part), F32)] * views,
        *halves,
    )
    order = [pieces[0]] + [to_origin(pieces[k], "view", k) for k in range(1, views)]
    return call(
        functools.partial(place_kernel, views, share),
        jax.ShapeDtypeStruct((1, channels, rows, part), F32),
        *order,
    )


def solution(mesh):
    in_specs = (
        P("view", None, ("group", "row"), None),
        P("depth", "view", ("group", "row"), None),
        P("view", "depth", ("group", "row"), None),
        P("view", "depth", ("group", "row"), None),
        P(None, "view", "depth", ("group", "row"), None),
    )
    out_specs = P("view", None, ("group", "row"), "depth")
    return jax.shard_map(
        per_device, mesh=mesh, in_specs=in_specs, out_specs=out_specs, check_vma=False
    )
```

time: 255 us -> 42.8 us (0.17)
  other arithmetic: 103 us -> 0.01 us
  local copies, waits for them, and re-layouts: 72.9 us -> 3.11 us
  blocking collectives: 22.7 us -> 0 us
  waiting for transfers between devices: 38.9 us -> 17.3 us
  between operations: 13.7 us -> 0.06 us
  Pallas kernels: 0 us -> 9.94 us
  starting transfers between devices: 3.76 us -> 12 us
    scatter-add x4 -> x0, other arithmetic: 93 us -> none  [the longest x1 23.4 us: spread(): result = result.at[:, flat_index + width + 1].add(frac_col * lower_part)]
    gather x8 -> x0, local copies, waits for them, and re-layouts: 63.9 us -> none  [corner(): return jnp.take(flattened, flat_index + shift_by, axis=1)]
    all_gather x1 -> x0, blocking collectives: 22.7 us -> none  [per_device(): full_cotangent = lax.all_gather(cotangent, 'view', axis=1, tiled=True)]
    psum x1 -> x0, waiting for transfers between devices: 22.7 us -> none  [per_device(): view_sum = lax.psum(warped, 'view')]
    ppermute x3 -> x9, waiting for transfers between devices: 1.56 us -> 17.3 us  [the longest x6 13.1 us: to_peer(): return lax.ppermute(block, axis, pairs_of(lax.axis_size(axis), k))]
    reduce_scatter x1 -> x0, waiting for transfers between devices: 14.7 us -> none  [depth_reduce(): lax.psum_scatter(partial_grad, 'depth', scatter_dimension=2, tiled=True)]
    pallas_call x0 -> x5, Pallas kernels: none -> 9.94 us  [call(): pl.pallas_call(body, out_shape=out_shape, in_specs=[VMEM] * len(args), ou...]
    ppermute x3 -> x9, starting transfers between devices: 3.72 us -> 12 us  [the longest x6 7.53 us: to_peer(): return lax.ppermute(block, axis, pairs_of(lax.axis_size(axis), k))]
  transfers between devices with their start and end apart: 5 -> 9, of which waited for: 4 -> 7; matrix products, arithmetic and copies ran while one was open for 1% -> 0% of each run, Pallas kernels for 0% -> 0%
where the time goes in v1:
time: 42.8 us; the launch traced here: 42.4 us
  waiting for transfers between devices  17.3 us (40%)
  starting transfers between devices  12 us (28%)
  Pallas kernels  9.94 us (23%)
  local copies, waits for them, and re-layouts  3.11 us (7%)
    ppermute x6, waiting for transfers between devices, to_peer(): return lax.ppermute(block, axis, pairs_of(lax.axis_size(axis), k))  13.1 us
    pallas_call x5, Pallas kernels, call(): pl.pallas_call(body, out_shape=out_shape, in_specs=[VMEM] * len(args), ou...  9.94 us
    ppermute x6, starting transfers between devices, to_peer(): return lax.ppermute(block, axis, pairs_of(lax.axis_size(axis), k))  7.53 us
    ppermute x3, starting transfers between devices, to_origin(): lax.ppermute(block, axis, [(b, a) for a, b in pairs_of(lax.axis_size(axis...  4.45 us
    ppermute x3, waiting for transfers between devices, to_origin(): lax.ppermute(block, axis, [(b, a) for a, b in pairs_of(lax.axis_size(axis...  4.19 us
    unnamed x10, local copies, waits for them, and re-layouts  3.1 us
  transfers between devices with their start and end apart: 9, of which 7 were waited for; matrix products, arithmetic and copies ran while one was open for 0% of the time, Pallas kernels for 0%

profile of v1, /device:TPU:0, one launch (start us, length us, event | category | flops | bytes accessed | tf_op | source)
XLA Modules:
  0.0 42.4 jit_solution(5769757371506935139)
XLA Ops:
  0.0 0.9 %copy-done = f32[1,32,2,512]{3,2,1,0:T(2,128)S(1)} copy-done((f32[1,32,2,512]{3,2,1,0:T(2,128)S(1)}, f32[1,32,2,512]{3,2,1,0:T(2,128)}, u32[]{:S(2)}) %copy-start) | copy-done | bytes 131096
  0.9 0.8 %copy-done.1 = s32[2,1,4,2,512]{4,3,2,1,0:T(2,128)S(1)} copy-done((s32[2,1,4,2,512]{4,3,2,1,0:T(2,128)S(1)}, s32[2,1,4,2,512]{4,3,2,1,0:T(2,128)}, u32[]{:S(2)}) %copy-start.1) | copy-done | bytes 32792
  1.7 0.7 %copy-done.2 = s32[1,4,2,512]{3,2,1,0:T(2,128)S(1)} copy-done((s32[1,4,2,512]{3,2,1,0:T(2,128)S(1)}, s32[1,4,2,512]{3,2,1,0:T(2,128)}, u32[]{:S(2)}) %copy-start.2) | copy-done | bytes 16408
  2.4 0.7 %copy-done.3 = s32[1,4,2,512]{3,2,1,0:T(2,128)S(1)} copy-done((s32[1,4,2,512]{3,2,1,0:T(2,128)S(1)}, s32[1,4,2,512]{3,2,1,0:T(2,128)}, u32[]{:S(2)}) %copy-start.3) | copy-done | bytes 16408
  3.1 0.1 shard_map.55
  3.2 3.1 %collective-permute-start = (f32[6,8,512]{2,1,0:T(8,128)S(1)}, f32[6,8,512]{2,1,0:T(8,128)S(1)}, u32[]{:S(2)}, u32[]{:S(2)}) collective-permute-start(f32[6,8,512]{2,1,0:T(8,128)S(1)} %get-tuple-element.18), channel_id=1, source_target_pairs={{0,4},{4,0},{8,12},{12,8},{1,5},{5,1},{9,13},{13,9},{2,6},{6,2},{1... | collective-permute-start | bytes 294920 | tf_op jit(solution)/shard_map/ppermute | solution.py:29
  6.3 2.6 %collective-permute-start.1 = (f32[6,8,512]{2,1,0:T(8,128)S(1)}, f32[6,8,512]{2,1,0:T(8,128)S(1)}, u32[]{:S(2)}, u32[]{:S(2)}) collective-permute-start(f32[6,8,512]{2,1,0:T(8,128)S(1)} %get-tuple-element.19), channel_id=1, source_target_pairs={{0,8},{4,12},{8,0},{12,4},{1,9},{5,13},{9,1},{13,5},{2,10},{6,14},... | collective-permute-start | bytes 294920 | tf_op jit(solution)/shard_map/ppermute | solution.py:29
  8.9 0.2 collective-permute-done.refs_1_
  9.1 7.6 %collective-permute-done.1.refs_2_ = f32[6,8,512]{2,1,0:T(8,128)S(1)} collective-permute-done((f32[6,8,512]{2,1,0:T(8,128)S(1)}, f32[6,8,512]{2,1,0:T(8,128)S(1)}, u32[]{:S(2)}, u32[]{:S(2)}) %collective-permute-start.1) | collective-permute-done | bytes 98336 | tf_op jit(solution)/shard_map/ppermute | solution.py:29
  16.7 0.0 copy-start.4
  16.7 0.1 collective-permute-start.3
  16.8 1.3 %collective-permute-done.3.refs_4_ = f32[4,2,8,512]{3,2,1,0:T(8,128)S(1)} collective-permute-done((f32[4,2,8,512]{3,2,1,0:T(8,128)S(1)}, f32[4,2,8,512]{3,2,1,0:T(8,128)S(1)}, u32[]{:S(2)}, u32[]{:S(2)}) %collective-permute-start.3) | collective-permute-done | bytes 131104 | tf_op jit(solution)/shard_map/ppermute | solution.py:29
  18.2 9.2 %shard_map.56 = (f32[4,2,8,512]{3,2,1,0:T(8,128)S(1)}, f32[4,2,8,512]{3,2,1,0:T(8,128)S(1)}) custom-call(f32[6,8,512]{2,1,0:T(8,128)S(1)} %get-tuple-element.17.refs_0_, f32[6,8,512]{2,1,0:T(8,128)S(1)} %collective-permute-done.refs_1_, f32[6,8,512]{2,1,0:T(8,128)S(1)} %collective-permute-done.1.refs_2_, f32[6,8,512]{2,1,0:T(8,128)S(1)} %collective-permute-done.2.refs_3_, ...), custom_call_target="tpu_custom_call" | custom-call | flops 2684354560 | bytes 655360 | tf_op jit(solution)/shard_map/pallas_call | solution.py:39
  27.3 0.2 collective-permute-start.4
  27.5 1.2 %collective-permute-done.4.rim_ref = f32[4,2,8,512]{3,2,1,0:T(8,128)S(1)} collective-permute-done((f32[4,2,8,512]{3,2,1,0:T(8,128)S(1)}, f32[4,2,8,512]{3,2,1,0:T(8,128)S(1)}, u32[]{:S(2)}, u32[]{:S(2)}) %collective-permute-start.4) | collective-permute-done | bytes 131104 | tf_op jit(solution)/shard_map/ppermute | solution.py:29
  28.8 1.6 %collective-permute-start.5 = (f32[4,2,8,256]{3,2,1,0:T(8,128)S(1)}, f32[4,2,8,256]{3,2,1,0:T(8,128)S(1)}, u32[]{:S(2)}, u32[]{:S(2)}) collective-permute-start(f32[4,2,8,256]{3,2,1,0:T(8,128)S(1)} %get-tuple-element.24), channel_id=1, source_target_pairs={{0,2},{2,0},{1,3},{3,1},{4,6},{6,4},{5,7},{7,5},{8,10},{10,8},{9,1... | collective-permute-start | bytes 196616 | tf_op jit(solution)/shard_map/ppermute | solution.py:29
  30.3 2.8 %collective-permute-done.5.refs_1_ = f32[4,2,8,256]{3,2,1,0:T(8,128)S(1)} collective-permute-done((f32[4,2,8,256]{3,2,1,0:T(8,128)S(1)}, f32[4,2,8,256]{3,2,1,0:T(8,128)S(1)}, u32[]{:S(2)}, u32[]{:S(2)}) %collective-permute-start.5) | collective-permute-done | bytes 65568 | tf_op jit(solution)/shard_map/ppermute | solution.py:29
  33.1 1.6 %collective-permute-start.6 = (f32[2,8,256]{2,1,0:T(8,128)S(1)}, f32[2,8,256]{2,1,0:T(8,128)S(1)}, u32[]{:S(2)}, u32[]{:S(2)}) collective-permute-start(f32[2,8,256]{2,1,0:T(8,128)S(1)} %get-tuple-element.26), channel_id=1, source_target_pairs={{4,0},{0,4},{12,8},{8,12},{5,1},{1,5},{13,9},{9,13},{6,2},{2,6},{1... | collective-permute-start | bytes 49160 | tf_op jit(solution)/shard_map/ppermute | solution.py:33
  34.8 1.5 %collective-permute-start.7 = (f32[2,8,256]{2,1,0:T(8,128)S(1)}, f32[2,8,256]{2,1,0:T(8,128)S(1)}, u32[]{:S(2)}, u32[]{:S(2)}) collective-permute-start(f32[2,8,256]{2,1,0:T(8,128)S(1)} %get-tuple-element.27), channel_id=1, source_target_pairs={{8,0},{12,4},{0,8},{4,12},{9,1},{13,5},{1,9},{5,13},{10,2},{14,6},... | collective-permute-start | bytes 49160 | tf_op jit(solution)/shard_map/ppermute | solution.py:33
  36.2 1.3 %collective-permute-start.8 = (f32[2,8,256]{2,1,0:T(8,128)S(1)}, f32[2,8,256]{2,1,0:T(8,128)S(1)}, u32[]{:S(2)}, u32[]{:S(2)}) collective-permute-start(f32[2,8,256]{2,1,0:T(8,128)S(1)} %get-tuple-element.28), channel_id=1, source_target_pairs={{12,0},{8,4},{4,8},{0,12},{13,1},{9,5},{5,9},{1,13},{14,2},{10,6},... | collective-permute-start | bytes 49160 | tf_op jit(solution)/shard_map/ppermute | solution.py:33
  37.6 0.0 collective-permute-done.6.refs_1_
  37.6 2.0 %collective-permute-done.7.refs_2_ = f32[2,8,256]{2,1,0:T(8,128)S(1)} collective-permute-done((f32[2,8,256]{2,1,0:T(8,128)S(1)}, f32[2,8,256]{2,1,0:T(8,128)S(1)}, u32[]{:S(2)}, u32[]{:S(2)}) %collective-permute-start.7) | collective-permute-done | bytes 16416 | tf_op jit(solution)/shard_map/ppermute | solution.py:33
  39.6 2.2 %collective-permute-done.8.refs_3_ = f32[2,8,256]{2,1,0:T(8,128)S(1)} collective-permute-done((f32[2,8,256]{2,1,0:T(8,128)S(1)}, f32[2,8,256]{2,1,0:T(8,128)S(1)}, u32[]{:S(2)}, u32[]{:S(2)}) %collective-permute-start.8) | collective-permute-done | bytes 16416 | tf_op jit(solution)/shard_map/ppermute | solution.py:33
  41.7 0.7 %shard_map.59 = f32[1,32,2,256]{3,2,1,0:T(2,128)} custom-call(f32[2,8,256]{2,1,0:T(8,128)S(1)} %get-tuple-element.25.refs_0_, f32[2,8,256]{2,1,0:T(8,128)S(1)} %collective-permute-done.6.refs_1_, f32[2,8,256]{2,1,0:T(8,128)S(1)} %collective-permute-done.7.refs_2_, f32[2,8,256]{2,1,0:T(8,128)S(1)} %collective-permute-done.8.refs_3_), custom_call_target="tpu_custom_call" | custom-call | bytes 65536 | tf_op jit(solution)/shard_map/pallas_call | solution.py:39
  (14 shorter events, 0.1 us)
Async XLA Ops:
  0.0 0.9 %copy-start = (f32[1,32,2,512]{3,2,1,0:T(2,128)S(1)}, f32[1,32,2,512]{3,2,1,0:T(2,128)}, u32[]{:S(2)}) copy-start(f32[1,32,2,512]{3,2,1,0:T(2,128)} %feat_ref.1) | copy-start | bytes 393220
  0.9 0.8 %copy-start.1 = (s32[2,1,4,2,512]{4,3,2,1,0:T(2,128)S(1)}, s32[2,1,4,2,512]{4,3,2,1,0:T(2,128)}, u32[]{:S(2)}) copy-start(s32[2,1,4,2,512]{4,3,2,1,0:T(2,128)} %frac_ref.1) | copy-start | bytes 98308
  1.7 0.7 %copy-start.2 = (s32[1,4,2,512]{3,2,1,0:T(2,128)S(1)}, s32[1,4,2,512]{3,2,1,0:T(2,128)}, u32[]{:S(2)}) copy-start(s32[1,4,2,512]{3,2,1,0:T(2,128)} %row_ref.1) | copy-start | bytes 49156
  2.4 0.7 %copy-start.3 = (s32[1,4,2,512]{3,2,1,0:T(2,128)S(1)}, s32[1,4,2,512]{3,2,1,0:T(2,128)}, u32[]{:S(2)}) copy-start(s32[1,4,2,512]{3,2,1,0:T(2,128)} %col_ref.1) | copy-start | bytes 49156
  3.2 5.9 %collective-permute-start = (f32[6,8,512]{2,1,0:T(8,128)S(1)}, f32[6,8,512]{2,1,0:T(8,128)S(1)}, u32[]{:S(2)}, u32[]{:S(2)}) collective-permute-start(f32[6,8,512]{2,1,0:T(8,128)S(1)} %get-tuple-element.18), channel_id=1, source_target_pairs={{0,4},{4,0},{8,12},{12,8},{1,5},{5,1},{9,13},{13,9},{2,6},{6,2},{1... | collective-permute-start | bytes 294920 | tf_op jit(solution)/shard_map/ppermute | solution.py:29
  6.3 10.4 %collective-permute-start.1 = (f32[6,8,512]{2,1,0:T(8,128)S(1)}, f32[6,8,512]{2,1,0:T(8,128)S(1)}, u32[]{:S(2)}, u32[]{:S(2)}) collective-permute-start(f32[6,8,512]{2,1,0:T(8,128)S(1)} %get-tuple-element.19), channel_id=1, source_target_pairs={{0,8},{4,12},{8,0},{12,4},{1,9},{5,13},{9,1},{13,5},{2,10},{6,14},... | collective-permute-start | bytes 294920 | tf_op jit(solution)/shard_map/ppermute | solution.py:29
  8.9 7.8 %collective-permute-start.2 = (f32[6,8,512]{2,1,0:T(8,128)S(1)}, f32[6,8,512]{2,1,0:T(8,128)S(1)}, u32[]{:S(2)}, u32[]{:S(2)}) collective-permute-start(f32[6,8,512]{2,1,0:T(8,128)S(1)} %get-tuple-element.20), channel_id=1, source_target_pairs={{0,12},{4,8},{8,4},{12,0},{1,13},{5,9},{9,5},{13,1},{2,14},{6,10},... | collective-permute-start | bytes 294920 | tf_op jit(solution)/shard_map/ppermute | solution.py:29
  16.7 1.4 %copy-start.4 = (f32[4,8,2,512]{3,2,1,0:T(2,128)S(1)}, f32[4,8,2,512]{3,2,1,0:T(2,128)}, u32[]{:S(2)}) copy-start(f32[4,8,2,512]{3,2,1,0:T(2,128)} %refs_5_.1) | copy-start | bytes 393220
  16.7 1.4 %collective-permute-start.3 = (f32[4,2,8,512]{3,2,1,0:T(8,128)S(1)}, f32[4,2,8,512]{3,2,1,0:T(8,128)S(1)}, u32[]{:S(2)}, u32[]{:S(2)}) collective-permute-start(f32[4,2,8,512]{3,2,1,0:T(8,128)S(1)} %pad_maximum_fusion), channel_id=1, source_target_pairs={{0,1},{1,0},{2,3},{3,2},{4,5},{5,4},{6,7},{7,6},{8,9},{9,8},{10,11... | collective-permute-start | bytes 393224 | tf_op jit(solution)/shard_map/ppermute | solution.py:29
  27.3 1.4 %collective-permute-start.4 = (f32[4,2,8,512]{3,2,1,0:T(8,128)S(1)}, f32[4,2,8,512]{3,2,1,0:T(8,128)S(1)}, u32[]{:S(2)}, u32[]{:S(2)}) collective-permute-start(f32[4,2,8,512]{3,2,1,0:T(8,128)S(1)} %get-tuple-element.22), channel_id=1, source_target_pairs={{0,1},{1,0},{2,3},{3,2},{4,5},{5,4},{6,7},{7,6},{8,9},{9,8},{10,11... | collective-permute-start | bytes 393224 | tf_op jit(solution)/shard_map/ppermute | solution.py:29
  28.8 4.3 %collective-permute-start.5 = (f32[4,2,8,256]{3,2,1,0:T(8,128)S(1)}, f32[4,2,8,256]{3,2,1,0:T(8,128)S(1)}, u32[]{:S(2)}, u32[]{:S(2)}) collective-permute-start(f32[4,2,8,256]{3,2,1,0:T(8,128)S(1)} %get-tuple-element.24), channel_id=1, source_target_pairs={{0,2},{2,0},{1,3},{3,1},{4,6},{6,4},{5,7},{7,5},{8,10},{10,8},{9,1... | collective-permute-start | bytes 196616 | tf_op jit(solution)/shard_map/ppermute | solution.py:29
  33.1 4.5 %collective-permute-start.6 = (f32[2,8,256]{2,1,0:T(8,128)S(1)}, f32[2,8,256]{2,1,0:T(8,128)S(1)}, u32[]{:S(2)}, u32[]{:S(2)}) collective-permute-start(f32[2,8,256]{2,1,0:T(8,128)S(1)} %get-tuple-element.26), channel_id=1, source_target_pairs={{4,0},{0,4},{12,8},{8,12},{5,1},{1,5},{13,9},{9,13},{6,2},{2,6},{1... | collective-permute-start | bytes 49160 | tf_op jit(solution)/shard_map/ppermute | solution.py:33
  34.8 4.8 %collective-permute-start.7 = (f32[2,8,256]{2,1,0:T(8,128)S(1)}, f32[2,8,256]{2,1,0:T(8,128)S(1)}, u32[]{:S(2)}, u32[]{:S(2)}) collective-permute-start(f32[2,8,256]{2,1,0:T(8,128)S(1)} %get-tuple-element.27), channel_id=1, source_target_pairs={{8,0},{12,4},{0,8},{4,12},{9,1},{13,5},{1,9},{5,13},{10,2},{14,6},... | collective-permute-start | bytes 49160 | tf_op jit(solution)/shard_map/ppermute | solution.py:33
  36.2 5.5 %collective-permute-start.8 = (f32[2,8,256]{2,1,0:T(8,128)S(1)}, f32[2,8,256]{2,1,0:T(8,128)S(1)}, u32[]{:S(2)}, u32[]{:S(2)}) collective-permute-start(f32[2,8,256]{2,1,0:T(8,128)S(1)} %get-tuple-element.28), channel_id=1, source_target_pairs={{12,0},{8,4},{4,8},{0,12},{13,1},{9,5},{5,9},{1,13},{14,2},{10,6},... | collective-permute-start | bytes 49160 | tf_op jit(solution)/shard_map/ppermute | solution.py:33

commit v2 on v1

v2 whole, which is shorter than its diff:
```python
import functools

import jax
import jax.numpy as jnp
from jax import lax
from jax.experimental import pallas as pl
from jax.experimental.pallas import tpu as pltpu
from jax.sharding import PartitionSpec as P

HALO = 2
BF = jnp.bfloat16
F32 = jnp.float32
VMEM = pl.BlockSpec(memory_space=pltpu.VMEM)


def peer(me, k, count):
    if count & (count - 1) == 0:
        return lax.bitwise_xor(me, jnp.int32(k))
    return lax.rem(me + k, jnp.int32(count))


def pairs_of(count, k):
    if count & (count - 1) == 0:
        return [(i, i ^ k) for i in range(count)]
    return [(i, (i + k) % count) for i in range(count)]


def to_peer(block, axis, k):
    return lax.ppermute(block, axis, pairs_of(lax.axis_size(axis), k))


def to_origin(block, axis, k):
    return lax.ppermute(block, axis, [(b, a) for a, b in pairs_of(lax.axis_size(axis), k)])


def call(body, out_shape, *args, scratch=(), flops=0, hbm=False, after=()):
    moved = sum(a.size * 4 for a in args)
    many = isinstance(out_shape, (tuple, list))
    if hbm:
        args = [pltpu.with_memory_space_constraint(a, pltpu.HBM) for a in args]
    space = pltpu.HBM if hbm else pltpu.VMEM
    count = len(args)

    def run(*refs):
        body(*refs[:count], *refs[count + len(after) :])

    return pl.pallas_call(
        run,
        out_shape=out_shape,
        in_specs=[pl.BlockSpec(memory_space=space)] * count
        + [pl.BlockSpec(memory_space=pl.ANY)] * len(after),
        out_specs=[VMEM] * len(out_shape) if many else VMEM,
        scratch_shapes=scratch,
        cost_estimate=pl.CostEstimate(flops=flops, bytes_accessed=moved, transcendentals=0),
        compiler_params=pltpu.CompilerParams(vmem_limit_bytes=24 << 20),
    )(*args, *after)


def pack_kernel(views, share, feat_hbm, row_hbm, col_hbm, frac_hbm, *refs):
    outs = refs[:views]
    feat_ref, row_ref, col_ref, frac_ref, sems = refs[views:]
    copies = [
        pltpu.make_async_copy(source, target, sems.at[i])
        for i, (source, target) in enumerate(
            ((feat_hbm, feat_ref), (row_hbm, row_ref), (col_hbm, col_ref), (frac_hbm, frac_ref))
        )
    ]
    for copy in copies:
        copy.start()
    for copy in copies:
        copy.wait()
    me = lax.axis_index("view")
    planes, rows = row_ref.shape[1:3]
    first = lax.axis_index("row") * rows
    width = feat_ref.shape[3]
    lanes = outs[0].shape[1]
    pages = -(-planes * rows // lanes)
    for d in range(planes):
        for y in range(rows):
            page, line = divmod(d * rows + y, lanes)
            top = (row_ref[0, d, y : y + 1, :] - (first + y - HALO)).astype(F32)
            col = col_ref[0, d, y : y + 1, :].astype(F32)
            fy = frac_ref[0, 0, d, y : y + 1, :].astype(F32) / 256.0
            fx = frac_ref[1, 0, d, y : y + 1, :].astype(F32) / 256.0
            for kind, value in enumerate((top, col, fy, fx)):
                for k in range(views):
                    outs[k][rows + kind * pages + page, line : line + 1, :] = value
    for k in range(views):
        base = peer(me, k, views) * share
        for y in range(rows):
            if share % 8:
                outs[k][y] = jnp.zeros((lanes, width), F32)
            for c in range(share):
                outs[k][y, c : c + 1, :] = feat_ref[0, base + c, y : y + 1, :]


def split(x):
    high = x.astype(BF)
    return high, (x - high.astype(F32)).astype(BF)


class Sizes:
    def __init__(self, packet, planes, rows):
        self.planes, self.rows = planes, rows
        self.lanes, self.width = packet.shape[1:]
        self.pages = -(-planes * rows // self.lanes)
        self.block = 256 if self.width % 256 == 0 else self.width
        self.segments = self.width // self.block
        self.window = 2 * HALO + 1
        self.padded = rows + 2 * HALO
        self.tall = self.segments * self.window * 2 * self.lanes

    def lookups(self):
        return pltpu.VMEM((self.window + 4 + self.segments, self.pages * self.lanes, self.width), F32)

    def one_hot(self):
        return (self.rows, self.block, self.planes * self.width)


def look_up(z, packet, t_ref):
    for page in range(z.pages):
        top, col, fy, fx = (packet[z.rows + kind * z.pages + page] for kind in range(4))
        lines = slice(page * z.lanes, (page + 1) * z.lanes)
        for i in range(z.window):
            t_ref[i, lines] = jnp.where(top == i, 1.0 - fy, jnp.where(top == i - 1, fy, 0.0))
        segment = jnp.zeros_like(col)
        for j in range(1, z.segments):
            segment = segment + jnp.where(col >= float(j * z.block), 1.0, 0.0)
        local = col - segment * float(z.block)
        t_ref[z.window, lines] = local
        t_ref[z.window + 1, lines] = segment
        t_ref[z.window + 2, lines] = 1.0 - fx
        t_ref[z.window + 3, lines] = fx
        for j in range(1, z.segments):
            border = (local == float(z.block - 1)) & (segment == float(j - 1))
            t_ref[z.window + 3 + j, lines] = jnp.where(border, fx, 0.0)


def build(z, t_ref, w_ref, d, y):
    at = pl.ds(d * z.rows + y, 1)
    local = t_ref[z.window, at, :]
    here, after = local.astype(BF), (local + 1.0).astype(BF)
    left, right = t_ref[z.window + 2, at, :].astype(BF), t_ref[z.window + 3, at, :].astype(BF)
    it = lax.broadcasted_iota(jnp.int32, (z.block, z.width), 0).astype(F32).astype(BF)
    hot = jnp.where(it == here, left, jnp.where(it == after, right, jnp.zeros((), BF)))
    columns = pl.ds(pl.multiple_of(d * z.width, 128), z.width)
    w_ref[y, :, columns] = hot


def each_plane(z, unroll, step):
    if unroll:
        for d in range(z.planes):
            step(d)
    else:
        lax.fori_loop(0, z.planes, lambda d, carry: (step(d), carry)[1], 0)


def forward(z, unroll, packet, halo, warped_ref, w_ref, t_ref, f_ref, b_ref):
    is_first = lax.axis_index("row") == 0
    look_up(z, packet, t_ref)
    half = z.window * 2 * z.lanes
    for r in range(z.padded):
        if r < HALO:
            x = jnp.where(is_first, 0.0, halo[z.rows - HALO + r])
        elif r < HALO + z.rows:
            x = packet[r - HALO]
        else:
            x = jnp.where(is_first, halo[r - HALO - z.rows], 0.0)
        both = jnp.concatenate(split(x), axis=0)
        for j in range(z.segments):
            for y in range(z.rows):
                if 0 <= r - y < z.window:
                    at = j * half + (r - y) * 2 * z.lanes
                    f_ref[y, at : at + 2 * z.lanes] = both[:, j * z.block : (j + 1) * z.block]
            if j:
                b_ref[r, j - 1] = jnp.broadcast_to(x[:, j * z.block : j * z.block + 1], x.shape)

    def step(d):
        for y in range(z.rows):
            build(z, t_ref, w_ref, d, y)
            at = pl.ds(d * z.rows + y, 1)
            columns = pl.ds(pl.multiple_of(d * z.width, 128), z.width)
            p = jnp.dot(f_ref[y], w_ref[y, :, columns], preferred_element_type=F32)
            segment = t_ref[z.window + 1, at, :]
            total = 0.0
            for i in range(z.window):
                value = 0.0
                for j in range(z.segments):
                    low = j * half + i * 2 * z.lanes
                    part = p[low : low + z.lanes] + p[low + z.lanes : low + 2 * z.lanes]
                    value = jnp.where(segment == float(j), part, value)
                for j in range(1, z.segments):
                    value = value + t_ref[z.window + 3 + j, at, :] * b_ref[y + i, j - 1]
                total = total + t_ref[i, at, :] * value
            warped_ref[d, y] = total

    each_plane(z, unroll, step)


def ahead_kernel(z, unroll, keep, count, *refs):
    packets, halo = refs[:count], refs[count]
    outs = refs[count + 1 : -3 if keep else -4]
    t_ref, f_ref, b_ref = refs[-3:]
    for v in range(count):
        w_ref = outs[count + v] if keep else refs[-4]
        forward(z, unroll, packets[v], halo.at[v], outs[v], w_ref, t_ref, f_ref, b_ref)


def backward(z, unroll, share, views, packet, warped, mean_ref, cot_ref, hot, fresh, work, own_ref, rim_ref):
    t_ref, l_ref, grad_ref, e_ref = work
    is_first = lax.axis_index("row") == 0
    half = z.window * 2 * z.lanes
    look_up(z, packet, t_ref)
    e_ref[...] = jnp.zeros_like(e_ref)

    def step(d):
        for y in range(z.rows):
            if fresh:
                build(z, t_ref, hot, d, y)
            at = pl.ds(d * z.rows + y, 1)
            columns = pl.ds(pl.multiple_of(d * z.width, 128), z.width)
            cot = cot_ref[d, :, y, :]
            if share % 8:
                rows = lax.broadcasted_iota(jnp.int32, (z.lanes, z.width), 0)
                wide = jnp.zeros((z.lanes, z.width), F32)
                for c in range(share):
                    wide = jnp.where(rows == c, cot[c : c + 1], wide)
                cot = wide
            g = (2.0 / views) * cot * (warped[d, y] - mean_ref[d, y])
            parts = []
            for i in range(z.window):
                term = t_ref[i, at, :] * g
                parts += split(term)
                for j in range(1, z.segments):
                    crossing = term * t_ref[z.window + 3 + j, at, :]
                    folded = crossing[:, :128]
                    for lane in range(128, z.width, 128):
                        folded = folded + crossing[:, lane : lane + 128]
                    e_ref[y + i, j - 1] += folded
            parts = jnp.concatenate(parts, axis=0)
            segment = t_ref[z.window + 1, at, :]
            for j in range(z.segments):
                mask = jnp.where(segment == float(j), 1.0, 0.0).astype(BF)
                l_ref[y, j * half : (j + 1) * half, columns] = parts * mask

    each_plane(z, unroll, step)
    for y in range(z.rows):
        p = lax.dot_general(
            l_ref[y], hot[y], (((1,), (1,)), ((), ())), preferred_element_type=F32
        )
        for i in range(z.window):
            for j in range(z.segments):
                low = j * half + i * 2 * z.lanes
                part = p[low : low + z.lanes] + p[low + z.lanes : low + 2 * z.lanes]
                columns = slice(j * z.block, (j + 1) * z.block)
                if y and i < z.window - 1:
                    grad_ref[y + i, :, columns] += part
                else:
                    grad_ref[y + i, :, columns] = part
    for r in range(z.padded):
        for j in range(1, z.segments):
            extra = jnp.sum(e_ref[r, j - 1], axis=1, keepdims=True)
            lane = lax.broadcasted_iota(jnp.int32, (z.lanes, 128), 1)
            columns = slice(j * z.block, j * z.block + 128)
            grad_ref[r, :, columns] += jnp.where(lane == 0, extra, 0.0)
    for r in range(z.rows):
        own_ref[r] = grad_ref[HALO + r]
    for r in range(HALO):
        rim_ref[r] = jnp.where(is_first, grad_ref[HALO + z.rows + r], grad_ref[r])


def turn_kernel(z, unroll, keep, share, views, late, count, *refs):
    early, hots_in = views - late, (count - late if keep else 0)
    packets, refs = refs[:count], refs[count:]
    halo, cot_ref, refs = refs[0], refs[1], refs[2:]
    ahead, refs = refs[:early], refs[early:]
    hots, refs = refs[:hots_in], refs[hots_in:]
    own_ref, rim_ref, mean_ref, warped_ref, w_ref, t_ref, f_ref, b_ref, l_ref, grad_ref, e_ref = refs
    for v in range(late):
        hot = w_ref.at[v if keep else 0]
        packet = packets[count - late + v]
        forward(z, unroll, packet, halo.at[v], warped_ref.at[v], hot, t_ref.at[0], f_ref, b_ref)
    warped = list(ahead) + [warped_ref.at[v] for v in range(late)]

    def average(d):
        for y in range(z.rows):
            mean_ref[d, y] = sum(w[d, y] for w in warped) / views

    each_plane(z, unroll, average)
    for v in reversed(range(count)):
        hot = w_ref.at[0]
        if keep:
            hot = hots[v] if v < count - late else w_ref.at[v - (count - late)]
        work = t_ref.at[v % 2], l_ref.at[v % 2], grad_ref.at[v % 2], e_ref.at[v % 2]
        backward(
            z, unroll, share, views, packets[v], warped[views - count + v], mean_ref, cot_ref, hot,
            not keep, work, own_ref.at[v], rim_ref.at[v],
        )


def rest_kernel(z, unroll, keep, share, views, count, *refs):
    packets, cot_ref, mean_ref, refs = refs[:count], refs[count], refs[count + 1], refs[count + 2 :]
    warped, refs = refs[:count], refs[count:]
    if keep:
        hots, refs = refs[:count], refs[count:]
    own_ref, rim_ref = refs[:2]
    t_ref, l_ref, grad_ref, e_ref = refs[-4:]
    for v in reversed(range(count)):
        work = t_ref.at[v % 2], l_ref.at[v % 2], grad_ref.at[v % 2], e_ref.at[v % 2]
        backward(
            z, unroll, share, views, packets[v], warped[v], mean_ref, cot_ref,
            hots[v] if keep else refs[2].at[0], not keep, work, own_ref.at[v], rim_ref.at[v],
        )


def stack_kernel(count, *refs):
    for v in range(count):
        refs[count][v] = refs[v][...]


def copy_kernel(in_ref, out_ref):
    out_ref[...] = in_ref[...]


def rows_kernel(count, *refs):
    rows = refs[count].shape[1]
    for v in range(count):
        refs[count][v] = refs[v][:rows]


def fold_kernel(depths, own_ref, rim_ref, *outs):
    views, rows, lanes, width = own_ref.shape
    part = width // depths
    me = lax.axis_index("depth")
    for k in range(depths):
        at = pl.multiple_of(peer(me, k, depths) * part, part)
        for v in range(views):
            for r in range(rows):
                outs[k][v, r] = own_ref[v, r, :, pl.ds(at, part)]
    is_first = lax.axis_index("row") == 0
    for k in range(depths):
        at = pl.multiple_of(peer(me, k, depths) * part, part)
        for v in range(views):
            for r in range(HALO):
                upper, lower = r, rows - HALO + r
                value = rim_ref[v, r, :, pl.ds(at, part)]
                outs[k][v, upper] += jnp.where(is_first, 0.0, value)
                outs[k][v, lower] += jnp.where(is_first, value, 0.0)


def sum_kernel(depths, views, *refs):
    for v in range(views):
        total = refs[0][v]
        for k in range(1, depths):
            total = total + refs[k][v]
        refs[depths + v][...] = total


def place_kernel(views, share, *refs):
    near, out_ref = len(refs) - 2, refs[-1]
    me = lax.axis_index("view")
    rows = out_ref.shape[2]
    for k in range(views):
        piece = refs[k] if k < near else refs[near].at[k - near]
        base = peer(me, k, views) * share
        for c in range(share):
            for r in range(rows):
                out_ref[0, base + c, r : r + 1, :] = piece[r, c : c + 1, :]


def per_device(features, cotangent, src_row, src_col, fractions):
    views = lax.axis_size("view")
    depths = lax.axis_size("depth")
    channels, rows, width = features.shape[1:]
    planes, share = cotangent.shape[:2]
    lanes = -(-share // 8) * 8
    pages = -(-planes * rows // lanes)
    packet = jax.ShapeDtypeStruct((rows + 4 * pages, lanes, width), F32)
    packets = call(
        functools.partial(pack_kernel, views, share),
        [packet] * views,
        features, src_row, src_col, fractions,
        scratch=[
            pltpu.VMEM(a.shape, a.dtype) for a in (features, src_row, src_col, fractions)
        ] + [pltpu.SemaphoreType.DMA((4,))],
        hbm=True,
    )
    packets = list(packets)
    z = Sizes(packet, planes, rows)
    keep = unroll = views <= 4
    if views <= 4:
        groups = [[k] for k in range(views)]
    else:
        groups = [[0], list(range(1, views // 2)), list(range(views // 2, views - 1)), [views - 1]]
    late = len(groups[-1])
    hot = jax.ShapeDtypeStruct(z.one_hot(), BF)
    warp = jax.ShapeDtypeStruct((planes, rows, lanes, width), F32)
    tables = [
        z.lookups(),
        pltpu.VMEM((rows, z.tall, z.block), BF),
        pltpu.VMEM((z.padded, max(z.segments - 1, 1), lanes, width), F32),
    ]
    flops = 2 * planes * rows * width * z.block * z.tall

    def halo_of(group, after=()):
        own_rows = call(
            functools.partial(rows_kernel, len(group)),
            jax.ShapeDtypeStruct((len(group), rows, lanes, width), F32),
            *[packets[k] for k in group],
            after=after,
        )
        return own_rows, to_peer(own_rows, "row", 1)

    def ahead(group, halo, after=()):
        count = len(group)
        results = call(
            functools.partial(ahead_kernel, z, unroll, keep, count),
            [warp] * count + ([hot] * count if keep else []),
            *[packets[k] for k in group], halo,
            scratch=([] if keep else [pltpu.VMEM(hot.shape, BF)]) + tables,
            flops=flops * count,
            after=after,
        )
        return results[:count], results[count:]

    halos = [halo_of(groups[0])]
    for k in range(views - 1, 0, -1):
        packets[k] = to_peer(packets[k], "view", k)
    halos.append(halo_of(groups[1]))
    warped, hots = ahead(groups[0], halos[0][1], (halos[1][0],))
    for at in range(1, len(groups) - 1):
        if at == len(groups) - 2:
            halos.append(halo_of(groups[at + 1], warped[-1:]))
            after = (halos[at + 1][0],)
        else:
            after = ()
        more, more_hots = ahead(groups[at], halos[at][1], after)
        warped, hots = warped + more, hots + more_hots
        if at + 1 < len(groups) - 1:
            halos.append(halo_of(groups[at + 1], warped[-1:]))
    first = views // 2
    last = views - first
    work = [
        pltpu.VMEM((2, rows, z.tall, planes * width), BF),
        pltpu.VMEM((2, z.padded, lanes, width), F32),
        pltpu.VMEM((2, z.padded, max(z.segments - 1, 1), lanes, 128), F32),
    ]
    twice = pltpu.VMEM((2,) + z.lookups().shape, F32)

    def results_of(count):
        return [
            jax.ShapeDtypeStruct((count, rows, lanes, width), F32),
            jax.ShapeDtypeStruct((count, HALO, lanes, width), F32),
        ]

    own, rim, mean = call(
        functools.partial(turn_kernel, z, unroll, keep, share, views, late, last),
        results_of(last) + [warp],
        *packets[first:], halos[-1][1], cotangent, *warped, *hots[first:],
        scratch=[
            pltpu.VMEM((late,) + warp.shape, F32),
            pltpu.VMEM((late if keep else 1,) + hot.shape, BF),
            twice, *tables[1:], *work,
        ],
        flops=flops * (last + late),
    )
    rim = call(copy_kernel, jax.ShapeDtypeStruct(rim.shape, F32), rim)
    own_rest, rim_rest = call(
        functools.partial(rest_kernel, z, unroll, keep, share, views, first),
        results_of(first),
        *packets[:first], cotangent, mean, *warped[:first], *hots[:first],
        scratch=([] if keep else [pltpu.VMEM((1,) + hot.shape, BF)]) + [twice, *work],
        flops=flops * first,
        after=(rim,),
    )
    part = width // depths
    pieces = []
    for own, rim in ((own, rim), (own_rest, rim_rest)):
        count = own.shape[0]
        rim = to_peer(rim, "row", 1)
        halves = call(
            functools.partial(fold_kernel, depths),
            [jax.ShapeDtypeStruct((count, rows, lanes, part), F32)] * depths,
            own, rim,
        )
        halves = [halves[0]] + [to_peer(halves[k], "depth", k) for k in range(1, depths)]
        sums = call(
            functools.partial(sum_kernel, depths, count),
            [jax.ShapeDtypeStruct((rows, lanes, part), F32)] * count,
            *halves,
        )
        pieces = list(sums) + pieces
    back = [pieces[0]] + [to_origin(pieces[k], "view", k) for k in range(1, views)]
    far = call(
        functools.partial(stack_kernel, last),
        jax.ShapeDtypeStruct((last, rows, lanes, part), F32),
        *back[first:],
    )
    return call(
        functools.partial(place_kernel, views, share),
        jax.ShapeDtypeStruct((1, channels, rows, part), F32),
        *back[:first], far,
    )


def solution(mesh):
    in_specs = (
        P("view", None, ("group", "row"), None),
        P("depth", "view", ("group", "row"), None),
        P("view", "depth", ("group", "row"), None),
        P("view", "depth", ("group", "row"), None),
        P(None, "view", "depth", ("group", "row"), None),
    )
    out_specs = P("view", None, ("group", "row"), "depth")
    return jax.shard_map(
        per_device, mesh=mesh, in_specs=in_specs, out_specs=out_specs, check_vma=False
    )
```

time: 42.8 us -> 34.1 us (0.80)
  waiting for transfers between devices: 17.3 us -> 12.1 us
  local copies, waits for them, and re-layouts: 3.11 us -> 0.01 us
  Pallas kernels: 9.94 us -> 8.43 us
  starting transfers between devices: 12 us -> 13.3 us
    ppermute x6 -> x11, waiting for transfers between devices: 13.1 us -> 7.96 us  [to_peer(): return lax.ppermute(block, axis, pairs_of(lax.axis_size(axis), k))]
    unnamed x10 -> x2, local copies, waits for them, and re-layouts: 3.1 us -> 0.01 us
    ppermute x6 -> x11, starting transfers between devices: 7.53 us -> 9.75 us  [to_peer(): return lax.ppermute(block, axis, pairs_of(lax.axis_size(axis), k))]
    pallas_call x5 -> x17, Pallas kernels: 9.94 us -> 8.43 us  [call(): pl.pallas_call(run, out_shape=out_shape, in_specs=[pl.BlockSpec(memory_sp...]
    ppermute x3, starting transfers between devices: 4.45 us -> 3.57 us  [to_origin(): lax.ppermute(block, axis, [(b, a) for a, b in pairs_of(lax.axis_size(axis...]
  transfers between devices with their start and end apart: 9 -> 14, of which waited for: 7 -> 6; matrix products, arithmetic and copies ran while one was open for 0% -> 0% of each run, Pallas kernels for 0% -> 13%
where the time goes in v2:
time: 34.1 us; the launch traced here: 33.9 us
  starting transfers between devices  13.3 us (39%)
  waiting for transfers between devices  12.1 us (35%)
  Pallas kernels  8.43 us (25%)
    ppermute x11, starting transfers between devices, to_peer(): return lax.ppermute(block, axis, pairs_of(lax.axis_size(axis), k))  9.75 us
    pallas_call x17, Pallas kernels, call(): pl.pallas_call(run, out_shape=out_shape, in_specs=[pl.BlockSpec(memory_sp...  8.43 us
    ppermute x11, waiting for transfers between devices, to_peer(): return lax.ppermute(block, axis, pairs_of(lax.axis_size(axis), k))  7.96 us
    ppermute x3, waiting for transfers between devices, to_origin(): lax.ppermute(block, axis, [(b, a) for a, b in pairs_of(lax.axis_size(axis...  4.1 us
    ppermute x3, starting transfers between devices, to_origin(): lax.ppermute(block, axis, [(b, a) for a, b in pairs_of(lax.axis_size(axis...  3.57 us
  transfers between devices with their start and end apart: 14, of which 6 were waited for; matrix products, arithmetic and copies ran while one was open for 0% of the time, Pallas kernels for 13%

profile of v2, /device:TPU:0, one launch (start us, length us, event | category | flops | bytes accessed | tf_op | source)
XLA Modules:
  0.0 33.9 jit_solution(875727786779160349)
XLA Ops:
  0.0 1.0 %shard_map.55 = (f32[6,8,512]{2,1,0:T(8,128)S(1)}, f32[6,8,512]{2,1,0:T(8,128)S(1)}, f32[6,8,512]{2,1,0:T(8,128)S(1)}, f32[6,8,512]{2,1,0:T(8,128)S(1)}) custom-call(f32[1,32,2,512]{3,2,1,0:T(2,128)} %refs_0_.1, s32[1,4,2,512]{3,2,1,0:T(2,128)} %refs_1_.1, s32[1,4,2,512]{3,2,1,0:T(2,128)} %refs_2_.2, s32[2,1,4,2,512]{4,3,2,1,0:T(2,128)} %refs_3_.2), custom_call_target="tpu_custom_call" | custom-call | bytes 196608 | tf_op jit(solution)/shard_map/pallas_call | solution.py:47
  1.0 3.1 %collective-permute-start = (f32[6,8,512]{2,1,0:T(8,128)S(1)}, f32[6,8,512]{2,1,0:T(8,128)S(1)}, u32[]{:S(2)}, u32[]{:S(2)}) collective-permute-start(f32[6,8,512]{2,1,0:T(8,128)S(1)} %get-tuple-element.29), channel_id=1, source_target_pairs={{0,4},{4,0},{8,12},{12,8},{1,5},{5,1},{9,13},{13,9},{2,6},{6,2},{1... | collective-permute-start | bytes 294920 | tf_op jit(solution)/shard_map/ppermute | solution.py:29
  4.1 2.6 %collective-permute-start.1 = (f32[6,8,512]{2,1,0:T(8,128)S(1)}, f32[6,8,512]{2,1,0:T(8,128)S(1)}, u32[]{:S(2)}, u32[]{:S(2)}) collective-permute-start(f32[6,8,512]{2,1,0:T(8,128)S(1)} %get-tuple-element.30), channel_id=1, source_target_pairs={{0,8},{4,12},{8,0},{12,4},{1,9},{5,13},{9,1},{13,5},{2,10},{6,14},... | collective-permute-start | bytes 294920 | tf_op jit(solution)/shard_map/ppermute | solution.py:29
  6.7 0.2 collective-permute-done.refs_0_.refs_1_
  6.9 0.5 %collective-permute-start.5 = (f32[1,2,8,512]{3,2,1,0:T(8,128)S(1)}, f32[1,2,8,512]{3,2,1,0:T(8,128)S(1)}, u32[]{:S(2)}, u32[]{:S(2)}) collective-permute-start(f32[1,2,8,512]{3,2,1,0:T(8,128)S(1)} %shard_map.59), channel_id=1, source_target_pairs={{0,1},{1,0},{2,3},{3,2},{4,5},{5,4},{6,7},{7,6},{8,9},{9,8},{10,11... | collective-permute-start | bytes 98312 | tf_op jit(solution)/shard_map/ppermute | solution.py:29
  7.4 0.7 %collective-permute-done.3.refs_1_ = f32[1,2,8,512]{3,2,1,0:T(8,128)S(1)} collective-permute-done((f32[1,2,8,512]{3,2,1,0:T(8,128)S(1)}, f32[1,2,8,512]{3,2,1,0:T(8,128)S(1)}, u32[]{:S(2)}, u32[]{:S(2)}) %collective-permute-start.3) | collective-permute-done | bytes 32800 | tf_op jit(solution)/shard_map/ppermute | solution.py:29
  8.1 0.9 %shard_map.57 = (f32[4,2,8,512]{3,2,1,0:T(8,128)S(1)}, bf16[2,256,2048]{2,1,0:T(8,128)(2,1)S(1)}) custom-call(f32[6,8,512]{2,1,0:T(8,128)S(1)} %collective-permute-done.refs_0_.refs_1_, f32[1,2,8,512]{3,2,1,0:T(8,128)S(1)} %collective-permute-done.3.refs_1_), custom_call_target="tpu_custom_call" | custom-call | flops 335544320 | bytes 131072 | tf_op jit(solution)/shard_map/pallas_call | solution.py:47
  9.0 5.5 %collective-permute-done.1.refs_0_ = f32[6,8,512]{2,1,0:T(8,128)S(1)} collective-permute-done((f32[6,8,512]{2,1,0:T(8,128)S(1)}, f32[6,8,512]{2,1,0:T(8,128)S(1)}, u32[]{:S(2)}, u32[]{:S(2)}) %collective-permute-start.1) | collective-permute-done | bytes 98336 | tf_op jit(solution)/shard_map/ppermute | solution.py:29
  14.6 0.5 %collective-permute-start.4 = (f32[1,2,8,512]{3,2,1,0:T(8,128)S(1)}, f32[1,2,8,512]{3,2,1,0:T(8,128)S(1)}, u32[]{:S(2)}, u32[]{:S(2)}) collective-permute-start(f32[1,2,8,512]{3,2,1,0:T(8,128)S(1)} %shard_map.58.refs_2_), channel_id=1, source_target_pairs={{0,1},{1,0},{2,3},{3,2},{4,5},{5,4},{6,7},{7,6},{8,9},{9,8},{10,11... | collective-permute-start | bytes 98312 | tf_op jit(solution)/shard_map/ppermute | solution.py:29
  15.1 0.9 %shard_map.60 = (f32[4,2,8,512]{3,2,1,0:T(8,128)S(1)}, bf16[2,256,2048]{2,1,0:T(8,128)(2,1)S(1)}) custom-call(f32[6,8,512]{2,1,0:T(8,128)S(1)} %get-tuple-element.28.refs_0_, f32[1,2,8,512]{3,2,1,0:T(8,128)S(1)} %collective-permute-done.5.refs_1_, f32[1,2,8,512]{3,2,1,0:T(8,128)S(1)} %shard_map.56.refs_2_), custom_call_target="tpu_custom_call" | custom-call | flops 335544320 | bytes 131072 | tf_op jit(solution)/shard_map/pallas_call | solution.py:47
  16.0 0.9 %shard_map.62 = (f32[4,2,8,512]{3,2,1,0:T(8,128)S(1)}, bf16[2,256,2048]{2,1,0:T(8,128)(2,1)S(1)}) custom-call(f32[6,8,512]{2,1,0:T(8,128)S(1)} %collective-permute-done.1.refs_0_, f32[1,2,8,512]{3,2,1,0:T(8,128)S(1)} %collective-permute-done.6.refs_1_, f32[1,2,8,512]{3,2,1,0:T(8,128)S(1)} %shard_map.58.refs_2_), custom_call_target="tpu_custom_call" | custom-call | flops 335544320 | bytes 131072 | tf_op jit(solution)/shard_map/pallas_call | solution.py:47
  16.9 2.4 %shard_map.63 = (f32[2,2,8,512]{3,2,1,0:T(8,128)S(1)}, f32[2,2,8,512]{3,2,1,0:T(8,128)S(1)}, f32[4,2,8,512]{3,2,1,0:T(8,128)S(1)}) custom-call(f32[6,8,512]{2,1,0:T(8,128)S(1)} %collective-permute-done.1.refs_0_, f32[6,8,512]{2,1,0:T(8,128)S(1)} %collective-permute-done.2.refs_0_.refs_1_, f32[1,2,8,512]{3,2,1,0:T(8,128)S(1)} %collective-permute-done.4.refs_2_, ...), custom_call_target="tpu_custom_call" | custom-call | flops 1006632960 | bytes 4947968 | tf_op jit(solution)/shard_map/pallas_call | solution.py:47
  19.3 0.1 collective-permute-start.10
  19.5 1.6 %shard_map.65 = (f32[2,2,8,512]{3,2,1,0:T(8,128)S(1)}, f32[2,2,8,512]{3,2,1,0:T(8,128)S(1)}) custom-call(f32[6,8,512]{2,1,0:T(8,128)S(1)} %get-tuple-element.28.refs_0_, f32[6,8,512]{2,1,0:T(8,128)S(1)} %collective-permute-done.refs_0_.refs_1_, f32[4,8,2,512]{3,2,1,0:T(2,128)S(1)} %copy-done, f32[4,2,8,512]{3,2,1,0:T(8,128)S(1)} %get-tuple-element.36.refs_3_, ...), custom_call_target="tpu_custom_call" | custom-call | flops 671088640 | bytes 9109504 | tf_op jit(solution)/shard_map/pallas_call | solution.py:47
  21.1 0.5 %collective-permute-start.7 = (f32[2,2,8,512]{3,2,1,0:T(8,128)S(1)}, f32[2,2,8,512]{3,2,1,0:T(8,128)S(1)}, u32[]{:S(2)}, u32[]{:S(2)}) collective-permute-start(f32[2,2,8,512]{3,2,1,0:T(8,128)S(1)} %get-tuple-element.41), channel_id=1, source_target_pairs={{0,1},{1,0},{2,3},{3,2},{4,5},{5,4},{6,7},{7,6},{8,9},{9,8},{10,11... | collective-permute-start | bytes 196616 | tf_op jit(solution)/shard_map/ppermute | solution.py:29
  21.6 1.6 %collective-permute-start.11 = (f32[2,2,8,256]{3,2,1,0:T(8,128)S(1)}, f32[2,2,8,256]{3,2,1,0:T(8,128)S(1)}, u32[]{:S(2)}, u32[]{:S(2)}) collective-permute-start(f32[2,2,8,256]{3,2,1,0:T(8,128)S(1)} %get-tuple-element.48), channel_id=1, source_target_pairs={{0,2},{2,0},{1,3},{3,1},{4,6},{6,4},{5,7},{7,5},{8,10},{10,8},{9,1... | collective-permute-start | bytes 98312 | tf_op jit(solution)/shard_map/ppermute | solution.py:29
  23.2 0.9 %collective-permute-start.8 = (f32[2,2,8,256]{3,2,1,0:T(8,128)S(1)}, f32[2,2,8,256]{3,2,1,0:T(8,128)S(1)}, u32[]{:S(2)}, u32[]{:S(2)}) collective-permute-start(f32[2,2,8,256]{3,2,1,0:T(8,128)S(1)} %get-tuple-element.43), channel_id=1, source_target_pairs={{0,2},{2,0},{1,3},{3,1},{4,6},{6,4},{5,7},{7,5},{8,10},{10,8},{9,1... | collective-permute-start | bytes 98312 | tf_op jit(solution)/shard_map/ppermute | solution.py:29
  24.1 1.5 %collective-permute-done.11.refs_1_ = f32[2,2,8,256]{3,2,1,0:T(8,128)S(1)} collective-permute-done((f32[2,2,8,256]{3,2,1,0:T(8,128)S(1)}, f32[2,2,8,256]{3,2,1,0:T(8,128)S(1)}, u32[]{:S(2)}, u32[]{:S(2)}) %collective-permute-start.11) | collective-permute-done | bytes 32800 | tf_op jit(solution)/shard_map/ppermute | solution.py:29
  25.6 2.1 %collective-permute-start.12 = (f32[2,8,256]{2,1,0:T(8,128)S(1)}, f32[2,8,256]{2,1,0:T(8,128)S(1)}, u32[]{:S(2)}, u32[]{:S(2)}) collective-permute-start(f32[2,8,256]{2,1,0:T(8,128)S(1)} %get-tuple-element.49), channel_id=1, source_target_pairs={{8,0},{12,4},{0,8},{4,12},{9,1},{13,5},{1,9},{5,13},{10,2},{14,6},... | collective-permute-start | bytes 49160 | tf_op jit(solution)/shard_map/ppermute | solution.py:33
  27.7 1.3 %collective-permute-start.13 = (f32[2,8,256]{2,1,0:T(8,128)S(1)}, f32[2,8,256]{2,1,0:T(8,128)S(1)}, u32[]{:S(2)}, u32[]{:S(2)}) collective-permute-start(f32[2,8,256]{2,1,0:T(8,128)S(1)} %get-tuple-element.50), channel_id=1, source_target_pairs={{12,0},{8,4},{4,8},{0,12},{13,1},{9,5},{5,9},{1,13},{14,2},{10,6},... | collective-permute-start | bytes 49160 | tf_op jit(solution)/shard_map/ppermute | solution.py:33
  29.1 0.1 collective-permute-start.9
  29.2 1.1 %collective-permute-done.12.refs_0_ = f32[2,8,256]{2,1,0:T(8,128)S(1)} collective-permute-done((f32[2,8,256]{2,1,0:T(8,128)S(1)}, f32[2,8,256]{2,1,0:T(8,128)S(1)}, u32[]{:S(2)}, u32[]{:S(2)}) %collective-permute-start.12) | collective-permute-done | bytes 16416 | tf_op jit(solution)/shard_map/ppermute | solution.py:33
  30.2 3.0 %collective-permute-done.13.refs_1_ = f32[2,8,256]{2,1,0:T(8,128)S(1)} collective-permute-done((f32[2,8,256]{2,1,0:T(8,128)S(1)}, f32[2,8,256]{2,1,0:T(8,128)S(1)}, u32[]{:S(2)}, u32[]{:S(2)}) %collective-permute-start.13) | collective-permute-done | bytes 16416 | tf_op jit(solution)/shard_map/ppermute | solution.py:33
  33.3 0.7 %shard_map.71 = f32[1,32,2,256]{3,2,1,0:T(2,128)} custom-call(f32[2,8,256]{2,1,0:T(8,128)S(1)} %get-tuple-element.44.refs_0_, f32[2,8,256]{2,1,0:T(8,128)S(1)} %collective-permute-done.9.refs_1_, f32[2,2,8,256]{3,2,1,0:T(8,128)S(1)} %shard_map.70.refs_2_), custom_call_target="tpu_custom_call" | custom-call | bytes 65536 | tf_op jit(solution)/shard_map/pallas_call | solution.py:47
  (23 shorter events, 0.1 us)
Async XLA Ops:
  1.0 5.9 %collective-permute-start = (f32[6,8,512]{2,1,0:T(8,128)S(1)}, f32[6,8,512]{2,1,0:T(8,128)S(1)}, u32[]{:S(2)}, u32[]{:S(2)}) collective-permute-start(f32[6,8,512]{2,1,0:T(8,128)S(1)} %get-tuple-element.29), channel_id=1, source_target_pairs={{0,4},{4,0},{8,12},{12,8},{1,5},{5,1},{9,13},{13,9},{2,6},{6,2},{1... | collective-permute-start | bytes 294920 | tf_op jit(solution)/shard_map/ppermute | solution.py:29
  4.1 10.4 %collective-permute-start.1 = (f32[6,8,512]{2,1,0:T(8,128)S(1)}, f32[6,8,512]{2,1,0:T(8,128)S(1)}, u32[]{:S(2)}, u32[]{:S(2)}) collective-permute-start(f32[6,8,512]{2,1,0:T(8,128)S(1)} %get-tuple-element.30), channel_id=1, source_target_pairs={{0,8},{4,12},{8,0},{12,4},{1,9},{5,13},{9,1},{13,5},{2,10},{6,14},... | collective-permute-start | bytes 294920 | tf_op jit(solution)/shard_map/ppermute | solution.py:29
  6.7 7.8 %collective-permute-start.2 = (f32[6,8,512]{2,1,0:T(8,128)S(1)}, f32[6,8,512]{2,1,0:T(8,128)S(1)}, u32[]{:S(2)}, u32[]{:S(2)}) collective-permute-start(f32[6,8,512]{2,1,0:T(8,128)S(1)} %get-tuple-element.31), channel_id=1, source_target_pairs={{0,12},{4,8},{8,4},{12,0},{1,13},{5,9},{9,5},{13,1},{2,14},{6,10},... | collective-permute-start | bytes 294920 | tf_op jit(solution)/shard_map/ppermute | solution.py:29
  6.9 1.2 %collective-permute-start.3 = (f32[1,2,8,512]{3,2,1,0:T(8,128)S(1)}, f32[1,2,8,512]{3,2,1,0:T(8,128)S(1)}, u32[]{:S(2)}, u32[]{:S(2)}) collective-permute-start(f32[1,2,8,512]{3,2,1,0:T(8,128)S(1)} %shard_map.56.refs_2_), channel_id=1, source_target_pairs={{0,1},{1,0},{2,3},{3,2},{4,5},{5,4},{6,7},{7,6},{8,9},{9,8},{10,11... | collective-permute-start | bytes 98312 | tf_op jit(solution)/shard_map/ppermute | solution.py:29
  6.9 9.9 %copy-start = (f32[4,8,2,512]{3,2,1,0:T(2,128)S(1)}, f32[4,8,2,512]{3,2,1,0:T(2,128)}, u32[]{:S(2)}) copy-start(f32[4,8,2,512]{3,2,1,0:T(2,128)} %refs_2_.3) | copy-start | bytes 393220
  6.9 8.1 %collective-permute-start.5 = (f32[1,2,8,512]{3,2,1,0:T(8,128)S(1)}, f32[1,2,8,512]{3,2,1,0:T(8,128)S(1)}, u32[]{:S(2)}, u32[]{:S(2)}) collective-permute-start(f32[1,2,8,512]{3,2,1,0:T(8,128)S(1)} %shard_map.59), channel_id=1, source_target_pairs={{0,1},{1,0},{2,3},{3,2},{4,5},{5,4},{6,7},{7,6},{8,9},{9,8},{10,11... | collective-permute-start | bytes 98312 | tf_op jit(solution)/shard_map/ppermute | solution.py:29
  14.6 1.4 %collective-permute-start.6 = (f32[1,2,8,512]{3,2,1,0:T(8,128)S(1)}, f32[1,2,8,512]{3,2,1,0:T(8,128)S(1)}, u32[]{:S(2)}, u32[]{:S(2)}) collective-permute-start(f32[1,2,8,512]{3,2,1,0:T(8,128)S(1)} %shard_map.61), channel_id=1, source_target_pairs={{0,1},{1,0},{2,3},{3,2},{4,5},{5,4},{6,7},{7,6},{8,9},{9,8},{10,11... | collective-permute-start | bytes 98312 | tf_op jit(solution)/shard_map/ppermute | solution.py:29
  14.6 2.3 %collective-permute-start.4 = (f32[1,2,8,512]{3,2,1,0:T(8,128)S(1)}, f32[1,2,8,512]{3,2,1,0:T(8,128)S(1)}, u32[]{:S(2)}, u32[]{:S(2)}) collective-permute-start(f32[1,2,8,512]{3,2,1,0:T(8,128)S(1)} %shard_map.58.refs_2_), channel_id=1, source_target_pairs={{0,1},{1,0},{2,3},{3,2},{4,5},{5,4},{6,7},{7,6},{8,9},{9,8},{10,11... | collective-permute-start | bytes 98312 | tf_op jit(solution)/shard_map/ppermute | solution.py:29
  19.3 2.3 %collective-permute-start.10 = (f32[2,2,8,512]{3,2,1,0:T(8,128)S(1)}, f32[2,2,8,512]{3,2,1,0:T(8,128)S(1)}, u32[]{:S(2)}, u32[]{:S(2)}) collective-permute-start(f32[2,2,8,512]{3,2,1,0:T(8,128)S(1)} %shard_map.64.refs_8_), channel_id=1, source_target_pairs={{0,1},{1,0},{2,3},{3,2},{4,5},{5,4},{6,7},{7,6},{8,9},{9,8},{10,11... | collective-permute-start | bytes 196616 | tf_op jit(solution)/shard_map/ppermute | solution.py:29
  21.1 2.1 %collective-permute-start.7 = (f32[2,2,8,512]{3,2,1,0:T(8,128)S(1)}, f32[2,2,8,512]{3,2,1,0:T(8,128)S(1)}, u32[]{:S(2)}, u32[]{:S(2)}) collective-permute-start(f32[2,2,8,512]{3,2,1,0:T(8,128)S(1)} %get-tuple-element.41), channel_id=1, source_target_pairs={{0,1},{1,0},{2,3},{3,2},{4,5},{5,4},{6,7},{7,6},{8,9},{9,8},{10,11... | collective-permute-start | bytes 196616 | tf_op jit(solution)/shard_map/ppermute | solution.py:29
  21.6 4.0 %collective-permute-start.11 = (f32[2,2,8,256]{3,2,1,0:T(8,128)S(1)}, f32[2,2,8,256]{3,2,1,0:T(8,128)S(1)}, u32[]{:S(2)}, u32[]{:S(2)}) collective-permute-start(f32[2,2,8,256]{3,2,1,0:T(8,128)S(1)} %get-tuple-element.48), channel_id=1, source_target_pairs={{0,2},{2,0},{1,3},{3,1},{4,6},{6,4},{5,7},{7,5},{8,10},{10,8},{9,1... | collective-permute-start | bytes 98312 | tf_op jit(solution)/shard_map/ppermute | solution.py:29
  23.2 5.9 %collective-permute-start.8 = (f32[2,2,8,256]{3,2,1,0:T(8,128)S(1)}, f32[2,2,8,256]{3,2,1,0:T(8,128)S(1)}, u32[]{:S(2)}, u32[]{:S(2)}) collective-permute-start(f32[2,2,8,256]{3,2,1,0:T(8,128)S(1)} %get-tuple-element.43), channel_id=1, source_target_pairs={{0,2},{2,0},{1,3},{3,1},{4,6},{6,4},{5,7},{7,5},{8,10},{10,8},{9,1... | collective-permute-start | bytes 98312 | tf_op jit(solution)/shard_map/ppermute | solution.py:29
  25.6 4.6 %collective-permute-start.12 = (f32[2,8,256]{2,1,0:T(8,128)S(1)}, f32[2,8,256]{2,1,0:T(8,128)S(1)}, u32[]{:S(2)}, u32[]{:S(2)}) collective-permute-start(f32[2,8,256]{2,1,0:T(8,128)S(1)} %get-tuple-element.49), channel_id=1, source_target_pairs={{8,0},{12,4},{0,8},{4,12},{9,1},{13,5},{1,9},{5,13},{10,2},{14,6},... | collective-permute-start | bytes 49160 | tf_op jit(solution)/shard_map/ppermute | solution.py:33
  27.7 5.5 %collective-permute-start.13 = (f32[2,8,256]{2,1,0:T(8,128)S(1)}, f32[2,8,256]{2,1,0:T(8,128)S(1)}, u32[]{:S(2)}, u32[]{:S(2)}) collective-permute-start(f32[2,8,256]{2,1,0:T(8,128)S(1)} %get-tuple-element.50), channel_id=1, source_target_pairs={{12,0},{8,4},{4,8},{0,12},{13,1},{9,5},{5,9},{1,13},{14,2},{10,6},... | collective-permute-start | bytes 49160 | tf_op jit(solution)/shard_map/ppermute | solution.py:33
  29.1 4.2 %collective-permute-start.9 = (f32[2,8,256]{2,1,0:T(8,128)S(1)}, f32[2,8,256]{2,1,0:T(8,128)S(1)}, u32[]{:S(2)}, u32[]{:S(2)}) collective-permute-start(f32[2,8,256]{2,1,0:T(8,128)S(1)} %get-tuple-element.45), channel_id=1, source_target_pairs={{4,0},{0,4},{12,8},{8,12},{5,1},{1,5},{13,9},{9,13},{6,2},{2,6},{1... | collective-permute-start | bytes 49160 | tf_op jit(solution)/shard_map/ppermute | solution.py:33

commit v3 on v2

--- a/solution.py
+++ b/solution.py
@@ -113,8 +113,9 @@
     def lookups(self):
         return pltpu.VMEM((self.window + 4 + self.segments, self.pages * self.lanes, self.width), F32)
 
-    def one_hot(self):
-        return (self.rows, self.block, self.planes * self.width)
+    def one_hot(self, turned=False):
+        length = self.planes * self.width
+        return (self.rows,) + ((length, self.block) if turned else (self.block, length))
 
 
 def look_up(z, packet, t_ref):
@@ -197,16 +198,20 @@
     each_plane(z, unroll, step)
 
 
-def ahead_kernel(z, unroll, keep, count, *refs):
+def ahead_kernel(z, unroll, keep, turned, count, *refs):
     packets, halo = refs[:count], refs[count]
-    outs = refs[count + 1 : -3 if keep else -4]
+    own_hot = turned or not keep
+    outs = refs[count + 1 : -4 if own_hot else -3]
     t_ref, f_ref, b_ref = refs[-3:]
     for v in range(count):
-        w_ref = outs[count + v] if keep else refs[-4]
+        w_ref = refs[-4] if own_hot else outs[count + v]
         forward(z, unroll, packets[v], halo.at[v], outs[v], w_ref, t_ref, f_ref, b_ref)
-
-
-def backward(z, unroll, share, views, packet, warped, mean_ref, cot_ref, hot, fresh, work, own_ref, rim_ref):
+        if turned:
+            for y in range(z.rows):
+                outs[count + v][y] = w_ref[y].T
+
+
+def backward(z, unroll, share, views, packet, warped, mean_ref, cot_ref, hot, fresh, turned, work, own_ref, rim_ref):
     t_ref, l_ref, grad_ref, e_ref = work
     is_first = lax.axis_index("row") == 0
     half = z.window * 2 * z.lanes
@@ -246,7 +251,7 @@
     each_plane(z, unroll, step)
     for y in range(z.rows):
         p = lax.dot_general(
-            l_ref[y], hot[y], (((1,), (1,)), ((), ())), preferred_element_type=F32
+            l_ref[y], hot[y], (((1,), (0 if turned else 1,)), ((), ())), preferred_element_type=F32
         )
         for i in range(z.window):
             for j in range(z.segments):
@@ -294,7 +299,7 @@
         work = t_ref.at[v % 2], l_ref.at[v % 2], grad_ref.at[v % 2], e_ref.at[v % 2]
         backward(
             z, unroll, share, views, packets[v], warped[views - count + v], mean_ref, cot_ref, hot,
-            not keep, work, own_ref.at[v], rim_ref.at[v],
+            not keep, keep and hot.shape != w_ref.at[0].shape, work, own_ref.at[v], rim_ref.at[v],
         )
 
 
@@ -309,7 +314,7 @@
         work = t_ref.at[v % 2], l_ref.at[v % 2], grad_ref.at[v % 2], e_ref.at[v % 2]
         backward(
             z, unroll, share, views, packets[v], warped[v], mean_ref, cot_ref,
-            hots[v] if keep else refs[2].at[0], not keep, work, own_ref.at[v], rim_ref.at[v],
+            hots[v] if keep else refs[2].at[0], not keep, False, work, own_ref.at[v], rim_ref.at[v],
         )
 
 
@@ -361,7 +366,7 @@
     me = lax.axis_index("view")
     rows = out_ref.shape[2]
     for k in range(views):
-        piece = refs[k] if k < near else refs[near].at[k - near]
+        piece = refs[k] if k < near else refs[near].at[views - 1 - k]
         base = peer(me, k, views) * share
         for c in range(share):
             for r in range(rows):
@@ -411,13 +416,14 @@
         )
         return own_rows, to_peer(own_rows, "row", 1)
 
-    def ahead(group, halo, after=()):
+    def ahead(group, halo, after=(), turned=False):
         count = len(group)
+        shape = jax.ShapeDtypeStruct(z.one_hot(turned), BF)
         results = call(
-            functools.partial(ahead_kernel, z, unroll, keep, count),
-            [warp] * count + ([hot] * count if keep else []),
+            functools.partial(ahead_kernel, z, unroll, keep, turned, count),
+            [warp] * count + ([shape] * count if keep else []),
             *[packets[k] for k in group], halo,
-            scratch=([] if keep else [pltpu.VMEM(hot.shape, BF)]) + tables,
+            scratch=([] if keep and not turned else [pltpu.VMEM(hot.shape, BF)]) + tables,
             flops=flops * count,
             after=after,
         )
@@ -434,11 +440,11 @@
             after = (halos[at + 1][0],)
         else:
             after = ()
-        more, more_hots = ahead(groups[at], halos[at][1], after)
+        more, more_hots = ahead(groups[at], halos[at][1], after, keep and groups[at] == [1])
         warped, hots = warped + more, hots + more_hots
         if at + 1 < len(groups) - 1:
             halos.append(halo_of(groups[at + 1], warped[-1:]))
-    first = views // 2
+    first = max(views // 4, 1)
     last = views - first
     work = [
         pltpu.VMEM((2, rows, z.tall, planes * width), BF),
@@ -475,13 +481,14 @@
     )
     part = width // depths
     pieces = []
-    for own, rim in ((own, rim), (own_rest, rim_rest)):
+    for own, rim, after in ((own, rim, (own_rest,)), (own_rest, rim_rest, ())):
         count = own.shape[0]
         rim = to_peer(rim, "row", 1)
         halves = call(
             functools.partial(fold_kernel, depths),
             [jax.ShapeDtypeStruct((count, rows, lanes, part), F32)] * depths,
             own, rim,
+            after=after,
         )
         halves = [halves[0]] + [to_peer(halves[k], "depth", k) for k in range(1, depths)]
         sums = call(
@@ -494,7 +501,7 @@
     far = call(
         functools.partial(stack_kernel, last),
         jax.ShapeDtypeStruct((last, rows, lanes, part), F32),
-        *back[first:],
+        *back[:first - 1 : -1],
     )
     return call(
         functools.partial(place_kernel, views, share),

time: 34.1 us -> 33.4 us (0.979)
  waiting for transfers between devices: 12.1 us -> 11.4 us
    ppermute x3, waiting for transfers between devices: 4.1 us -> 2.72 us  [to_origin(): lax.ppermute(block, axis, [(b, a) for a, b in pairs_of(lax.axis_size(axis...]
    ppermute x3, starting transfers between devices: 3.57 us -> 4.45 us  [to_origin(): lax.ppermute(block, axis, [(b, a) for a, b in pairs_of(lax.axis_size(axis...]
    ppermute x11, starting transfers between devices: 9.75 us -> 8.98 us  [to_peer(): return lax.ppermute(block, axis, pairs_of(lax.axis_size(axis), k))]
    ppermute x11, waiting for transfers between devices: 7.96 us -> 8.69 us  [to_peer(): return lax.ppermute(block, axis, pairs_of(lax.axis_size(axis), k))]
  transfers between devices with their start and end apart: 14 -> 14, of which waited for: 6 -> 8; matrix products, arithmetic and copies ran while one was open for 0% -> 0% of each run, Pallas kernels for 13% -> 11%
where the time goes in v3:
time: 33.4 us; the launch traced here: 33.2 us
  starting transfers between devices  13.4 us (40%)
  waiting for transfers between devices  11.4 us (34%)
  Pallas kernels  8.26 us (25%)
    ppermute x11, starting transfers between devices, to_peer(): return lax.ppermute(block, axis, pairs_of(lax.axis_size(axis), k))  8.98 us
    ppermute x11, waiting for transfers between devices, to_peer(): return lax.ppermute(block, axis, pairs_of(lax.axis_size(axis), k))  8.69 us
    pallas_call x17, Pallas kernels, call(): pl.pallas_call(run, out_shape=out_shape, in_specs=[pl.BlockSpec(memory_sp...  8.26 us
    ppermute x3, starting transfers between devices, to_origin(): lax.ppermute(block, axis, [(b, a) for a, b in pairs_of(lax.axis_size(axis...  4.45 us
    ppermute x3, waiting for transfers between devices, to_origin(): lax.ppermute(block, axis, [(b, a) for a, b in pairs_of(lax.axis_size(axis...  2.72 us
  transfers between devices with their start and end apart: 14, of which 8 were waited for; matrix products, arithmetic and copies ran while one was open for 0% of the time, Pallas kernels for 11%

profile of v3, /device:TPU:0, one launch (start us, length us, event | category | flops | bytes accessed | tf_op | source)
XLA Modules:
  0.0 33.2 jit_solution(12352433324088572342)
XLA Ops:
  0.0 1.0 %shard_map.55 = (f32[6,8,512]{2,1,0:T(8,128)S(1)}, f32[6,8,512]{2,1,0:T(8,128)S(1)}, f32[6,8,512]{2,1,0:T(8,128)S(1)}, f32[6,8,512]{2,1,0:T(8,128)S(1)}) custom-call(f32[1,32,2,512]{3,2,1,0:T(2,128)} %refs_0_.1, s32[1,4,2,512]{3,2,1,0:T(2,128)} %refs_1_.2, s32[1,4,2,512]{3,2,1,0:T(2,128)} %refs_2_.1, s32[2,1,4,2,512]{4,3,2,1,0:T(2,128)} %refs_3_.1), custom_call_target="tpu_custom_call" | custom-call | bytes 196608 | tf_op jit(solution)/shard_map/pallas_call | solution.py:47
  1.0 3.1 %collective-permute-start = (f32[6,8,512]{2,1,0:T(8,128)S(1)}, f32[6,8,512]{2,1,0:T(8,128)S(1)}, u32[]{:S(2)}, u32[]{:S(2)}) collective-permute-start(f32[6,8,512]{2,1,0:T(8,128)S(1)} %get-tuple-element.28), channel_id=1, source_target_pairs={{0,4},{4,0},{8,12},{12,8},{1,5},{5,1},{9,13},{13,9},{2,6},{6,2},{1... | collective-permute-start | bytes 294920 | tf_op jit(solution)/shard_map/ppermute | solution.py:29
  4.1 2.6 %collective-permute-start.1 = (f32[6,8,512]{2,1,0:T(8,128)S(1)}, f32[6,8,512]{2,1,0:T(8,128)S(1)}, u32[]{:S(2)}, u32[]{:S(2)}) collective-permute-start(f32[6,8,512]{2,1,0:T(8,128)S(1)} %get-tuple-element.29), channel_id=1, source_target_pairs={{0,8},{4,12},{8,0},{12,4},{1,9},{5,13},{9,1},{13,5},{2,10},{6,14},... | collective-permute-start | bytes 294920 | tf_op jit(solution)/shard_map/ppermute | solution.py:29
  6.7 0.2 collective-permute-done.refs_0_
  6.9 0.5 %collective-permute-start.5 = (f32[1,2,8,512]{3,2,1,0:T(8,128)S(1)}, f32[1,2,8,512]{3,2,1,0:T(8,128)S(1)}, u32[]{:S(2)}, u32[]{:S(2)}) collective-permute-start(f32[1,2,8,512]{3,2,1,0:T(8,128)S(1)} %shard_map.59), channel_id=1, source_target_pairs={{0,1},{1,0},{2,3},{3,2},{4,5},{5,4},{6,7},{7,6},{8,9},{9,8},{10,11... | collective-permute-start | bytes 98312 | tf_op jit(solution)/shard_map/ppermute | solution.py:29
  7.4 0.7 %collective-permute-done.3.refs_1_ = f32[1,2,8,512]{3,2,1,0:T(8,128)S(1)} collective-permute-done((f32[1,2,8,512]{3,2,1,0:T(8,128)S(1)}, f32[1,2,8,512]{3,2,1,0:T(8,128)S(1)}, u32[]{:S(2)}, u32[]{:S(2)}) %collective-permute-start.3) | collective-permute-done | bytes 32800 | tf_op jit(solution)/shard_map/ppermute | solution.py:29
  8.1 1.0 %shard_map.57 = (f32[4,2,8,512]{3,2,1,0:T(8,128)S(1)}, bf16[2,2048,256]{2,1,0:T(8,128)(2,1)S(1)}) custom-call(f32[6,8,512]{2,1,0:T(8,128)S(1)} %collective-permute-done.refs_0_, f32[1,2,8,512]{3,2,1,0:T(8,128)S(1)} %collective-permute-done.3.refs_1_), custom_call_target="tpu_custom_call" | custom-call | flops 335544320 | bytes 131072 | tf_op jit(solution)/shard_map/pallas_call | solution.py:47
  9.1 5.5 %collective-permute-done.1.refs_0_.refs_1_ = f32[6,8,512]{2,1,0:T(8,128)S(1)} collective-permute-done((f32[6,8,512]{2,1,0:T(8,128)S(1)}, f32[6,8,512]{2,1,0:T(8,128)S(1)}, u32[]{:S(2)}, u32[]{:S(2)}) %collective-permute-start.1) | collective-permute-done | bytes 98336 | tf_op jit(solution)/shard_map/ppermute | solution.py:29
  14.6 0.5 %collective-permute-start.4 = (f32[1,2,8,512]{3,2,1,0:T(8,128)S(1)}, f32[1,2,8,512]{3,2,1,0:T(8,128)S(1)}, u32[]{:S(2)}, u32[]{:S(2)}) collective-permute-start(f32[1,2,8,512]{3,2,1,0:T(8,128)S(1)} %shard_map.58.refs_2_), channel_id=1, source_target_pairs={{0,1},{1,0},{2,3},{3,2},{4,5},{5,4},{6,7},{7,6},{8,9},{9,8},{10,11... | collective-permute-start | bytes 98312 | tf_op jit(solution)/shard_map/ppermute | solution.py:29
  15.1 0.9 %shard_map.60 = (f32[4,2,8,512]{3,2,1,0:T(8,128)S(1)}, bf16[2,256,2048]{2,1,0:T(8,128)(2,1)S(1)}) custom-call(f32[6,8,512]{2,1,0:T(8,128)S(1)} %get-tuple-element.27.refs_0_, f32[1,2,8,512]{3,2,1,0:T(8,128)S(1)} %collective-permute-done.5.refs_1_, f32[1,2,8,512]{3,2,1,0:T(8,128)S(1)} %shard_map.56.refs_2_), custom_call_target="tpu_custom_call" | custom-call | flops 335544320 | bytes 131072 | tf_op jit(solution)/shard_map/pallas_call | solution.py:47
  16.0 0.9 %shard_map.62 = (f32[4,2,8,512]{3,2,1,0:T(8,128)S(1)}, bf16[2,256,2048]{2,1,0:T(8,128)(2,1)S(1)}) custom-call(f32[6,8,512]{2,1,0:T(8,128)S(1)} %collective-permute-done.1.refs_0_.refs_1_, f32[1,2,8,512]{3,2,1,0:T(8,128)S(1)} %collective-permute-done.6.refs_1_, f32[1,2,8,512]{3,2,1,0:T(8,128)S(1)} %shard_map.58.refs_2_), custom_call_target="tpu_custom_call" | custom-call | flops 335544320 | bytes 131072 | tf_op jit(solution)/shard_map/pallas_call | solution.py:47
  16.9 2.9 %shard_map.63 = (f32[3,2,8,512]{3,2,1,0:T(8,128)S(1)}, f32[3,2,8,512]{3,2,1,0:T(8,128)S(1)}, f32[4,2,8,512]{3,2,1,0:T(8,128)S(1)}) custom-call(f32[6,8,512]{2,1,0:T(8,128)S(1)} %collective-permute-done.refs_0_, f32[6,8,512]{2,1,0:T(8,128)S(1)} %collective-permute-done.1.refs_0_.refs_1_, f32[6,8,512]{2,1,0:T(8,128)S(1)} %collective-permute-done.2.refs_0_.refs_2_, ...), custom_call_target="tpu_custom_call" | custom-call | flops 1342177280 | bytes 9240576 | tf_op jit(solution)/shard_map/pallas_call | solution.py:47
  20.0 0.9 %shard_map.65 = (f32[1,2,8,512]{3,2,1,0:T(8,128)S(1)}, f32[1,2,8,512]{3,2,1,0:T(8,128)S(1)}) custom-call(f32[6,8,512]{2,1,0:T(8,128)S(1)} %get-tuple-element.27.refs_0_, f32[4,8,2,512]{3,2,1,0:T(2,128)S(1)} %copy-done, f32[4,2,8,512]{3,2,1,0:T(8,128)S(1)} %get-tuple-element.36.refs_2_, f32[4,2,8,512]{3,2,1,0:T(8,128)S(1)} %get-tuple-element.32.refs_5_.refs_3_, ...), custom_call_target="tpu_custom_call" | custom-call | flops 335544320 | bytes 4685824 | tf_op jit(solution)/shard_map/pallas_call | solution.py:47
  20.8 0.3 %collective-permute-done.9.refs_1_ = f32[3,2,8,512]{3,2,1,0:T(8,128)S(1)} collective-permute-done((f32[3,2,8,512]{3,2,1,0:T(8,128)S(1)}, f32[3,2,8,512]{3,2,1,0:T(8,128)S(1)}, u32[]{:S(2)}, u32[]{:S(2)}) %collective-permute-start.9) | collective-permute-done | bytes 98336 | tf_op jit(solution)/shard_map/ppermute | solution.py:29
  21.2 1.6 %collective-permute-start.10 = (f32[3,2,8,256]{3,2,1,0:T(8,128)S(1)}, f32[3,2,8,256]{3,2,1,0:T(8,128)S(1)}, u32[]{:S(2)}, u32[]{:S(2)}) collective-permute-start(f32[3,2,8,256]{3,2,1,0:T(8,128)S(1)} %get-tuple-element.45), channel_id=1, source_target_pairs={{0,2},{2,0},{1,3},{3,1},{4,6},{6,4},{5,7},{7,5},{8,10},{10,8},{9,1... | collective-permute-start | bytes 147464 | tf_op jit(solution)/shard_map/ppermute | solution.py:29
  22.8 1.2 %collective-permute-done.7.refs_1_ = f32[1,2,8,512]{3,2,1,0:T(8,128)S(1)} collective-permute-done((f32[1,2,8,512]{3,2,1,0:T(8,128)S(1)}, f32[1,2,8,512]{3,2,1,0:T(8,128)S(1)}, u32[]{:S(2)}, u32[]{:S(2)}) %collective-permute-start.7) | collective-permute-done | bytes 32800 | tf_op jit(solution)/shard_map/ppermute | solution.py:29
  24.0 0.6 %collective-permute-start.8 = (f32[1,2,8,256]{3,2,1,0:T(8,128)S(1)}, f32[1,2,8,256]{3,2,1,0:T(8,128)S(1)}, u32[]{:S(2)}, u32[]{:S(2)}) collective-permute-start(f32[1,2,8,256]{3,2,1,0:T(8,128)S(1)} %get-tuple-element.42), channel_id=1, source_target_pairs={{0,2},{2,0},{1,3},{3,1},{4,6},{6,4},{5,7},{7,5},{8,10},{10,8},{9,1... | collective-permute-start | bytes 49160 | tf_op jit(solution)/shard_map/ppermute | solution.py:29
  24.6 0.8 %collective-permute-done.10.refs_1_ = f32[3,2,8,256]{3,2,1,0:T(8,128)S(1)} collective-permute-done((f32[3,2,8,256]{3,2,1,0:T(8,128)S(1)}, f32[3,2,8,256]{3,2,1,0:T(8,128)S(1)}, u32[]{:S(2)}, u32[]{:S(2)}) %collective-permute-start.10) | collective-permute-done | bytes 49184 | tf_op jit(solution)/shard_map/ppermute | solution.py:29
  25.4 2.5 %collective-permute-start.11 = (f32[2,8,256]{2,1,0:T(8,128)S(1)}, f32[2,8,256]{2,1,0:T(8,128)S(1)}, u32[]{:S(2)}, u32[]{:S(2)}) collective-permute-start(f32[2,8,256]{2,1,0:T(8,128)S(1)} %get-tuple-element.46), channel_id=1, source_target_pairs={{12,0},{8,4},{4,8},{0,12},{13,1},{9,5},{5,9},{1,13},{14,2},{10,6},... | collective-permute-start | bytes 49160 | tf_op jit(solution)/shard_map/ppermute | solution.py:33
  27.9 0.2 collective-permute-start.12
  28.2 1.7 %collective-permute-start.13 = (f32[2,8,256]{2,1,0:T(8,128)S(1)}, f32[2,8,256]{2,1,0:T(8,128)S(1)}, u32[]{:S(2)}, u32[]{:S(2)}) collective-permute-start(f32[2,8,256]{2,1,0:T(8,128)S(1)} %get-tuple-element.48), channel_id=1, source_target_pairs={{4,0},{0,4},{12,8},{8,12},{5,1},{1,5},{13,9},{9,13},{6,2},{2,6},{1... | collective-permute-start | bytes 49160 | tf_op jit(solution)/shard_map/ppermute | solution.py:33
  29.8 1.1 %collective-permute-done.11.refs_0_ = f32[2,8,256]{2,1,0:T(8,128)S(1)} collective-permute-done((f32[2,8,256]{2,1,0:T(8,128)S(1)}, f32[2,8,256]{2,1,0:T(8,128)S(1)}, u32[]{:S(2)}, u32[]{:S(2)}) %collective-permute-start.11) | collective-permute-done | bytes 16416 | tf_op jit(solution)/shard_map/ppermute | solution.py:33
  31.0 1.6 %collective-permute-done.12.refs_1_ = f32[2,8,256]{2,1,0:T(8,128)S(1)} collective-permute-done((f32[2,8,256]{2,1,0:T(8,128)S(1)}, f32[2,8,256]{2,1,0:T(8,128)S(1)}, u32[]{:S(2)}, u32[]{:S(2)}) %collective-permute-start.12) | collective-permute-done | bytes 16416 | tf_op jit(solution)/shard_map/ppermute | solution.py:33
  32.6 0.7 %shard_map.71 = f32[1,32,2,256]{3,2,1,0:T(2,128)} custom-call(f32[2,8,256]{2,1,0:T(8,128)S(1)} %shard_map.67.refs_0_, f32[3,2,8,256]{3,2,1,0:T(8,128)S(1)} %shard_map.70.refs_1_), custom_call_target="tpu_custom_call" | custom-call | bytes 65536 | tf_op jit(solution)/shard_map/pallas_call | solution.py:47
  (23 shorter events, 0.2 us)
Async XLA Ops:
  1.0 5.9 %collective-permute-start = (f32[6,8,512]{2,1,0:T(8,128)S(1)}, f32[6,8,512]{2,1,0:T(8,128)S(1)}, u32[]{:S(2)}, u32[]{:S(2)}) collective-permute-start(f32[6,8,512]{2,1,0:T(8,128)S(1)} %get-tuple-element.28), channel_id=1, source_target_pairs={{0,4},{4,0},{8,12},{12,8},{1,5},{5,1},{9,13},{13,9},{2,6},{6,2},{1... | collective-permute-start | bytes 294920 | tf_op jit(solution)/shard_map/ppermute | solution.py:29
  4.1 10.4 %collective-permute-start.1 = (f32[6,8,512]{2,1,0:T(8,128)S(1)}, f32[6,8,512]{2,1,0:T(8,128)S(1)}, u32[]{:S(2)}, u32[]{:S(2)}) collective-permute-start(f32[6,8,512]{2,1,0:T(8,128)S(1)} %get-tuple-element.29), channel_id=1, source_target_pairs={{0,8},{4,12},{8,0},{12,4},{1,9},{5,13},{9,1},{13,5},{2,10},{6,14},... | collective-permute-start | bytes 294920 | tf_op jit(solution)/shard_map/ppermute | solution.py:29
  6.7 7.8 %collective-permute-start.2 = (f32[6,8,512]{2,1,0:T(8,128)S(1)}, f32[6,8,512]{2,1,0:T(8,128)S(1)}, u32[]{:S(2)}, u32[]{:S(2)}) collective-permute-start(f32[6,8,512]{2,1,0:T(8,128)S(1)} %get-tuple-element.30), channel_id=1, source_target_pairs={{0,12},{4,8},{8,4},{12,0},{1,13},{5,9},{9,5},{13,1},{2,14},{6,10},... | collective-permute-start | bytes 294920 | tf_op jit(solution)/shard_map/ppermute | solution.py:29
  6.9 1.2 %collective-permute-start.3 = (f32[1,2,8,512]{3,2,1,0:T(8,128)S(1)}, f32[1,2,8,512]{3,2,1,0:T(8,128)S(1)}, u32[]{:S(2)}, u32[]{:S(2)}) collective-permute-start(f32[1,2,8,512]{3,2,1,0:T(8,128)S(1)} %shard_map.56.refs_2_), channel_id=1, source_target_pairs={{0,1},{1,0},{2,3},{3,2},{4,5},{5,4},{6,7},{7,6},{8,9},{9,8},{10,11... | collective-permute-start | bytes 98312 | tf_op jit(solution)/shard_map/ppermute | solution.py:29
  6.9 9.9 %copy-start = (f32[4,8,2,512]{3,2,1,0:T(2,128)S(1)}, f32[4,8,2,512]{3,2,1,0:T(2,128)}, u32[]{:S(2)}) copy-start(f32[4,8,2,512]{3,2,1,0:T(2,128)} %refs_1_.3) | copy-start | bytes 393220
  6.9 8.1 %collective-permute-start.5 = (f32[1,2,8,512]{3,2,1,0:T(8,128)S(1)}, f32[1,2,8,512]{3,2,1,0:T(8,128)S(1)}, u32[]{:S(2)}, u32[]{:S(2)}) collective-permute-start(f32[1,2,8,512]{3,2,1,0:T(8,128)S(1)} %shard_map.59), channel_id=1, source_target_pairs={{0,1},{1,0},{2,3},{3,2},{4,5},{5,4},{6,7},{7,6},{8,9},{9,8},{10,11... | collective-permute-start | bytes 98312 | tf_op jit(solution)/shard_map/ppermute | solution.py:29
  14.6 1.4 %collective-permute-start.6 = (f32[1,2,8,512]{3,2,1,0:T(8,128)S(1)}, f32[1,2,8,512]{3,2,1,0:T(8,128)S(1)}, u32[]{:S(2)}, u32[]{:S(2)}) collective-permute-start(f32[1,2,8,512]{3,2,1,0:T(8,128)S(1)} %shard_map.61), channel_id=1, source_target_pairs={{0,1},{1,0},{2,3},{3,2},{4,5},{5,4},{6,7},{7,6},{8,9},{9,8},{10,11... | collective-permute-start | bytes 98312 | tf_op jit(solution)/shard_map/ppermute | solution.py:29
  14.6 2.3 %collective-permute-start.4 = (f32[1,2,8,512]{3,2,1,0:T(8,128)S(1)}, f32[1,2,8,512]{3,2,1,0:T(8,128)S(1)}, u32[]{:S(2)}, u32[]{:S(2)}) collective-permute-start(f32[1,2,8,512]{3,2,1,0:T(8,128)S(1)} %shard_map.58.refs_2_), channel_id=1, source_target_pairs={{0,1},{1,0},{2,3},{3,2},{4,5},{5,4},{6,7},{7,6},{8,9},{9,8},{10,11... | collective-permute-start | bytes 98312 | tf_op jit(solution)/shard_map/ppermute | solution.py:29
  19.8 1.4 %collective-permute-start.9 = (f32[3,2,8,512]{3,2,1,0:T(8,128)S(1)}, f32[3,2,8,512]{3,2,1,0:T(8,128)S(1)}, u32[]{:S(2)}, u32[]{:S(2)}) collective-permute-start(f32[3,2,8,512]{3,2,1,0:T(8,128)S(1)} %shard_map.64.refs_5_), channel_id=1, source_target_pairs={{0,1},{1,0},{2,3},{3,2},{4,5},{5,4},{6,7},{7,6},{8,9},{9,8},{10,11... | collective-permute-start | bytes 294920 | tf_op jit(solution)/shard_map/ppermute | solution.py:29
  21.2 4.2 %collective-permute-start.10 = (f32[3,2,8,256]{3,2,1,0:T(8,128)S(1)}, f32[3,2,8,256]{3,2,1,0:T(8,128)S(1)}, u32[]{:S(2)}, u32[]{:S(2)}) collective-permute-start(f32[3,2,8,256]{3,2,1,0:T(8,128)S(1)} %get-tuple-element.45), channel_id=1, source_target_pairs={{0,2},{2,0},{1,3},{3,1},{4,6},{6,4},{5,7},{7,5},{8,10},{10,8},{9,1... | collective-permute-start | bytes 147464 | tf_op jit(solution)/shard_map/ppermute | solution.py:29
  22.8 1.2 %collective-permute-start.7 = (f32[1,2,8,512]{3,2,1,0:T(8,128)S(1)}, f32[1,2,8,512]{3,2,1,0:T(8,128)S(1)}, u32[]{:S(2)}, u32[]{:S(2)}) collective-permute-start(f32[1,2,8,512]{3,2,1,0:T(8,128)S(1)} %get-tuple-element.40), channel_id=1, source_target_pairs={{0,1},{1,0},{2,3},{3,2},{4,5},{5,4},{6,7},{7,6},{8,9},{9,8},{10,11... | collective-permute-start | bytes 98312 | tf_op jit(solution)/shard_map/ppermute | solution.py:29
  24.0 5.8 %collective-permute-start.8 = (f32[1,2,8,256]{3,2,1,0:T(8,128)S(1)}, f32[1,2,8,256]{3,2,1,0:T(8,128)S(1)}, u32[]{:S(2)}, u32[]{:S(2)}) collective-permute-start(f32[1,2,8,256]{3,2,1,0:T(8,128)S(1)} %get-tuple-element.42), channel_id=1, source_target_pairs={{0,2},{2,0},{1,3},{3,1},{4,6},{6,4},{5,7},{7,5},{8,10},{10,8},{9,1... | collective-permute-start | bytes 49160 | tf_op jit(solution)/shard_map/ppermute | solution.py:29
  25.4 5.6 %collective-permute-start.11 = (f32[2,8,256]{2,1,0:T(8,128)S(1)}, f32[2,8,256]{2,1,0:T(8,128)S(1)}, u32[]{:S(2)}, u32[]{:S(2)}) collective-permute-start(f32[2,8,256]{2,1,0:T(8,128)S(1)} %get-tuple-element.46), channel_id=1, source_target_pairs={{12,0},{8,4},{4,8},{0,12},{13,1},{9,5},{5,9},{1,13},{14,2},{10,6},... | collective-permute-start | bytes 49160 | tf_op jit(solution)/shard_map/ppermute | solution.py:33
  27.9 4.6 %collective-permute-start.12 = (f32[2,8,256]{2,1,0:T(8,128)S(1)}, f32[2,8,256]{2,1,0:T(8,128)S(1)}, u32[]{:S(2)}, u32[]{:S(2)}) collective-permute-start(f32[2,8,256]{2,1,0:T(8,128)S(1)} %get-tuple-element.47), channel_id=1, source_target_pairs={{8,0},{12,4},{0,8},{4,12},{9,1},{13,5},{1,9},{5,13},{10,2},{14,6},... | collective-permute-start | bytes 49160 | tf_op jit(solution)/shard_map/ppermute | solution.py:33
  28.2 4.4 %collective-permute-start.13 = (f32[2,8,256]{2,1,0:T(8,128)S(1)}, f32[2,8,256]{2,1,0:T(8,128)S(1)}, u32[]{:S(2)}, u32[]{:S(2)}) collective-permute-start(f32[2,8,256]{2,1,0:T(8,128)S(1)} %get-tuple-element.48), channel_id=1, source_target_pairs={{4,0},{0,4},{12,8},{8,12},{5,1},{1,5},{13,9},{9,13},{6,2},{2,6},{1... | collective-permute-start | bytes 49160 | tf_op jit(solution)/shard_map/ppermute | solution.py:33

commit v4 on v3

--- a/solution.py
+++ b/solution.py
@@ -276,7 +276,7 @@
 
 def turn_kernel(z, unroll, keep, share, views, late, count, *refs):
     early, hots_in = views - late, (count - late if keep else 0)
-    packets, refs = refs[:count], refs[count:]
+    packets, refs = (refs[count - 1],) + refs[: count - 1], refs[count:]
     halo, cot_ref, refs = refs[0], refs[1], refs[2:]
     ahead, refs = refs[:early], refs[early:]
     hots, refs = refs[:hots_in], refs[hots_in:]
@@ -366,7 +366,7 @@
     me = lax.axis_index("view")
     rows = out_ref.shape[2]
     for k in range(views):
-        piece = refs[k] if k < near else refs[near].at[views - 1 - k]
+        piece = refs[k + 1] if k < near else refs[0].at[views - 1 - k]
         base = peer(me, k, views) * share
         for c in range(share):
             for r in range(rows):
@@ -429,21 +429,18 @@
         )
         return results[:count], results[count:]
 
-    halos = [halo_of(groups[0])]
-    for k in range(views - 1, 0, -1):
+    own_halo = halo_of([0])[1]
+    for k in range(1, views):
         packets[k] = to_peer(packets[k], "view", k)
-    halos.append(halo_of(groups[1]))
-    warped, hots = ahead(groups[0], halos[0][1], (halos[1][0],))
-    for at in range(1, len(groups) - 1):
-        if at == len(groups) - 2:
-            halos.append(halo_of(groups[at + 1], warped[-1:]))
-            after = (halos[at + 1][0],)
-        else:
-            after = ()
-        more, more_hots = ahead(groups[at], halos[at][1], after, keep and groups[at] == [1])
+    warped, hots = ahead([0], own_halo)
+    middle = list(range(1, views - late))
+    sent, middle_halo = halo_of(middle[::-1], warped)
+    last_sent, last_halo = halo_of(groups[-1], (sent,))
+    for k in middle:
+        at = len(middle) - k
+        after = (last_sent,) if k == 1 else warped[-1:]
+        more, more_hots = ahead([k], middle_halo[at : at + 1], after, keep and k == 1)
         warped, hots = warped + more, hots + more_hots
-        if at + 1 < len(groups) - 1:
-            halos.append(halo_of(groups[at + 1], warped[-1:]))
     first = max(views // 4, 1)
     last = views - first
     work = [
@@ -462,7 +459,7 @@
     own, rim, mean = call(
         functools.partial(turn_kernel, z, unroll, keep, share, views, late, last),
         results_of(last) + [warp],
-        *packets[first:], halos[-1][1], cotangent, *warped, *hots[first:],
+        *packets[first + 1 :], packets[first], last_halo, cotangent, *warped, *hots[first:],
         scratch=[
             pltpu.VMEM((late,) + warp.shape, F32),
             pltpu.VMEM((late if keep else 1,) + hot.shape, BF),
@@ -506,7 +503,7 @@
     return call(
         functools.partial(place_kernel, views, share),
         jax.ShapeDtypeStruct((1, channels, rows, part), F32),
-        *back[:first], far,
+        far, *back[:first],
     )
 
 

time: 33.4 us -> 33.1 us (level)
  starting transfers between devices: 13.4 us -> 13 us
    ppermute x3, waiting for transfers between devices: 2.72 us -> 3.47 us  [to_origin(): lax.ppermute(block, axis, [(b, a) for a, b in pairs_of(lax.axis_size(axis...]
    ppermute x11 -> x10, waiting for transfers between devices: 8.69 us -> 8.12 us  [to_peer(): return lax.ppermute(block, axis, pairs_of(lax.axis_size(axis), k))]
    ppermute x11 -> x10, starting transfers between devices: 8.98 us -> 8.56 us  [to_peer(): return lax.ppermute(block, axis, pairs_of(lax.axis_size(axis), k))]
    pallas_call x17 -> x16, Pallas kernels: 8.26 us -> 8.26 us  [call(): pl.pallas_call(run, out_shape=out_shape, in_specs=[pl.BlockSpec(memory_sp...]
  transfers between devices with their start and end apart: 14 -> 13, of which waited for: 8 -> 9; matrix products, arithmetic and copies ran while one was open for 0% -> 0% of each run, Pallas kernels for 11% -> 11%
where the time goes in v4:
time: 33.1 us; the launch traced here: 33 us
  starting transfers between devices  13 us (39%)
  waiting for transfers between devices  11.6 us (35%)
  Pallas kernels  8.26 us (25%)
    ppermute x10, starting transfers between devices, to_peer(): return lax.ppermute(block, axis, pairs_of(lax.axis_size(axis), k))  8.56 us
    pallas_call x16, Pallas kernels, call(): pl.pallas_call(run, out_shape=out_shape, in_specs=[pl.BlockSpec(memory_sp...  8.26 us
    ppermute x10, waiting for transfers between devices, to_peer(): return lax.ppermute(block, axis, pairs_of(lax.axis_size(axis), k))  8.12 us
    ppermute x3, starting transfers between devices, to_origin(): lax.ppermute(block, axis, [(b, a) for a, b in pairs_of(lax.axis_size(axis...  4.45 us
    ppermute x3, waiting for transfers between devices, to_origin(): lax.ppermute(block, axis, [(b, a) for a, b in pairs_of(lax.axis_size(axis...  3.47 us
  transfers between devices with their start and end apart: 13, of which 9 were waited for; matrix products, arithmetic and copies ran while one was open for 0% of the time, Pallas kernels for 11%

profile of v4, /device:TPU:0, one launch (start us, length us, event | category | flops | bytes accessed | tf_op | source)
XLA Modules:
  0.0 33.0 jit_solution(8505699698165606832)
XLA Ops:
  0.0 1.0 %shard_map.55 = (f32[6,8,512]{2,1,0:T(8,128)S(1)}, f32[6,8,512]{2,1,0:T(8,128)S(1)}, f32[6,8,512]{2,1,0:T(8,128)S(1)}, f32[6,8,512]{2,1,0:T(8,128)S(1)}) custom-call(f32[1,32,2,512]{3,2,1,0:T(2,128)} %refs_0_.1, s32[1,4,2,512]{3,2,1,0:T(2,128)} %refs_1_.2, s32[1,4,2,512]{3,2,1,0:T(2,128)} %refs_2_.1, s32[2,1,4,2,512]{4,3,2,1,0:T(2,128)} %refs_3_.1), custom_call_target="tpu_custom_call" | custom-call | bytes 196608 | tf_op jit(solution)/shard_map/pallas_call | solution.py:47
  1.0 4.1 %collective-permute-start = (f32[6,8,512]{2,1,0:T(8,128)S(1)}, f32[6,8,512]{2,1,0:T(8,128)S(1)}, u32[]{:S(2)}, u32[]{:S(2)}) collective-permute-start(f32[6,8,512]{2,1,0:T(8,128)S(1)} %get-tuple-element.27), channel_id=1, source_target_pairs={{0,8},{4,12},{8,0},{12,4},{1,9},{5,13},{9,1},{13,5},{2,10},{6,14},... | collective-permute-start | bytes 294920 | tf_op jit(solution)/shard_map/ppermute | solution.py:29
  5.1 1.6 %collective-permute-start.2 = (f32[6,8,512]{2,1,0:T(8,128)S(1)}, f32[6,8,512]{2,1,0:T(8,128)S(1)}, u32[]{:S(2)}, u32[]{:S(2)}) collective-permute-start(f32[6,8,512]{2,1,0:T(8,128)S(1)} %get-tuple-element.29), channel_id=1, source_target_pairs={{0,4},{4,0},{8,12},{12,8},{1,5},{5,1},{9,13},{13,9},{2,6},{6,2},{1... | collective-permute-start | bytes 294920 | tf_op jit(solution)/shard_map/ppermute | solution.py:29
  6.7 0.1 collective-permute-start.1
  6.8 1.1 %collective-permute-done.3.refs_1_ = f32[1,2,8,512]{3,2,1,0:T(8,128)S(1)} collective-permute-done((f32[1,2,8,512]{3,2,1,0:T(8,128)S(1)}, f32[1,2,8,512]{3,2,1,0:T(8,128)S(1)}, u32[]{:S(2)}, u32[]{:S(2)}) %collective-permute-start.3) | collective-permute-done | bytes 32800 | tf_op jit(solution)/shard_map/ppermute | solution.py:29
  7.9 0.9 %shard_map.57 = (f32[4,2,8,512]{3,2,1,0:T(8,128)S(1)}, bf16[2,256,2048]{2,1,0:T(8,128)(2,1)S(1)}) custom-call(f32[6,8,512]{2,1,0:T(8,128)S(1)} %get-tuple-element.30.refs_0_, f32[1,2,8,512]{3,2,1,0:T(8,128)S(1)} %collective-permute-done.3.refs_1_), custom_call_target="tpu_custom_call" | custom-call | flops 335544320 | bytes 131072 | tf_op jit(solution)/shard_map/pallas_call | solution.py:47
  8.8 1.2 %collective-permute-done.refs_0_ = f32[6,8,512]{2,1,0:T(8,128)S(1)} collective-permute-done((f32[6,8,512]{2,1,0:T(8,128)S(1)}, f32[6,8,512]{2,1,0:T(8,128)S(1)}, u32[]{:S(2)}, u32[]{:S(2)}) %collective-permute-start) | collective-permute-done | bytes 98336 | tf_op jit(solution)/shard_map/ppermute | solution.py:29
  10.0 0.4 %collective-permute-done.2.refs_1_.refs_0_.refs_2_ = f32[6,8,512]{2,1,0:T(8,128)S(1)} collective-permute-done((f32[6,8,512]{2,1,0:T(8,128)S(1)}, f32[6,8,512]{2,1,0:T(8,128)S(1)}, u32[]{:S(2)}, u32[]{:S(2)}) %collective-permute-start.2) | collective-permute-done | bytes 98336 | tf_op jit(solution)/shard_map/ppermute | solution.py:29
  10.4 3.5 %collective-permute-done.1.refs_0_.refs_1_ = f32[6,8,512]{2,1,0:T(8,128)S(1)} collective-permute-done((f32[6,8,512]{2,1,0:T(8,128)S(1)}, f32[6,8,512]{2,1,0:T(8,128)S(1)}, u32[]{:S(2)}, u32[]{:S(2)}) %collective-permute-start.1) | collective-permute-done | bytes 98336 | tf_op jit(solution)/shard_map/ppermute | solution.py:29
  13.9 1.0 %shard_map.60 = (f32[4,2,8,512]{3,2,1,0:T(8,128)S(1)}, bf16[2,2048,256]{2,1,0:T(8,128)(2,1)S(1)}) custom-call(f32[6,8,512]{2,1,0:T(8,128)S(1)} %collective-permute-done.2.refs_1_.refs_0_.refs_2_, f32[1,2,8,512]{3,2,1,0:T(8,128)S(1)} %get-tuple-element.50.refs_1_, f32[1,2,8,512]{3,2,1,0:T(8,128)S(1)} %shard_map.59.refs_2_), custom_call_target="tpu_custom_call" | custom-call | flops 335544320 | bytes 131072 | tf_op jit(solution)/shard_map/pallas_call | solution.py:47
  14.8 0.9 %shard_map.61 = (f32[4,2,8,512]{3,2,1,0:T(8,128)S(1)}, bf16[2,256,2048]{2,1,0:T(8,128)(2,1)S(1)}) custom-call(f32[6,8,512]{2,1,0:T(8,128)S(1)} %collective-permute-done.refs_0_, f32[1,2,8,512]{3,2,1,0:T(8,128)S(1)} %get-tuple-element.49.refs_1_, f32[4,2,8,512]{3,2,1,0:T(8,128)S(1)} %get-tuple-element.32.refs_2_.refs_6_), custom_call_target="tpu_custom_call" | custom-call | flops 335544320 | bytes 131072 | tf_op jit(solution)/shard_map/pallas_call | solution.py:47
  15.7 2.9 %shard_map.62 = (f32[3,2,8,512]{3,2,1,0:T(8,128)S(1)}, f32[3,2,8,512]{3,2,1,0:T(8,128)S(1)}, f32[4,2,8,512]{3,2,1,0:T(8,128)S(1)}) custom-call(f32[6,8,512]{2,1,0:T(8,128)S(1)} %collective-permute-done.refs_0_, f32[6,8,512]{2,1,0:T(8,128)S(1)} %collective-permute-done.1.refs_0_.refs_1_, f32[6,8,512]{2,1,0:T(8,128)S(1)} %collective-permute-done.2.refs_1_.refs_0_.refs_2_, ...), custom_call_target="tpu_custom_call" | custom-call | flops 1342177280 | bytes 9240576 | tf_op jit(solution)/shard_map/pallas_call | solution.py:47
  18.7 0.6 %collective-permute-start.6 = (f32[3,2,8,512]{3,2,1,0:T(8,128)S(1)}, f32[3,2,8,512]{3,2,1,0:T(8,128)S(1)}, u32[]{:S(2)}, u32[]{:S(2)}) collective-permute-start(f32[3,2,8,512]{3,2,1,0:T(8,128)S(1)} %shard_map.63.refs_5_), channel_id=1, source_target_pairs={{0,1},{1,0},{2,3},{3,2},{4,5},{5,4},{6,7},{7,6},{8,9},{9,8},{10,11... | collective-permute-start | bytes 294920 | tf_op jit(solution)/shard_map/ppermute | solution.py:29
  19.2 0.9 %shard_map.64 = (f32[1,2,8,512]{3,2,1,0:T(8,128)S(1)}, f32[1,2,8,512]{3,2,1,0:T(8,128)S(1)}) custom-call(f32[6,8,512]{2,1,0:T(8,128)S(1)} %get-tuple-element.30.refs_0_, f32[4,8,2,512]{3,2,1,0:T(2,128)S(1)} %copy-done, f32[4,2,8,512]{3,2,1,0:T(8,128)S(1)} %get-tuple-element.38.refs_2_, f32[4,2,8,512]{3,2,1,0:T(8,128)S(1)} %get-tuple-element.31.refs_2_.refs_5_.refs_3_, ...), custom_call_target="tpu_custom_call" | custom-call | flops 335544320 | bytes 4685824 | tf_op jit(solution)/shard_map/pallas_call | solution.py:47
  20.1 0.1 collective-permute-done.6.refs_1_
  20.2 1.6 %collective-permute-start.7 = (f32[3,2,8,256]{3,2,1,0:T(8,128)S(1)}, f32[3,2,8,256]{3,2,1,0:T(8,128)S(1)}, u32[]{:S(2)}, u32[]{:S(2)}) collective-permute-start(f32[3,2,8,256]{3,2,1,0:T(8,128)S(1)} %get-tuple-element.42), channel_id=1, source_target_pairs={{0,2},{2,0},{1,3},{3,1},{4,6},{6,4},{5,7},{7,5},{8,10},{10,8},{9,1... | collective-permute-start | bytes 147464 | tf_op jit(solution)/shard_map/ppermute | solution.py:29
  21.8 1.1 %collective-permute-done.11.refs_1_ = f32[1,2,8,512]{3,2,1,0:T(8,128)S(1)} collective-permute-done((f32[1,2,8,512]{3,2,1,0:T(8,128)S(1)}, f32[1,2,8,512]{3,2,1,0:T(8,128)S(1)}, u32[]{:S(2)}, u32[]{:S(2)}) %collective-permute-start.11) | collective-permute-done | bytes 32800 | tf_op jit(solution)/shard_map/ppermute | solution.py:29
  23.0 0.6 %collective-permute-start.12 = (f32[1,2,8,256]{3,2,1,0:T(8,128)S(1)}, f32[1,2,8,256]{3,2,1,0:T(8,128)S(1)}, u32[]{:S(2)}, u32[]{:S(2)}) collective-permute-start(f32[1,2,8,256]{3,2,1,0:T(8,128)S(1)} %get-tuple-element.48), channel_id=1, source_target_pairs={{0,2},{2,0},{1,3},{3,1},{4,6},{6,4},{5,7},{7,5},{8,10},{10,8},{9,1... | collective-permute-start | bytes 49160 | tf_op jit(solution)/shard_map/ppermute | solution.py:29
  23.6 0.8 %collective-permute-done.7.refs_1_ = f32[3,2,8,256]{3,2,1,0:T(8,128)S(1)} collective-permute-done((f32[3,2,8,256]{3,2,1,0:T(8,128)S(1)}, f32[3,2,8,256]{3,2,1,0:T(8,128)S(1)}, u32[]{:S(2)}, u32[]{:S(2)}) %collective-permute-start.7) | collective-permute-done | bytes 49184 | tf_op jit(solution)/shard_map/ppermute | solution.py:29
  24.4 3.2 %collective-permute-start.8 = (f32[2,8,256]{2,1,0:T(8,128)S(1)}, f32[2,8,256]{2,1,0:T(8,128)S(1)}, u32[]{:S(2)}, u32[]{:S(2)}) collective-permute-start(f32[2,8,256]{2,1,0:T(8,128)S(1)} %get-tuple-element.43), channel_id=1, source_target_pairs={{12,0},{8,4},{4,8},{0,12},{13,1},{9,5},{5,9},{1,13},{14,2},{10,6},... | collective-permute-start | bytes 49160 | tf_op jit(solution)/shard_map/ppermute | solution.py:33
  27.6 1.3 %collective-permute-start.10 = (f32[2,8,256]{2,1,0:T(8,128)S(1)}, f32[2,8,256]{2,1,0:T(8,128)S(1)}, u32[]{:S(2)}, u32[]{:S(2)}) collective-permute-start(f32[2,8,256]{2,1,0:T(8,128)S(1)} %get-tuple-element.45), channel_id=1, source_target_pairs={{4,0},{0,4},{12,8},{8,12},{5,1},{1,5},{13,9},{9,13},{6,2},{2,6},{1... | collective-permute-start | bytes 49160 | tf_op jit(solution)/shard_map/ppermute | solution.py:33
  28.8 1.2 %collective-permute-done.8.refs_0_ = f32[2,8,256]{2,1,0:T(8,128)S(1)} collective-permute-done((f32[2,8,256]{2,1,0:T(8,128)S(1)}, f32[2,8,256]{2,1,0:T(8,128)S(1)}, u32[]{:S(2)}, u32[]{:S(2)}) %collective-permute-start.8) | collective-permute-done | bytes 16416 | tf_op jit(solution)/shard_map/ppermute | solution.py:33
  30.1 2.2 %collective-permute-done.9.refs_1_ = f32[2,8,256]{2,1,0:T(8,128)S(1)} collective-permute-done((f32[2,8,256]{2,1,0:T(8,128)S(1)}, f32[2,8,256]{2,1,0:T(8,128)S(1)}, u32[]{:S(2)}, u32[]{:S(2)}) %collective-permute-start.9) | collective-permute-done | bytes 16416 | tf_op jit(solution)/shard_map/ppermute | solution.py:33
  32.3 0.7 %shard_map.70 = f32[1,32,2,256]{3,2,1,0:T(2,128)} custom-call(f32[3,2,8,256]{3,2,1,0:T(8,128)S(1)} %shard_map.67.refs_0_, f32[2,8,256]{2,1,0:T(8,128)S(1)} %shard_map.69.refs_1_), custom_call_target="tpu_custom_call" | custom-call | bytes 65536 | tf_op jit(solution)/shard_map/pallas_call | solution.py:47
  (21 shorter events, 0.2 us)
Async XLA Ops:
  1.0 9.0 %collective-permute-start = (f32[6,8,512]{2,1,0:T(8,128)S(1)}, f32[6,8,512]{2,1,0:T(8,128)S(1)}, u32[]{:S(2)}, u32[]{:S(2)}) collective-permute-start(f32[6,8,512]{2,1,0:T(8,128)S(1)} %get-tuple-element.27), channel_id=1, source_target_pairs={{0,8},{4,12},{8,0},{12,4},{1,9},{5,13},{9,1},{13,5},{2,10},{6,14},... | collective-permute-start | bytes 294920 | tf_op jit(solution)/shard_map/ppermute | solution.py:29
  5.1 5.2 %collective-permute-start.2 = (f32[6,8,512]{2,1,0:T(8,128)S(1)}, f32[6,8,512]{2,1,0:T(8,128)S(1)}, u32[]{:S(2)}, u32[]{:S(2)}) collective-permute-start(f32[6,8,512]{2,1,0:T(8,128)S(1)} %get-tuple-element.29), channel_id=1, source_target_pairs={{0,4},{4,0},{8,12},{12,8},{1,5},{5,1},{9,13},{13,9},{2,6},{6,2},{1... | collective-permute-start | bytes 294920 | tf_op jit(solution)/shard_map/ppermute | solution.py:29
  6.7 1.2 %collective-permute-start.3 = (f32[1,2,8,512]{3,2,1,0:T(8,128)S(1)}, f32[1,2,8,512]{3,2,1,0:T(8,128)S(1)}, u32[]{:S(2)}, u32[]{:S(2)}) collective-permute-start(f32[1,2,8,512]{3,2,1,0:T(8,128)S(1)} %shard_map.56), channel_id=1, source_target_pairs={{0,1},{1,0},{2,3},{3,2},{4,5},{5,4},{6,7},{7,6},{8,9},{9,8},{10,11... | collective-permute-start | bytes 98312 | tf_op jit(solution)/shard_map/ppermute | solution.py:29
  6.7 9.0 %copy-start = (f32[4,8,2,512]{3,2,1,0:T(2,128)S(1)}, f32[4,8,2,512]{3,2,1,0:T(2,128)}, u32[]{:S(2)}) copy-start(f32[4,8,2,512]{3,2,1,0:T(2,128)} %refs_1_.3) | copy-start | bytes 393220
  6.7 7.1 %collective-permute-start.1 = (f32[6,8,512]{2,1,0:T(8,128)S(1)}, f32[6,8,512]{2,1,0:T(8,128)S(1)}, u32[]{:S(2)}, u32[]{:S(2)}) collective-permute-start(f32[6,8,512]{2,1,0:T(8,128)S(1)} %get-tuple-element.28), channel_id=1, source_target_pairs={{0,12},{4,8},{8,4},{12,0},{1,13},{5,9},{9,5},{13,1},{2,14},{6,10},... | collective-permute-start | bytes 294920 | tf_op jit(solution)/shard_map/ppermute | solution.py:29
  10.4 3.5 %collective-permute-start.5 = (f32[2,2,8,512]{3,2,1,0:T(8,128)S(1)}, f32[2,2,8,512]{3,2,1,0:T(8,128)S(1)}, u32[]{:S(2)}, u32[]{:S(2)}) collective-permute-start(f32[2,2,8,512]{3,2,1,0:T(8,128)S(1)} %shard_map.58.refs_1_), channel_id=1, source_target_pairs={{0,1},{1,0},{2,3},{3,2},{4,5},{5,4},{6,7},{7,6},{8,9},{9,8},{10,11... | collective-permute-start | bytes 196616 | tf_op jit(solution)/shard_map/ppermute | solution.py:29
  13.8 1.9 %collective-permute-start.4 = (f32[1,2,8,512]{3,2,1,0:T(8,128)S(1)}, f32[1,2,8,512]{3,2,1,0:T(8,128)S(1)}, u32[]{:S(2)}, u32[]{:S(2)}) collective-permute-start(f32[1,2,8,512]{3,2,1,0:T(8,128)S(1)} %shard_map.59.refs_2_), channel_id=1, source_target_pairs={{0,1},{1,0},{2,3},{3,2},{4,5},{5,4},{6,7},{7,6},{8,9},{9,8},{10,11... | collective-permute-start | bytes 98312 | tf_op jit(solution)/shard_map/ppermute | solution.py:29
  18.7 1.5 %collective-permute-start.6 = (f32[3,2,8,512]{3,2,1,0:T(8,128)S(1)}, f32[3,2,8,512]{3,2,1,0:T(8,128)S(1)}, u32[]{:S(2)}, u32[]{:S(2)}) collective-permute-start(f32[3,2,8,512]{3,2,1,0:T(8,128)S(1)} %shard_map.63.refs_5_), channel_id=1, source_target_pairs={{0,1},{1,0},{2,3},{3,2},{4,5},{5,4},{6,7},{7,6},{8,9},{9,8},{10,11... | collective-permute-start | bytes 294920 | tf_op jit(solution)/shard_map/ppermute | solution.py:29
  20.2 4.2 %collective-permute-start.7 = (f32[3,2,8,256]{3,2,1,0:T(8,128)S(1)}, f32[3,2,8,256]{3,2,1,0:T(8,128)S(1)}, u32[]{:S(2)}, u32[]{:S(2)}) collective-permute-start(f32[3,2,8,256]{3,2,1,0:T(8,128)S(1)} %get-tuple-element.42), channel_id=1, source_target_pairs={{0,2},{2,0},{1,3},{3,1},{4,6},{6,4},{5,7},{7,5},{8,10},{10,8},{9,1... | collective-permute-start | bytes 147464 | tf_op jit(solution)/shard_map/ppermute | solution.py:29
  21.8 1.2 %collective-permute-start.11 = (f32[1,2,8,512]{3,2,1,0:T(8,128)S(1)}, f32[1,2,8,512]{3,2,1,0:T(8,128)S(1)}, u32[]{:S(2)}, u32[]{:S(2)}) collective-permute-start(f32[1,2,8,512]{3,2,1,0:T(8,128)S(1)} %get-tuple-element.46), channel_id=1, source_target_pairs={{0,1},{1,0},{2,3},{3,2},{4,5},{5,4},{6,7},{7,6},{8,9},{9,8},{10,11... | collective-permute-start | bytes 98312 | tf_op jit(solution)/shard_map/ppermute | solution.py:29
  23.0 5.8 %collective-permute-start.12 = (f32[1,2,8,256]{3,2,1,0:T(8,128)S(1)}, f32[1,2,8,256]{3,2,1,0:T(8,128)S(1)}, u32[]{:S(2)}, u32[]{:S(2)}) collective-permute-start(f32[1,2,8,256]{3,2,1,0:T(8,128)S(1)} %get-tuple-element.48), channel_id=1, source_target_pairs={{0,2},{2,0},{1,3},{3,1},{4,6},{6,4},{5,7},{7,5},{8,10},{10,8},{9,1... | collective-permute-start | bytes 49160 | tf_op jit(solution)/shard_map/ppermute | solution.py:29
  24.4 5.7 %collective-permute-start.8 = (f32[2,8,256]{2,1,0:T(8,128)S(1)}, f32[2,8,256]{2,1,0:T(8,128)S(1)}, u32[]{:S(2)}, u32[]{:S(2)}) collective-permute-start(f32[2,8,256]{2,1,0:T(8,128)S(1)} %get-tuple-element.43), channel_id=1, source_target_pairs={{12,0},{8,4},{4,8},{0,12},{13,1},{9,5},{5,9},{1,13},{14,2},{10,6},... | collective-permute-start | bytes 49160 | tf_op jit(solution)/shard_map/ppermute | solution.py:33
  27.5 4.8 %collective-permute-start.9 = (f32[2,8,256]{2,1,0:T(8,128)S(1)}, f32[2,8,256]{2,1,0:T(8,128)S(1)}, u32[]{:S(2)}, u32[]{:S(2)}) collective-permute-start(f32[2,8,256]{2,1,0:T(8,128)S(1)} %get-tuple-element.44), channel_id=1, source_target_pairs={{8,0},{12,4},{0,8},{4,12},{9,1},{13,5},{1,9},{5,13},{10,2},{14,6},... | collective-permute-start | bytes 49160 | tf_op jit(solution)/shard_map/ppermute | solution.py:33
  27.6 4.7 %collective-permute-start.10 = (f32[2,8,256]{2,1,0:T(8,128)S(1)}, f32[2,8,256]{2,1,0:T(8,128)S(1)}, u32[]{:S(2)}, u32[]{:S(2)}) collective-permute-start(f32[2,8,256]{2,1,0:T(8,128)S(1)} %get-tuple-element.45), channel_id=1, source_target_pairs={{4,0},{0,4},{12,8},{8,12},{5,1},{1,5},{13,9},{9,13},{6,2},{2,6},{1... | collective-permute-start | bytes 49160 | tf_op jit(solution)/shard_map/ppermute | solution.py:33

commit v5 on v4

--- a/solution.py
+++ b/solution.py
@@ -156,7 +156,7 @@
         lax.fori_loop(0, z.planes, lambda d, carry: (step(d), carry)[1], 0)
 
 
-def forward(z, unroll, packet, halo, warped_ref, w_ref, t_ref, f_ref, b_ref):
+def forward(z, unroll, fresh, packet, halo, warped_ref, w_ref, t_ref, f_ref, b_ref):
     is_first = lax.axis_index("row") == 0
     look_up(z, packet, t_ref)
     half = z.window * 2 * z.lanes
@@ -178,7 +178,8 @@
 
     def step(d):
         for y in range(z.rows):
-            build(z, t_ref, w_ref, d, y)
+            if fresh:
+                build(z, t_ref, w_ref, d, y)
             at = pl.ds(d * z.rows + y, 1)
             columns = pl.ds(pl.multiple_of(d * z.width, 128), z.width)
             p = jnp.dot(f_ref[y], w_ref[y, :, columns], preferred_element_type=F32)
@@ -198,17 +199,27 @@
     each_plane(z, unroll, step)
 
 
+def hot_kernel(z, unroll, packet, hot, t_ref):
+    look_up(z, packet, t_ref)
+
+    def step(d):
+        for y in range(z.rows):
+            build(z, t_ref, hot, d, y)
+
+    each_plane(z, unroll, step)
+
+
 def ahead_kernel(z, unroll, keep, turned, count, *refs):
-    packets, halo = refs[:count], refs[count]
-    own_hot = turned or not keep
-    outs = refs[count + 1 : -4 if own_hot else -3]
+    packets, halo, refs = refs[:count], refs[count], refs[count + 1 :]
+    if keep:
+        hots, refs = refs[:count], refs[count:]
     t_ref, f_ref, b_ref = refs[-3:]
     for v in range(count):
-        w_ref = refs[-4] if own_hot else outs[count + v]
-        forward(z, unroll, packets[v], halo.at[v], outs[v], w_ref, t_ref, f_ref, b_ref)
+        hot = hots[v] if keep else refs[-4]
+        forward(z, unroll, not keep, packets[v], halo.at[v], refs[v], hot, t_ref, f_ref, b_ref)
         if turned:
             for y in range(z.rows):
-                outs[count + v][y] = w_ref[y].T
+                refs[count + v][y] = hot[y].T
 
 
 def backward(z, unroll, share, views, packet, warped, mean_ref, cot_ref, hot, fresh, turned, work, own_ref, rim_ref):
@@ -274,17 +285,18 @@
         rim_ref[r] = jnp.where(is_first, grad_ref[HALO + z.rows + r], grad_ref[r])
 
 
-def turn_kernel(z, unroll, keep, share, views, late, count, *refs):
-    early, hots_in = views - late, (count - late if keep else 0)
+def turn_kernel(z, unroll, keep, share, views, late, ids, *refs):
+    count = len(ids)
+    early, hots_in = views - late, (count if keep else 0)
     packets, refs = (refs[count - 1],) + refs[: count - 1], refs[count:]
     halo, cot_ref, refs = refs[0], refs[1], refs[2:]
     ahead, refs = refs[:early], refs[early:]
     hots, refs = refs[:hots_in], refs[hots_in:]
     own_ref, rim_ref, mean_ref, warped_ref, w_ref, t_ref, f_ref, b_ref, l_ref, grad_ref, e_ref = refs
     for v in range(late):
-        hot = w_ref.at[v if keep else 0]
+        hot = hots[count - late + v] if keep else w_ref.at[0]
         packet = packets[count - late + v]
-        forward(z, unroll, packet, halo.at[v], warped_ref.at[v], hot, t_ref.at[0], f_ref, b_ref)
+        forward(z, unroll, not keep, packet, halo.at[v], warped_ref.at[v], hot, t_ref.at[0], f_ref, b_ref)
     warped = list(ahead) + [warped_ref.at[v] for v in range(late)]
 
     def average(d):
@@ -295,10 +307,10 @@
     for v in reversed(range(count)):
         hot = w_ref.at[0]
         if keep:
-            hot = hots[v] if v < count - late else w_ref.at[v - (count - late)]
+            hot = hots[v]
         work = t_ref.at[v % 2], l_ref.at[v % 2], grad_ref.at[v % 2], e_ref.at[v % 2]
         backward(
-            z, unroll, share, views, packets[v], warped[views - count + v], mean_ref, cot_ref, hot,
+            z, unroll, share, views, packets[v], warped[ids[v]], mean_ref, cot_ref, hot,
             not keep, keep and hot.shape != w_ref.at[0].shape, work, own_ref.at[v], rim_ref.at[v],
         )
 
@@ -416,33 +428,45 @@
         )
         return own_rows, to_peer(own_rows, "row", 1)
 
-    def ahead(group, halo, after=(), turned=False):
+    def hot_of(k, after=()):
+        return call(
+            functools.partial(hot_kernel, z, unroll), hot, packets[k],
+            scratch=[z.lookups()], flops=flops // 4, after=after,
+        )
+
+    def ahead(group, halo, hots, after=(), turned=False):
         count = len(group)
         shape = jax.ShapeDtypeStruct(z.one_hot(turned), BF)
         results = call(
             functools.partial(ahead_kernel, z, unroll, keep, turned, count),
-            [warp] * count + ([shape] * count if keep else []),
-            *[packets[k] for k in group], halo,
-            scratch=([] if keep and not turned else [pltpu.VMEM(hot.shape, BF)]) + tables,
+            [warp] * count + ([shape] * count if turned else []),
+            *[packets[k] for k in group], halo, *hots,
+            scratch=([] if keep else [pltpu.VMEM(hot.shape, BF)]) + tables,
             flops=flops * count,
             after=after,
         )
-        return results[:count], results[count:]
+        results = list(results)
+        return results[:count], results[count:] or list(hots)
 
     own_halo = halo_of([0])[1]
     for k in range(1, views):
         packets[k] = to_peer(packets[k], "view", k)
-    warped, hots = ahead([0], own_halo)
+    warped, hots = ahead([0], own_halo, [hot_of(0)] if keep else [], turned=keep)
     middle = list(range(1, views - late))
     sent, middle_halo = halo_of(middle[::-1], warped)
-    last_sent, last_halo = halo_of(groups[-1], (sent,))
+    raw = {k: [hot_of(k, (sent,))] if keep else [] for k in middle}
+    last_sent, last_halo = halo_of(groups[-1], (sent, *sum(raw.values(), [])))
     for k in middle:
         at = len(middle) - k
         after = (last_sent,) if k == 1 else warped[-1:]
-        more, more_hots = ahead([k], middle_halo[at : at + 1], after, keep and k == 1)
+        more, more_hots = ahead([k], middle_halo[at : at + 1], raw[k], after)
         warped, hots = warped + more, hots + more_hots
+    if keep:
+        hots += [hot_of(k, (last_sent,)) for k in groups[-1]]
     first = max(views // 4, 1)
-    last = views - first
+    near = list(range(1, first + 1))
+    main = [0] + list(range(first + 1, views))
+    last = len(main)
     work = [
         pltpu.VMEM((2, rows, z.tall, planes * width), BF),
         pltpu.VMEM((2, z.padded, lanes, width), F32),
@@ -457,12 +481,13 @@
         ]
 
     own, rim, mean = call(
-        functools.partial(turn_kernel, z, unroll, keep, share, views, late, last),
+        functools.partial(turn_kernel, z, unroll, keep, share, views, late, tuple(main)),
         results_of(last) + [warp],
-        *packets[first + 1 :], packets[first], last_halo, cotangent, *warped, *hots[first:],
+        *[packets[k] for k in main[1:]], packets[0], last_halo, cotangent, *warped,
+        *([hots[k] for k in main] if keep else []),
         scratch=[
             pltpu.VMEM((late,) + warp.shape, F32),
-            pltpu.VMEM((late if keep else 1,) + hot.shape, BF),
+            pltpu.VMEM((1,) + hot.shape, BF),
             twice, *tables[1:], *work,
         ],
         flops=flops * (last + late),
@@ -471,14 +496,15 @@
     own_rest, rim_rest = call(
         functools.partial(rest_kernel, z, unroll, keep, share, views, first),
         results_of(first),
-        *packets[:first], cotangent, mean, *warped[:first], *hots[:first],
+        *[packets[k] for k in near], cotangent, mean, *[warped[k] for k in near],
+        *([hots[k] for k in near] if keep else []),
         scratch=([] if keep else [pltpu.VMEM((1,) + hot.shape, BF)]) + [twice, *work],
         flops=flops * first,
         after=(rim,),
     )
     part = width // depths
-    pieces = []
-    for own, rim, after in ((own, rim, (own_rest,)), (own_rest, rim_rest, ())):
+    pieces = {}
+    for ids, own, rim, after in ((main, own, rim, (own_rest,)), (near, own_rest, rim_rest, ())):
         count = own.shape[0]
         rim = to_peer(rim, "row", 1)
         halves = call(
@@ -493,17 +519,18 @@
             [jax.ShapeDtypeStruct((rows, lanes, part), F32)] * count,
             *halves,
         )
-        pieces = list(sums) + pieces
+        pieces.update(zip(ids, sums))
     back = [pieces[0]] + [to_origin(pieces[k], "view", k) for k in range(1, views)]
+    edge = first + 1
     far = call(
-        functools.partial(stack_kernel, last),
-        jax.ShapeDtypeStruct((last, rows, lanes, part), F32),
-        *back[:first - 1 : -1],
+        functools.partial(stack_kernel, views - edge),
+        jax.ShapeDtypeStruct((views - edge, rows, lanes, part), F32),
+        *back[:first:-1],
     )
     return call(
         functools.partial(place_kernel, views, share),
         jax.ShapeDtypeStruct((1, channels, rows, part), F32),
-        far, *back[:first],
+        far, *back[:edge],
     )
 
 

time: 33.1 us -> 32.8 us (level)
  waiting for transfers between devices: 11.6 us -> 10.5 us
  Pallas kernels: 8.26 us -> 9.04 us
    ppermute x10, waiting for transfers between devices: 8.12 us -> 6.94 us  [to_peer(): return lax.ppermute(block, axis, pairs_of(lax.axis_size(axis), k))]
    pallas_call x16 -> x20, Pallas kernels: 8.26 us -> 9.04 us  [call(): pl.pallas_call(run, out_shape=out_shape, in_specs=[pl.BlockSpec(memory_sp...]
  transfers between devices with their start and end apart: 13 -> 13, of which waited for: 9 -> 9; matrix products, arithmetic and copies ran while one was open for 0% -> 0% of each run, Pallas kernels for 11% -> 14%
where the time goes in v5:
time: 32.8 us; the launch traced here: 32.7 us
  starting transfers between devices  13 us (40%)
  waiting for transfers between devices  10.5 us (32%)
  Pallas kernels  9.04 us (28%)
    pallas_call x20, Pallas kernels, call(): pl.pallas_call(run, out_shape=out_shape, in_specs=[pl.BlockSpec(memory_sp...  9.04 us
    ppermute x10, starting transfers between devices, to_peer(): return lax.ppermute(block, axis, pairs_of(lax.axis_size(axis), k))  8.5 us
    ppermute x10, waiting for transfers between devices, to_peer(): return lax.ppermute(block, axis, pairs_of(lax.axis_size(axis), k))  6.94 us
    ppermute x3, starting transfers between devices, to_origin(): lax.ppermute(block, axis, [(b, a) for a, b in pairs_of(lax.axis_size(axis...  4.51 us
    ppermute x3, waiting for transfers between devices, to_origin(): lax.ppermute(block, axis, [(b, a) for a, b in pairs_of(lax.axis_size(axis...  3.55 us
  transfers between devices with their start and end apart: 13, of which 9 were waited for; matrix products, arithmetic and copies ran while one was open for 0% of the time, Pallas kernels for 14%

profile of v5, /device:TPU:0, one launch (start us, length us, event | category | flops | bytes accessed | tf_op | source)
XLA Modules:
  0.0 32.7 jit_solution(14803274375228838460)
XLA Ops:
  0.0 1.0 %shard_map.55 = (f32[6,8,512]{2,1,0:T(8,128)S(1)}, f32[6,8,512]{2,1,0:T(8,128)S(1)}, f32[6,8,512]{2,1,0:T(8,128)S(1)}, f32[6,8,512]{2,1,0:T(8,128)S(1)}) custom-call(f32[1,32,2,512]{3,2,1,0:T(2,128)} %refs_0_.1, s32[1,4,2,512]{3,2,1,0:T(2,128)} %refs_1_.2, s32[1,4,2,512]{3,2,1,0:T(2,128)} %refs_2_.1, s32[2,1,4,2,512]{4,3,2,1,0:T(2,128)} %refs_3_.1), custom_call_target="tpu_custom_call" | custom-call | bytes 196608 | tf_op jit(solution)/shard_map/pallas_call | solution.py:47
  1.0 4.1 %collective-permute-start = (f32[6,8,512]{2,1,0:T(8,128)S(1)}, f32[6,8,512]{2,1,0:T(8,128)S(1)}, u32[]{:S(2)}, u32[]{:S(2)}) collective-permute-start(f32[6,8,512]{2,1,0:T(8,128)S(1)} %get-tuple-element.23), channel_id=1, source_target_pairs={{0,8},{4,12},{8,0},{12,4},{1,9},{5,13},{9,1},{13,5},{2,10},{6,14},... | collective-permute-start | bytes 294920 | tf_op jit(solution)/shard_map/ppermute | solution.py:29
  5.1 1.6 %collective-permute-start.2 = (f32[6,8,512]{2,1,0:T(8,128)S(1)}, f32[6,8,512]{2,1,0:T(8,128)S(1)}, u32[]{:S(2)}, u32[]{:S(2)}) collective-permute-start(f32[6,8,512]{2,1,0:T(8,128)S(1)} %get-tuple-element.26), channel_id=1, source_target_pairs={{0,4},{4,0},{8,12},{12,8},{1,5},{5,1},{9,13},{13,9},{2,6},{6,2},{1... | collective-permute-start | bytes 294920 | tf_op jit(solution)/shard_map/ppermute | solution.py:29
  6.7 0.5 %shard_map.57.refs_2_ = bf16[2,256,2048]{2,1,0:T(8,128)(2,1)S(1)} custom-call(f32[6,8,512]{2,1,0:T(8,128)S(1)} %get-tuple-element.25.refs_0_.refs_2_), custom_call_target="tpu_custom_call" | custom-call | flops 83886080 | bytes 98304 | tf_op jit(solution)/shard_map/pallas_call | solution.py:47
  7.2 0.7 %collective-permute-done.3.refs_1_ = f32[1,2,8,512]{3,2,1,0:T(8,128)S(1)} collective-permute-done((f32[1,2,8,512]{3,2,1,0:T(8,128)S(1)}, f32[1,2,8,512]{3,2,1,0:T(8,128)S(1)}, u32[]{:S(2)}, u32[]{:S(2)}) %collective-permute-start.3) | collective-permute-done | bytes 32800 | tf_op jit(solution)/shard_map/ppermute | solution.py:29
  7.9 0.8 %shard_map.58 = (f32[4,2,8,512]{3,2,1,0:T(8,128)S(1)}, bf16[2,2048,256]{2,1,0:T(8,128)(2,1)S(1)}) custom-call(f32[6,8,512]{2,1,0:T(8,128)S(1)} %get-tuple-element.25.refs_0_.refs_2_, f32[1,2,8,512]{3,2,1,0:T(8,128)S(1)} %collective-permute-done.3.refs_1_, bf16[2,256,2048]{2,1,0:T(8,128)(2,1)S(1)} %shard_map.57.refs_2_), custom_call_target="tpu_custom_call" | custom-call | flops 335544320 | bytes 4325376 | tf_op jit(solution)/shard_map/pallas_call | solution.py:47
  8.7 1.3 %collective-permute-done.refs_0_ = f32[6,8,512]{2,1,0:T(8,128)S(1)} collective-permute-done((f32[6,8,512]{2,1,0:T(8,128)S(1)}, f32[6,8,512]{2,1,0:T(8,128)S(1)}, u32[]{:S(2)}, u32[]{:S(2)}) %collective-permute-start) | collective-permute-done | bytes 98336 | tf_op jit(solution)/shard_map/ppermute | solution.py:29
  10.4 0.5 %shard_map.61.refs_3_.refs_2_.refs_9_ = bf16[2,256,2048]{2,1,0:T(8,128)(2,1)S(1)} custom-call(f32[6,8,512]{2,1,0:T(8,128)S(1)} %collective-permute-done.refs_0_, f32[2,2,8,512]{3,2,1,0:T(8,128)S(1)} %shard_map.59.refs_1_), custom_call_target="tpu_custom_call" | custom-call | flops 83886080 | bytes 98304 | tf_op jit(solution)/shard_map/pallas_call | solution.py:47
  10.9 0.5 %shard_map.60.refs_2_.refs_4_ = bf16[2,256,2048]{2,1,0:T(8,128)(2,1)S(1)} custom-call(f32[6,8,512]{2,1,0:T(8,128)S(1)} %collective-permute-done.2.refs_1_.refs_0_, f32[2,2,8,512]{3,2,1,0:T(8,128)S(1)} %shard_map.59.refs_1_), custom_call_target="tpu_custom_call" | custom-call | flops 83886080 | bytes 98304 | tf_op jit(solution)/shard_map/pallas_call | solution.py:47
  11.3 2.5 %collective-permute-done.1.refs_0_.refs_1_ = f32[6,8,512]{2,1,0:T(8,128)S(1)} collective-permute-done((f32[6,8,512]{2,1,0:T(8,128)S(1)}, f32[6,8,512]{2,1,0:T(8,128)S(1)}, u32[]{:S(2)}, u32[]{:S(2)}) %collective-permute-start.1) | collective-permute-done | bytes 98336 | tf_op jit(solution)/shard_map/ppermute | solution.py:29
  14.3 0.5 %shard_map.63.refs_3_.refs_6_ = f32[4,2,8,512]{3,2,1,0:T(8,128)S(1)} custom-call(f32[6,8,512]{2,1,0:T(8,128)S(1)} %collective-permute-done.2.refs_1_.refs_0_, f32[1,2,8,512]{3,2,1,0:T(8,128)S(1)} %get-tuple-element.42.refs_1_, bf16[2,256,2048]{2,1,0:T(8,128)(2,1)S(1)} %shard_map.60.refs_2_.refs_4_, f32[1,2,8,512]{3,2,1,0:T(8,128)S(1)} %shard_map.62.refs_3_.refs_1_), custom_call_target="tpu_custom_call" | custom-call | flops 335544320 | bytes 4325376 | tf_op jit(solution)/shard_map/pallas_call | solution.py:47
  14.9 0.5 %shard_map.64.refs_7_ = f32[4,2,8,512]{3,2,1,0:T(8,128)S(1)} custom-call(f32[6,8,512]{2,1,0:T(8,128)S(1)} %collective-permute-done.refs_0_, f32[1,2,8,512]{3,2,1,0:T(8,128)S(1)} %get-tuple-element.41.refs_1_, bf16[2,256,2048]{2,1,0:T(8,128)(2,1)S(1)} %shard_map.61.refs_3_.refs_2_.refs_9_, f32[4,2,8,512]{3,2,1,0:T(8,128)S(1)} %shard_map.63.refs_3_.refs_6_), custom_call_target="tpu_custom_call" | custom-call | flops 335544320 | bytes 4325376 | tf_op jit(solution)/shard_map/pallas_call | solution.py:47
  15.5 2.7 %shard_map.66 = (f32[3,2,8,512]{3,2,1,0:T(8,128)S(1)}, f32[3,2,8,512]{3,2,1,0:T(8,128)S(1)}, f32[4,2,8,512]{3,2,1,0:T(8,128)S(1)}) custom-call(f32[6,8,512]{2,1,0:T(8,128)S(1)} %collective-permute-done.refs_0_, f32[6,8,512]{2,1,0:T(8,128)S(1)} %collective-permute-done.1.refs_0_.refs_1_, f32[6,8,512]{2,1,0:T(8,128)S(1)} %get-tuple-element.25.refs_0_.refs_2_, ...), custom_call_target="tpu_custom_call" | custom-call | flops 1342177280 | bytes 13434880 | tf_op jit(solution)/shard_map/pallas_call | solution.py:47
  18.2 0.6 %collective-permute-start.6 = (f32[3,2,8,512]{3,2,1,0:T(8,128)S(1)}, f32[3,2,8,512]{3,2,1,0:T(8,128)S(1)}, u32[]{:S(2)}, u32[]{:S(2)}) collective-permute-start(f32[3,2,8,512]{3,2,1,0:T(8,128)S(1)} %shard_map.67.refs_5_), channel_id=1, source_target_pairs={{0,1},{1,0},{2,3},{3,2},{4,5},{5,4},{6,7},{7,6},{8,9},{9,8},{10,11... | collective-permute-start | bytes 294920 | tf_op jit(solution)/shard_map/ppermute | solution.py:29
  18.8 0.9 %shard_map.68 = (f32[1,2,8,512]{3,2,1,0:T(8,128)S(1)}, f32[1,2,8,512]{3,2,1,0:T(8,128)S(1)}) custom-call(f32[6,8,512]{2,1,0:T(8,128)S(1)} %collective-permute-done.2.refs_1_.refs_0_, f32[4,8,2,512]{3,2,1,0:T(2,128)S(1)} %copy-done, f32[4,2,8,512]{3,2,1,0:T(8,128)S(1)} %get-tuple-element.31.refs_2_, f32[4,2,8,512]{3,2,1,0:T(8,128)S(1)} %shard_map.63.refs_3_.refs_6_, ...), custom_call_target="tpu_custom_call" | custom-call | flops 335544320 | bytes 4685824 | tf_op jit(solution)/shard_map/pallas_call | solution.py:47
  19.8 1.6 %collective-permute-start.7 = (f32[3,2,8,256]{3,2,1,0:T(8,128)S(1)}, f32[3,2,8,256]{3,2,1,0:T(8,128)S(1)}, u32[]{:S(2)}, u32[]{:S(2)}) collective-permute-start(f32[3,2,8,256]{3,2,1,0:T(8,128)S(1)} %get-tuple-element.34), channel_id=1, source_target_pairs={{0,2},{2,0},{1,3},{3,1},{4,6},{6,4},{5,7},{7,5},{8,10},{10,8},{9,1... | collective-permute-start | bytes 147464 | tf_op jit(solution)/shard_map/ppermute | solution.py:29
  21.4 1.1 %collective-permute-done.10.refs_1_ = f32[1,2,8,512]{3,2,1,0:T(8,128)S(1)} collective-permute-done((f32[1,2,8,512]{3,2,1,0:T(8,128)S(1)}, f32[1,2,8,512]{3,2,1,0:T(8,128)S(1)}, u32[]{:S(2)}, u32[]{:S(2)}) %collective-permute-start.10) | collective-permute-done | bytes 32800 | tf_op jit(solution)/shard_map/ppermute | solution.py:29
  22.6 0.6 %collective-permute-start.11 = (f32[1,2,8,256]{3,2,1,0:T(8,128)S(1)}, f32[1,2,8,256]{3,2,1,0:T(8,128)S(1)}, u32[]{:S(2)}, u32[]{:S(2)}) collective-permute-start(f32[1,2,8,256]{3,2,1,0:T(8,128)S(1)} %get-tuple-element.40), channel_id=1, source_target_pairs={{0,2},{2,0},{1,3},{3,1},{4,6},{6,4},{5,7},{7,5},{8,10},{10,8},{9,1... | collective-permute-start | bytes 49160 | tf_op jit(solution)/shard_map/ppermute | solution.py:29
  23.2 0.8 %collective-permute-done.7.refs_1_ = f32[3,2,8,256]{3,2,1,0:T(8,128)S(1)} collective-permute-done((f32[3,2,8,256]{3,2,1,0:T(8,128)S(1)}, f32[3,2,8,256]{3,2,1,0:T(8,128)S(1)}, u32[]{:S(2)}, u32[]{:S(2)}) %collective-permute-start.7) | collective-permute-done | bytes 49184 | tf_op jit(solution)/shard_map/ppermute | solution.py:29
  24.0 3.4 %collective-permute-start.8 = (f32[2,8,256]{2,1,0:T(8,128)S(1)}, f32[2,8,256]{2,1,0:T(8,128)S(1)}, u32[]{:S(2)}, u32[]{:S(2)}) collective-permute-start(f32[2,8,256]{2,1,0:T(8,128)S(1)} %get-tuple-element.35), channel_id=1, source_target_pairs={{12,0},{8,4},{4,8},{0,12},{13,1},{9,5},{5,9},{1,13},{14,2},{10,6},... | collective-permute-start | bytes 49160 | tf_op jit(solution)/shard_map/ppermute | solution.py:33
  27.4 1.1 %collective-permute-start.12 = (f32[2,8,256]{2,1,0:T(8,128)S(1)}, f32[2,8,256]{2,1,0:T(8,128)S(1)}, u32[]{:S(2)}, u32[]{:S(2)}) collective-permute-start(f32[2,8,256]{2,1,0:T(8,128)S(1)} %shard_map.73), channel_id=1, source_target_pairs={{4,0},{0,4},{12,8},{8,12},{5,1},{1,5},{13,9},{9,13},{6,2},{2,6},{1... | collective-permute-start | bytes 49160 | tf_op jit(solution)/shard_map/ppermute | solution.py:33
  28.5 1.1 %collective-permute-done.8.refs_0_ = f32[2,8,256]{2,1,0:T(8,128)S(1)} collective-permute-done((f32[2,8,256]{2,1,0:T(8,128)S(1)}, f32[2,8,256]{2,1,0:T(8,128)S(1)}, u32[]{:S(2)}, u32[]{:S(2)}) %collective-permute-start.8) | collective-permute-done | bytes 16416 | tf_op jit(solution)/shard_map/ppermute | solution.py:33
  29.6 2.4 %collective-permute-done.9.refs_1_ = f32[2,8,256]{2,1,0:T(8,128)S(1)} collective-permute-done((f32[2,8,256]{2,1,0:T(8,128)S(1)}, f32[2,8,256]{2,1,0:T(8,128)S(1)}, u32[]{:S(2)}, u32[]{:S(2)}) %collective-permute-start.9) | collective-permute-done | bytes 16416 | tf_op jit(solution)/shard_map/ppermute | solution.py:33
  32.0 0.7 %shard_map.74 = f32[1,32,2,256]{3,2,1,0:T(2,128)} custom-call(f32[2,2,8,256]{3,2,1,0:T(8,128)S(1)} %shard_map.71.refs_0_, f32[2,8,256]{2,1,0:T(8,128)S(1)} %get-tuple-element.37.refs_1_, f32[2,8,256]{2,1,0:T(8,128)S(1)} %collective-permute-done.12.refs_2_), custom_call_target="tpu_custom_call" | custom-call | bytes 65536 | tf_op jit(solution)/shard_map/pallas_call | solution.py:47
  (25 shorter events, 1.0 us)
Async XLA Ops:
  1.0 9.0 %collective-permute-start = (f32[6,8,512]{2,1,0:T(8,128)S(1)}, f32[6,8,512]{2,1,0:T(8,128)S(1)}, u32[]{:S(2)}, u32[]{:S(2)}) collective-permute-start(f32[6,8,512]{2,1,0:T(8,128)S(1)} %get-tuple-element.23), channel_id=1, source_target_pairs={{0,8},{4,12},{8,0},{12,4},{1,9},{5,13},{9,1},{13,5},{2,10},{6,14},... | collective-permute-start | bytes 294920 | tf_op jit(solution)/shard_map/ppermute | solution.py:29
  5.1 5.2 %collective-permute-start.2 = (f32[6,8,512]{2,1,0:T(8,128)S(1)}, f32[6,8,512]{2,1,0:T(8,128)S(1)}, u32[]{:S(2)}, u32[]{:S(2)}) collective-permute-start(f32[6,8,512]{2,1,0:T(8,128)S(1)} %get-tuple-element.26), channel_id=1, source_target_pairs={{0,4},{4,0},{8,12},{12,8},{1,5},{5,1},{9,13},{13,9},{2,6},{6,2},{1... | collective-permute-start | bytes 294920 | tf_op jit(solution)/shard_map/ppermute | solution.py:29
  6.7 1.2 %collective-permute-start.3 = (f32[1,2,8,512]{3,2,1,0:T(8,128)S(1)}, f32[1,2,8,512]{3,2,1,0:T(8,128)S(1)}, u32[]{:S(2)}, u32[]{:S(2)}) collective-permute-start(f32[1,2,8,512]{3,2,1,0:T(8,128)S(1)} %shard_map.56), channel_id=1, source_target_pairs={{0,1},{1,0},{2,3},{3,2},{4,5},{5,4},{6,7},{7,6},{8,9},{9,8},{10,11... | collective-permute-start | bytes 98312 | tf_op jit(solution)/shard_map/ppermute | solution.py:29
  6.7 7.1 %collective-permute-start.1 = (f32[6,8,512]{2,1,0:T(8,128)S(1)}, f32[6,8,512]{2,1,0:T(8,128)S(1)}, u32[]{:S(2)}, u32[]{:S(2)}) collective-permute-start(f32[6,8,512]{2,1,0:T(8,128)S(1)} %get-tuple-element.24), channel_id=1, source_target_pairs={{0,12},{4,8},{8,4},{12,0},{1,13},{5,9},{9,5},{13,1},{2,14},{6,10},... | collective-permute-start | bytes 294920 | tf_op jit(solution)/shard_map/ppermute | solution.py:29
  10.4 3.9 %collective-permute-start.5 = (f32[2,2,8,512]{3,2,1,0:T(8,128)S(1)}, f32[2,2,8,512]{3,2,1,0:T(8,128)S(1)}, u32[]{:S(2)}, u32[]{:S(2)}) collective-permute-start(f32[2,2,8,512]{3,2,1,0:T(8,128)S(1)} %shard_map.59.refs_1_), channel_id=1, source_target_pairs={{0,1},{1,0},{2,3},{3,2},{4,5},{5,4},{6,7},{7,6},{8,9},{9,8},{10,11... | collective-permute-start | bytes 196616 | tf_op jit(solution)/shard_map/ppermute | solution.py:29
  13.8 1.6 %collective-permute-start.4 = (f32[1,2,8,512]{3,2,1,0:T(8,128)S(1)}, f32[1,2,8,512]{3,2,1,0:T(8,128)S(1)}, u32[]{:S(2)}, u32[]{:S(2)}) collective-permute-start(f32[1,2,8,512]{3,2,1,0:T(8,128)S(1)} %shard_map.62.refs_3_.refs_1_), channel_id=1, source_target_pairs={{0,1},{1,0},{2,3},{3,2},{4,5},{5,4},{6,7},{7,6},{8,9},{9,8},{10,11... | collective-permute-start | bytes 98312 | tf_op jit(solution)/shard_map/ppermute | solution.py:29
  14.3 1.1 %copy-start = (f32[4,8,2,512]{3,2,1,0:T(2,128)S(1)}, f32[4,8,2,512]{3,2,1,0:T(2,128)}, u32[]{:S(2)}) copy-start(f32[4,8,2,512]{3,2,1,0:T(2,128)} %refs_1_.3) | copy-start | bytes 393220
  18.2 1.5 %collective-permute-start.6 = (f32[3,2,8,512]{3,2,1,0:T(8,128)S(1)}, f32[3,2,8,512]{3,2,1,0:T(8,128)S(1)}, u32[]{:S(2)}, u32[]{:S(2)}) collective-permute-start(f32[3,2,8,512]{3,2,1,0:T(8,128)S(1)} %shard_map.67.refs_5_), channel_id=1, source_target_pairs={{0,1},{1,0},{2,3},{3,2},{4,5},{5,4},{6,7},{7,6},{8,9},{9,8},{10,11... | collective-permute-start | bytes 294920 | tf_op jit(solution)/shard_map/ppermute | solution.py:29
  19.8 4.2 %collective-permute-start.7 = (f32[3,2,8,256]{3,2,1,0:T(8,128)S(1)}, f32[3,2,8,256]{3,2,1,0:T(8,128)S(1)}, u32[]{:S(2)}, u32[]{:S(2)}) collective-permute-start(f32[3,2,8,256]{3,2,1,0:T(8,128)S(1)} %get-tuple-element.34), channel_id=1, source_target_pairs={{0,2},{2,0},{1,3},{3,1},{4,6},{6,4},{5,7},{7,5},{8,10},{10,8},{9,1... | collective-permute-start | bytes 147464 | tf_op jit(solution)/shard_map/ppermute | solution.py:29
  21.3 1.2 %collective-permute-start.10 = (f32[1,2,8,512]{3,2,1,0:T(8,128)S(1)}, f32[1,2,8,512]{3,2,1,0:T(8,128)S(1)}, u32[]{:S(2)}, u32[]{:S(2)}) collective-permute-start(f32[1,2,8,512]{3,2,1,0:T(8,128)S(1)} %get-tuple-element.38), channel_id=1, source_target_pairs={{0,1},{1,0},{2,3},{3,2},{4,5},{5,4},{6,7},{7,6},{8,9},{9,8},{10,11... | collective-permute-start | bytes 98312 | tf_op jit(solution)/shard_map/ppermute | solution.py:29
  22.6 4.8 %collective-permute-start.11 = (f32[1,2,8,256]{3,2,1,0:T(8,128)S(1)}, f32[1,2,8,256]{3,2,1,0:T(8,128)S(1)}, u32[]{:S(2)}, u32[]{:S(2)}) collective-permute-start(f32[1,2,8,256]{3,2,1,0:T(8,128)S(1)} %get-tuple-element.40), channel_id=1, source_target_pairs={{0,2},{2,0},{1,3},{3,1},{4,6},{6,4},{5,7},{7,5},{8,10},{10,8},{9,1... | collective-permute-start | bytes 49160 | tf_op jit(solution)/shard_map/ppermute | solution.py:29
  24.0 5.7 %collective-permute-start.8 = (f32[2,8,256]{2,1,0:T(8,128)S(1)}, f32[2,8,256]{2,1,0:T(8,128)S(1)}, u32[]{:S(2)}, u32[]{:S(2)}) collective-permute-start(f32[2,8,256]{2,1,0:T(8,128)S(1)} %get-tuple-element.35), channel_id=1, source_target_pairs={{12,0},{8,4},{4,8},{0,12},{13,1},{9,5},{5,9},{1,13},{14,2},{10,6},... | collective-permute-start | bytes 49160 | tf_op jit(solution)/shard_map/ppermute | solution.py:33
  27.4 4.6 %collective-permute-start.9 = (f32[2,8,256]{2,1,0:T(8,128)S(1)}, f32[2,8,256]{2,1,0:T(8,128)S(1)}, u32[]{:S(2)}, u32[]{:S(2)}) collective-permute-start(f32[2,8,256]{2,1,0:T(8,128)S(1)} %get-tuple-element.36), channel_id=1, source_target_pairs={{8,0},{12,4},{0,8},{4,12},{9,1},{13,5},{1,9},{5,13},{10,2},{14,6},... | collective-permute-start | bytes 49160 | tf_op jit(solution)/shard_map/ppermute | solution.py:33
  27.4 4.6 %collective-permute-start.12 = (f32[2,8,256]{2,1,0:T(8,128)S(1)}, f32[2,8,256]{2,1,0:T(8,128)S(1)}, u32[]{:S(2)}, u32[]{:S(2)}) collective-permute-start(f32[2,8,256]{2,1,0:T(8,128)S(1)} %shard_map.73), channel_id=1, source_target_pairs={{4,0},{0,4},{12,8},{8,12},{5,1},{1,5},{13,9},{9,13},{6,2},{2,6},{1... | collective-permute-start | bytes 49160 | tf_op jit(solution)/shard_map/ppermute | solution.py:33

commit v6 on v5

--- a/solution.py
+++ b/solution.py
@@ -288,7 +288,7 @@
 def turn_kernel(z, unroll, keep, share, views, late, ids, *refs):
     count = len(ids)
     early, hots_in = views - late, (count if keep else 0)
-    packets, refs = (refs[count - 1],) + refs[: count - 1], refs[count:]
+    packets, refs = refs[:count], refs[count:]
     halo, cot_ref, refs = refs[0], refs[1], refs[2:]
     ahead, refs = refs[:early], refs[early:]
     hots, refs = refs[:hots_in], refs[hots_in:]
@@ -324,9 +324,10 @@
     t_ref, l_ref, grad_ref, e_ref = refs[-4:]
     for v in reversed(range(count)):
         work = t_ref.at[v % 2], l_ref.at[v % 2], grad_ref.at[v % 2], e_ref.at[v % 2]
+        hot = hots[v] if keep else refs[2].at[0]
         backward(
-            z, unroll, share, views, packets[v], warped[v], mean_ref, cot_ref,
-            hots[v] if keep else refs[2].at[0], not keep, False, work, own_ref.at[v], rim_ref.at[v],
+            z, unroll, share, views, packets[v], warped[v], mean_ref, cot_ref, hot, not keep,
+            hot.shape != z.one_hot(), work, own_ref.at[v], rim_ref.at[v],
         )
 
 
@@ -464,8 +465,8 @@
     if keep:
         hots += [hot_of(k, (last_sent,)) for k in groups[-1]]
     first = max(views // 4, 1)
-    near = list(range(1, first + 1))
-    main = [0] + list(range(first + 1, views))
+    near = list(range(first + 1))
+    main = list(range(first + 1, views))
     last = len(main)
     work = [
         pltpu.VMEM((2, rows, z.tall, planes * width), BF),
@@ -483,7 +484,7 @@
     own, rim, mean = call(
         functools.partial(turn_kernel, z, unroll, keep, share, views, late, tuple(main)),
         results_of(last) + [warp],
-        *[packets[k] for k in main[1:]], packets[0], last_halo, cotangent, *warped,
+        *[packets[k] for k in main], last_halo, cotangent, *warped,
         *([hots[k] for k in main] if keep else []),
         scratch=[
             pltpu.VMEM((late,) + warp.shape, F32),
@@ -494,18 +495,20 @@
     )
     rim = call(copy_kernel, jax.ShapeDtypeStruct(rim.shape, F32), rim)
     own_rest, rim_rest = call(
-        functools.partial(rest_kernel, z, unroll, keep, share, views, first),
-        results_of(first),
+        functools.partial(rest_kernel, z, unroll, keep, share, views, len(near)),
+        results_of(len(near)),
         *[packets[k] for k in near], cotangent, mean, *[warped[k] for k in near],
         *([hots[k] for k in near] if keep else []),
         scratch=([] if keep else [pltpu.VMEM((1,) + hot.shape, BF)]) + [twice, *work],
-        flops=flops * first,
+        flops=flops * len(near),
         after=(rim,),
     )
     part = width // depths
-    pieces = {}
+    pieces, folded = {}, ()
     for ids, own, rim, after in ((main, own, rim, (own_rest,)), (near, own_rest, rim_rest, ())):
         count = own.shape[0]
+        if folded:
+            rim = call(copy_kernel, jax.ShapeDtypeStruct(rim.shape, F32), rim, after=folded)
         rim = to_peer(rim, "row", 1)
         halves = call(
             functools.partial(fold_kernel, depths),
@@ -513,6 +516,7 @@
             own, rim,
             after=after,
         )
+        folded = (halves[0],)
         halves = [halves[0]] + [to_peer(halves[k], "depth", k) for k in range(1, depths)]
         sums = call(
             functools.partial(sum_kernel, depths, count),

time: 32.8 us -> 32.6 us (level)
  waiting for transfers between devices: 10.5 us -> 9.75 us
  starting transfers between devices: 13 us -> 13.6 us
    ppermute x10, waiting for transfers between devices: 6.94 us -> 6.11 us  [to_peer(): return lax.ppermute(block, axis, pairs_of(lax.axis_size(axis), k))]
    ppermute x10, starting transfers between devices: 8.5 us -> 9.14 us  [to_peer(): return lax.ppermute(block, axis, pairs_of(lax.axis_size(axis), k))]
    pallas_call x20 -> x21, Pallas kernels: 9.04 us -> 8.96 us  [call(): pl.pallas_call(run, out_shape=out_shape, in_specs=[pl.BlockSpec(memory_sp...]
  transfers between devices with their start and end apart: 13 -> 13, of which waited for: 9 -> 7; matrix products, arithmetic and copies ran while one was open for 0% -> 0% of each run, Pallas kernels for 14% -> 15%
where the time goes in v6:
time: 32.6 us; the launch traced here: 32.5 us
  starting transfers between devices  13.6 us (42%)
  waiting for transfers between devices  9.75 us (30%)
  Pallas kernels  8.96 us (27%)
    ppermute x10, starting transfers between devices, to_peer(): return lax.ppermute(block, axis, pairs_of(lax.axis_size(axis), k))  9.14 us
    pallas_call x21, Pallas kernels, call(): pl.pallas_call(run, out_shape=out_shape, in_specs=[pl.BlockSpec(memory_sp...  8.96 us
    ppermute x10, waiting for transfers between devices, to_peer(): return lax.ppermute(block, axis, pairs_of(lax.axis_size(axis), k))  6.11 us
    ppermute x3, starting transfers between devices, to_origin(): lax.ppermute(block, axis, [(b, a) for a, b in pairs_of(lax.axis_size(axis...  4.45 us
    ppermute x3, waiting for transfers between devices, to_origin(): lax.ppermute(block, axis, [(b, a) for a, b in pairs_of(lax.axis_size(axis...  3.64 us
  transfers between devices with their start and end apart: 13, of which 7 were waited for; matrix products, arithmetic and copies ran while one was open for 0% of the time, Pallas kernels for 15%

profile of v6, /device:TPU:0, one launch (start us, length us, event | category | flops | bytes accessed | tf_op | source)
XLA Modules:
  0.0 32.5 jit_solution(8427036340096751033)
XLA Ops:
  0.0 1.0 %shard_map.55 = (f32[6,8,512]{2,1,0:T(8,128)S(1)}, f32[6,8,512]{2,1,0:T(8,128)S(1)}, f32[6,8,512]{2,1,0:T(8,128)S(1)}, f32[6,8,512]{2,1,0:T(8,128)S(1)}) custom-call(f32[1,32,2,512]{3,2,1,0:T(2,128)} %refs_0_.1, s32[1,4,2,512]{3,2,1,0:T(2,128)} %refs_1_.1, s32[1,4,2,512]{3,2,1,0:T(2,128)} %refs_2_.2, s32[2,1,4,2,512]{4,3,2,1,0:T(2,128)} %refs_3_.2), custom_call_target="tpu_custom_call" | custom-call | bytes 196608 | tf_op jit(solution)/shard_map/pallas_call | solution.py:47
  1.0 4.1 %collective-permute-start = (f32[6,8,512]{2,1,0:T(8,128)S(1)}, f32[6,8,512]{2,1,0:T(8,128)S(1)}, u32[]{:S(2)}, u32[]{:S(2)}) collective-permute-start(f32[6,8,512]{2,1,0:T(8,128)S(1)} %get-tuple-element.24), channel_id=1, source_target_pairs={{0,8},{4,12},{8,0},{12,4},{1,9},{5,13},{9,1},{13,5},{2,10},{6,14},... | collective-permute-start | bytes 294920 | tf_op jit(solution)/shard_map/ppermute | solution.py:29
  5.1 1.6 %collective-permute-start.2 = (f32[6,8,512]{2,1,0:T(8,128)S(1)}, f32[6,8,512]{2,1,0:T(8,128)S(1)}, u32[]{:S(2)}, u32[]{:S(2)}) collective-permute-start(f32[6,8,512]{2,1,0:T(8,128)S(1)} %get-tuple-element.26), channel_id=1, source_target_pairs={{0,4},{4,0},{8,12},{12,8},{1,5},{5,1},{9,13},{13,9},{2,6},{6,2},{1... | collective-permute-start | bytes 294920 | tf_op jit(solution)/shard_map/ppermute | solution.py:29
  6.7 0.5 %shard_map.57.refs_2_ = bf16[2,256,2048]{2,1,0:T(8,128)(2,1)S(1)} custom-call(f32[6,8,512]{2,1,0:T(8,128)S(1)} %get-tuple-element.27.refs_0_), custom_call_target="tpu_custom_call" | custom-call | flops 83886080 | bytes 98304 | tf_op jit(solution)/shard_map/pallas_call | solution.py:47
  7.2 0.7 %collective-permute-done.3.refs_1_ = f32[1,2,8,512]{3,2,1,0:T(8,128)S(1)} collective-permute-done((f32[1,2,8,512]{3,2,1,0:T(8,128)S(1)}, f32[1,2,8,512]{3,2,1,0:T(8,128)S(1)}, u32[]{:S(2)}, u32[]{:S(2)}) %collective-permute-start.3) | collective-permute-done | bytes 32800 | tf_op jit(solution)/shard_map/ppermute | solution.py:29
  7.9 0.8 %shard_map.58 = (f32[4,2,8,512]{3,2,1,0:T(8,128)S(1)}, bf16[2,2048,256]{2,1,0:T(8,128)(2,1)S(1)}) custom-call(f32[6,8,512]{2,1,0:T(8,128)S(1)} %get-tuple-element.27.refs_0_, f32[1,2,8,512]{3,2,1,0:T(8,128)S(1)} %collective-permute-done.3.refs_1_, bf16[2,256,2048]{2,1,0:T(8,128)(2,1)S(1)} %shard_map.57.refs_2_), custom_call_target="tpu_custom_call" | custom-call | flops 335544320 | bytes 4325376 | tf_op jit(solution)/shard_map/pallas_call | solution.py:47
  8.7 1.3 %collective-permute-done.refs_0_ = f32[6,8,512]{2,1,0:T(8,128)S(1)} collective-permute-done((f32[6,8,512]{2,1,0:T(8,128)S(1)}, f32[6,8,512]{2,1,0:T(8,128)S(1)}, u32[]{:S(2)}, u32[]{:S(2)}) %collective-permute-start) | collective-permute-done | bytes 98336 | tf_op jit(solution)/shard_map/ppermute | solution.py:29
  10.4 0.5 %shard_map.61.refs_3_.refs_2_.refs_7_ = bf16[2,256,2048]{2,1,0:T(8,128)(2,1)S(1)} custom-call(f32[6,8,512]{2,1,0:T(8,128)S(1)} %collective-permute-done.refs_0_, f32[2,2,8,512]{3,2,1,0:T(8,128)S(1)} %shard_map.59.refs_1_), custom_call_target="tpu_custom_call" | custom-call | flops 83886080 | bytes 98304 | tf_op jit(solution)/shard_map/pallas_call | solution.py:47
  10.9 0.5 %shard_map.60.refs_2_.refs_7_ = bf16[2,256,2048]{2,1,0:T(8,128)(2,1)S(1)} custom-call(f32[6,8,512]{2,1,0:T(8,128)S(1)} %collective-permute-done.2.refs_1_.refs_0_, f32[2,2,8,512]{3,2,1,0:T(8,128)S(1)} %shard_map.59.refs_1_), custom_call_target="tpu_custom_call" | custom-call | flops 83886080 | bytes 98304 | tf_op jit(solution)/shard_map/pallas_call | solution.py:47
  11.3 2.5 %collective-permute-done.1.refs_0_.refs_1_ = f32[6,8,512]{2,1,0:T(8,128)S(1)} collective-permute-done((f32[6,8,512]{2,1,0:T(8,128)S(1)}, f32[6,8,512]{2,1,0:T(8,128)S(1)}, u32[]{:S(2)}, u32[]{:S(2)}) %collective-permute-start.1) | collective-permute-done | bytes 98336 | tf_op jit(solution)/shard_map/ppermute | solution.py:29
  13.8 0.5 %shard_map.65.refs_8_ = bf16[2,256,2048]{2,1,0:T(8,128)(2,1)S(1)} custom-call(f32[6,8,512]{2,1,0:T(8,128)S(1)} %collective-permute-done.1.refs_0_.refs_1_, f32[1,2,8,512]{3,2,1,0:T(8,128)S(1)} %shard_map.62.refs_3_.refs_1_), custom_call_target="tpu_custom_call" | custom-call | flops 83886080 | bytes 98304 | tf_op jit(solution)/shard_map/pallas_call | solution.py:47
  14.3 0.5 %shard_map.63.refs_3_.refs_5_ = f32[4,2,8,512]{3,2,1,0:T(8,128)S(1)} custom-call(f32[6,8,512]{2,1,0:T(8,128)S(1)} %collective-permute-done.2.refs_1_.refs_0_, f32[1,2,8,512]{3,2,1,0:T(8,128)S(1)} %get-tuple-element.44.refs_1_, bf16[2,256,2048]{2,1,0:T(8,128)(2,1)S(1)} %shard_map.60.refs_2_.refs_7_, f32[1,2,8,512]{3,2,1,0:T(8,128)S(1)} %shard_map.62.refs_3_.refs_1_), custom_call_target="tpu_custom_call" | custom-call | flops 335544320 | bytes 4325376 | tf_op jit(solution)/shard_map/pallas_call | solution.py:47
  14.9 0.5 %shard_map.64.refs_6_ = f32[4,2,8,512]{3,2,1,0:T(8,128)S(1)} custom-call(f32[6,8,512]{2,1,0:T(8,128)S(1)} %collective-permute-done.refs_0_, f32[1,2,8,512]{3,2,1,0:T(8,128)S(1)} %get-tuple-element.43.refs_1_, bf16[2,256,2048]{2,1,0:T(8,128)(2,1)S(1)} %shard_map.61.refs_3_.refs_2_.refs_7_, f32[4,2,8,512]{3,2,1,0:T(8,128)S(1)} %shard_map.63.refs_3_.refs_5_), custom_call_target="tpu_custom_call" | custom-call | flops 335544320 | bytes 4325376 | tf_op jit(solution)/shard_map/pallas_call | solution.py:47
  15.5 2.2 %shard_map.66 = (f32[2,2,8,512]{3,2,1,0:T(8,128)S(1)}, f32[2,2,8,512]{3,2,1,0:T(8,128)S(1)}, f32[4,2,8,512]{3,2,1,0:T(8,128)S(1)}) custom-call(f32[6,8,512]{2,1,0:T(8,128)S(1)} %collective-permute-done.refs_0_, f32[6,8,512]{2,1,0:T(8,128)S(1)} %collective-permute-done.1.refs_0_.refs_1_, f32[1,2,8,512]{3,2,1,0:T(8,128)S(1)} %collective-permute-done.4.refs_2_, ...), custom_call_target="tpu_custom_call" | custom-call | flops 1006632960 | bytes 9142272 | tf_op jit(solution)/shard_map/pallas_call | solution.py:47
  17.7 0.6 %collective-permute-start.6 = (f32[2,2,8,512]{3,2,1,0:T(8,128)S(1)}, f32[2,2,8,512]{3,2,1,0:T(8,128)S(1)}, u32[]{:S(2)}, u32[]{:S(2)}) collective-permute-start(f32[2,2,8,512]{3,2,1,0:T(8,128)S(1)} %shard_map.67.refs_8_), channel_id=1, source_target_pairs={{0,1},{1,0},{2,3},{3,2},{4,5},{5,4},{6,7},{7,6},{8,9},{9,8},{10,11... | collective-permute-start | bytes 196616 | tf_op jit(solution)/shard_map/ppermute | solution.py:29
  18.3 1.3 %shard_map.68 = (f32[2,2,8,512]{3,2,1,0:T(8,128)S(1)}, f32[2,2,8,512]{3,2,1,0:T(8,128)S(1)}) custom-call(f32[6,8,512]{2,1,0:T(8,128)S(1)} %get-tuple-element.27.refs_0_, f32[6,8,512]{2,1,0:T(8,128)S(1)} %collective-permute-done.2.refs_1_.refs_0_, f32[4,8,2,512]{3,2,1,0:T(2,128)S(1)} %copy-done, f32[4,2,8,512]{3,2,1,0:T(8,128)S(1)} %get-tuple-element.31.refs_3_, ...), custom_call_target="tpu_custom_call" | custom-call | flops 671088640 | bytes 9109504 | tf_op jit(solution)/shard_map/pallas_call | solution.py:47
  19.7 1.6 %collective-permute-start.7 = (f32[2,2,8,256]{3,2,1,0:T(8,128)S(1)}, f32[2,2,8,256]{3,2,1,0:T(8,128)S(1)}, u32[]{:S(2)}, u32[]{:S(2)}) collective-permute-start(f32[2,2,8,256]{3,2,1,0:T(8,128)S(1)} %get-tuple-element.35), channel_id=1, source_target_pairs={{0,2},{2,0},{1,3},{3,1},{4,6},{6,4},{5,7},{7,5},{8,10},{10,8},{9,1... | collective-permute-start | bytes 98312 | tf_op jit(solution)/shard_map/ppermute | solution.py:29
  21.3 1.2 %collective-permute-start.11 = (f32[2,2,8,256]{3,2,1,0:T(8,128)S(1)}, f32[2,2,8,256]{3,2,1,0:T(8,128)S(1)}, u32[]{:S(2)}, u32[]{:S(2)}) collective-permute-start(f32[2,2,8,256]{3,2,1,0:T(8,128)S(1)} %get-tuple-element.40), channel_id=1, source_target_pairs={{0,2},{2,0},{1,3},{3,1},{4,6},{6,4},{5,7},{7,5},{8,10},{10,8},{9,1... | collective-permute-start | bytes 98312 | tf_op jit(solution)/shard_map/ppermute | solution.py:29
  22.5 1.2 %collective-permute-done.7.refs_1_ = f32[2,2,8,256]{3,2,1,0:T(8,128)S(1)} collective-permute-done((f32[2,2,8,256]{3,2,1,0:T(8,128)S(1)}, f32[2,2,8,256]{3,2,1,0:T(8,128)S(1)}, u32[]{:S(2)}, u32[]{:S(2)}) %collective-permute-start.7) | collective-permute-done | bytes 32800 | tf_op jit(solution)/shard_map/ppermute | solution.py:29
  23.7 3.5 %collective-permute-start.8 = (f32[2,8,256]{2,1,0:T(8,128)S(1)}, f32[2,8,256]{2,1,0:T(8,128)S(1)}, u32[]{:S(2)}, u32[]{:S(2)}) collective-permute-start(f32[2,8,256]{2,1,0:T(8,128)S(1)} %get-tuple-element.36), channel_id=1, source_target_pairs={{12,0},{8,4},{4,8},{0,12},{13,1},{9,5},{5,9},{1,13},{14,2},{10,6},... | collective-permute-start | bytes 49160 | tf_op jit(solution)/shard_map/ppermute | solution.py:33
  27.2 1.0 %collective-permute-start.12 = (f32[2,8,256]{2,1,0:T(8,128)S(1)}, f32[2,8,256]{2,1,0:T(8,128)S(1)}, u32[]{:S(2)}, u32[]{:S(2)}) collective-permute-start(f32[2,8,256]{2,1,0:T(8,128)S(1)} %get-tuple-element.42), channel_id=1, source_target_pairs={{4,0},{0,4},{12,8},{8,12},{5,1},{1,5},{13,9},{9,13},{6,2},{2,6},{1... | collective-permute-start | bytes 49160 | tf_op jit(solution)/shard_map/ppermute | solution.py:33
  28.2 1.1 %collective-permute-done.8.refs_0_ = f32[2,8,256]{2,1,0:T(8,128)S(1)} collective-permute-done((f32[2,8,256]{2,1,0:T(8,128)S(1)}, f32[2,8,256]{2,1,0:T(8,128)S(1)}, u32[]{:S(2)}, u32[]{:S(2)}) %collective-permute-start.8) | collective-permute-done | bytes 16416 | tf_op jit(solution)/shard_map/ppermute | solution.py:33
  29.3 2.6 %collective-permute-done.9.refs_1_ = f32[2,8,256]{2,1,0:T(8,128)S(1)} collective-permute-done((f32[2,8,256]{2,1,0:T(8,128)S(1)}, f32[2,8,256]{2,1,0:T(8,128)S(1)}, u32[]{:S(2)}, u32[]{:S(2)}) %collective-permute-start.9) | collective-permute-done | bytes 16416 | tf_op jit(solution)/shard_map/ppermute | solution.py:33
  31.8 0.7 %shard_map.75 = f32[1,32,2,256]{3,2,1,0:T(2,128)} custom-call(f32[2,2,8,256]{3,2,1,0:T(8,128)S(1)} %shard_map.71.refs_0_, f32[2,8,256]{2,1,0:T(8,128)S(1)} %get-tuple-element.41.refs_1_, f32[2,8,256]{2,1,0:T(8,128)S(1)} %collective-permute-done.12.refs_2_), custom_call_target="tpu_custom_call" | custom-call | bytes 65536 | tf_op jit(solution)/shard_map/pallas_call | solution.py:47
  (26 shorter events, 0.6 us)
Async XLA Ops:
  1.0 9.0 %collective-permute-start = (f32[6,8,512]{2,1,0:T(8,128)S(1)}, f32[6,8,512]{2,1,0:T(8,128)S(1)}, u32[]{:S(2)}, u32[]{:S(2)}) collective-permute-start(f32[6,8,512]{2,1,0:T(8,128)S(1)} %get-tuple-element.24), channel_id=1, source_target_pairs={{0,8},{4,12},{8,0},{12,4},{1,9},{5,13},{9,1},{13,5},{2,10},{6,14},... | collective-permute-start | bytes 294920 | tf_op jit(solution)/shard_map/ppermute | solution.py:29
  5.1 5.2 %collective-permute-start.2 = (f32[6,8,512]{2,1,0:T(8,128)S(1)}, f32[6,8,512]{2,1,0:T(8,128)S(1)}, u32[]{:S(2)}, u32[]{:S(2)}) collective-permute-start(f32[6,8,512]{2,1,0:T(8,128)S(1)} %get-tuple-element.26), channel_id=1, source_target_pairs={{0,4},{4,0},{8,12},{12,8},{1,5},{5,1},{9,13},{13,9},{2,6},{6,2},{1... | collective-permute-start | bytes 294920 | tf_op jit(solution)/shard_map/ppermute | solution.py:29
  6.7 1.2 %collective-permute-start.3 = (f32[1,2,8,512]{3,2,1,0:T(8,128)S(1)}, f32[1,2,8,512]{3,2,1,0:T(8,128)S(1)}, u32[]{:S(2)}, u32[]{:S(2)}) collective-permute-start(f32[1,2,8,512]{3,2,1,0:T(8,128)S(1)} %shard_map.56), channel_id=1, source_target_pairs={{0,1},{1,0},{2,3},{3,2},{4,5},{5,4},{6,7},{7,6},{8,9},{9,8},{10,11... | collective-permute-start | bytes 98312 | tf_op jit(solution)/shard_map/ppermute | solution.py:29
  6.7 7.1 %collective-permute-start.1 = (f32[6,8,512]{2,1,0:T(8,128)S(1)}, f32[6,8,512]{2,1,0:T(8,128)S(1)}, u32[]{:S(2)}, u32[]{:S(2)}) collective-permute-start(f32[6,8,512]{2,1,0:T(8,128)S(1)} %get-tuple-element.25), channel_id=1, source_target_pairs={{0,12},{4,8},{8,4},{12,0},{1,13},{5,9},{9,5},{13,1},{2,14},{6,10},... | collective-permute-start | bytes 294920 | tf_op jit(solution)/shard_map/ppermute | solution.py:29
  10.4 3.9 %collective-permute-start.5 = (f32[2,2,8,512]{3,2,1,0:T(8,128)S(1)}, f32[2,2,8,512]{3,2,1,0:T(8,128)S(1)}, u32[]{:S(2)}, u32[]{:S(2)}) collective-permute-start(f32[2,2,8,512]{3,2,1,0:T(8,128)S(1)} %shard_map.59.refs_1_), channel_id=1, source_target_pairs={{0,1},{1,0},{2,3},{3,2},{4,5},{5,4},{6,7},{7,6},{8,9},{9,8},{10,11... | collective-permute-start | bytes 196616 | tf_op jit(solution)/shard_map/ppermute | solution.py:29
  13.8 1.6 %collective-permute-start.4 = (f32[1,2,8,512]{3,2,1,0:T(8,128)S(1)}, f32[1,2,8,512]{3,2,1,0:T(8,128)S(1)}, u32[]{:S(2)}, u32[]{:S(2)}) collective-permute-start(f32[1,2,8,512]{3,2,1,0:T(8,128)S(1)} %shard_map.62.refs_3_.refs_1_), channel_id=1, source_target_pairs={{0,1},{1,0},{2,3},{3,2},{4,5},{5,4},{6,7},{7,6},{8,9},{9,8},{10,11... | collective-permute-start | bytes 98312 | tf_op jit(solution)/shard_map/ppermute | solution.py:29
  14.3 1.1 %copy-start = (f32[4,8,2,512]{3,2,1,0:T(2,128)S(1)}, f32[4,8,2,512]{3,2,1,0:T(2,128)}, u32[]{:S(2)}) copy-start(f32[4,8,2,512]{3,2,1,0:T(2,128)} %refs_2_.3) | copy-start | bytes 393220
  17.7 1.9 %collective-permute-start.6 = (f32[2,2,8,512]{3,2,1,0:T(8,128)S(1)}, f32[2,2,8,512]{3,2,1,0:T(8,128)S(1)}, u32[]{:S(2)}, u32[]{:S(2)}) collective-permute-start(f32[2,2,8,512]{3,2,1,0:T(8,128)S(1)} %shard_map.67.refs_8_), channel_id=1, source_target_pairs={{0,1},{1,0},{2,3},{3,2},{4,5},{5,4},{6,7},{7,6},{8,9},{9,8},{10,11... | collective-permute-start | bytes 196616 | tf_op jit(solution)/shard_map/ppermute | solution.py:29
  19.6 1.6 %collective-permute-start.10 = (f32[2,2,8,512]{3,2,1,0:T(8,128)S(1)}, f32[2,2,8,512]{3,2,1,0:T(8,128)S(1)}, u32[]{:S(2)}, u32[]{:S(2)}) collective-permute-start(f32[2,2,8,512]{3,2,1,0:T(8,128)S(1)} %shard_map.72), channel_id=1, source_target_pairs={{0,1},{1,0},{2,3},{3,2},{4,5},{5,4},{6,7},{7,6},{8,9},{9,8},{10,11... | collective-permute-start | bytes 196616 | tf_op jit(solution)/shard_map/ppermute | solution.py:29
  19.7 4.0 %collective-permute-start.7 = (f32[2,2,8,256]{3,2,1,0:T(8,128)S(1)}, f32[2,2,8,256]{3,2,1,0:T(8,128)S(1)}, u32[]{:S(2)}, u32[]{:S(2)}) collective-permute-start(f32[2,2,8,256]{3,2,1,0:T(8,128)S(1)} %get-tuple-element.35), channel_id=1, source_target_pairs={{0,2},{2,0},{1,3},{3,1},{4,6},{6,4},{5,7},{7,5},{8,10},{10,8},{9,1... | collective-permute-start | bytes 98312 | tf_op jit(solution)/shard_map/ppermute | solution.py:29
  21.3 5.9 %collective-permute-start.11 = (f32[2,2,8,256]{3,2,1,0:T(8,128)S(1)}, f32[2,2,8,256]{3,2,1,0:T(8,128)S(1)}, u32[]{:S(2)}, u32[]{:S(2)}) collective-permute-start(f32[2,2,8,256]{3,2,1,0:T(8,128)S(1)} %get-tuple-element.40), channel_id=1, source_target_pairs={{0,2},{2,0},{1,3},{3,1},{4,6},{6,4},{5,7},{7,5},{8,10},{10,8},{9,1... | collective-permute-start | bytes 98312 | tf_op jit(solution)/shard_map/ppermute | solution.py:29
  23.7 5.5 %collective-permute-start.8 = (f32[2,8,256]{2,1,0:T(8,128)S(1)}, f32[2,8,256]{2,1,0:T(8,128)S(1)}, u32[]{:S(2)}, u32[]{:S(2)}) collective-permute-start(f32[2,8,256]{2,1,0:T(8,128)S(1)} %get-tuple-element.36), channel_id=1, source_target_pairs={{12,0},{8,4},{4,8},{0,12},{13,1},{9,5},{5,9},{1,13},{14,2},{10,6},... | collective-permute-start | bytes 49160 | tf_op jit(solution)/shard_map/ppermute | solution.py:33
  27.2 4.6 %collective-permute-start.9 = (f32[2,8,256]{2,1,0:T(8,128)S(1)}, f32[2,8,256]{2,1,0:T(8,128)S(1)}, u32[]{:S(2)}, u32[]{:S(2)}) collective-permute-start(f32[2,8,256]{2,1,0:T(8,128)S(1)} %get-tuple-element.37), channel_id=1, source_target_pairs={{8,0},{12,4},{0,8},{4,12},{9,1},{13,5},{1,9},{5,13},{10,2},{14,6},... | collective-permute-start | bytes 49160 | tf_op jit(solution)/shard_map/ppermute | solution.py:33
  27.2 4.6 %collective-permute-start.12 = (f32[2,8,256]{2,1,0:T(8,128)S(1)}, f32[2,8,256]{2,1,0:T(8,128)S(1)}, u32[]{:S(2)}, u32[]{:S(2)}) collective-permute-start(f32[2,8,256]{2,1,0:T(8,128)S(1)} %get-tuple-element.42), channel_id=1, source_target_pairs={{4,0},{0,4},{12,8},{8,12},{5,1},{1,5},{13,9},{9,13},{6,2},{2,6},{1... | collective-permute-start | bytes 49160 | tf_op jit(solution)/shard_map/ppermute | solution.py:33

commit v7 on v6

--- a/solution.py
+++ b/solution.py
@@ -457,7 +457,11 @@
     sent, middle_halo = halo_of(middle[::-1], warped)
     raw = {k: [hot_of(k, (sent,))] if keep else [] for k in middle}
     last_sent, last_halo = halo_of(groups[-1], (sent, *sum(raw.values(), [])))
-    for k in middle:
+    if keep and middle:
+        back = middle[::-1]
+        more, more_hots = ahead(back, middle_halo, sum([raw[k] for k in back], []), (last_sent,))
+        warped, hots = warped + more[::-1], hots + more_hots[::-1]
+    for k in [] if keep else middle:
         at = len(middle) - k
         after = (last_sent,) if k == 1 else warped[-1:]
         more, more_hots = ahead([k], middle_halo[at : at + 1], raw[k], after)

time: 32.6 us -> 32.5 us (level)
    pallas_call x21 -> x20, Pallas kernels: 8.96 us -> 8.81 us  [call(): pl.pallas_call(run, out_shape=out_shape, in_specs=[pl.BlockSpec(memory_sp...]
where the time goes in v7:
time: 32.5 us; the launch traced here: 32.3 us
  starting transfers between devices  13.6 us (42%)
  waiting for transfers between devices  9.76 us (30%)
  Pallas kernels  8.81 us (27%)
    ppermute x10, starting transfers between devices, to_peer(): return lax.ppermute(block, axis, pairs_of(lax.axis_size(axis), k))  9.13 us
    pallas_call x20, Pallas kernels, call(): pl.pallas_call(run, out_shape=out_shape, in_specs=[pl.BlockSpec(memory_sp...  8.81 us
    ppermute x10, waiting for transfers between devices, to_peer(): return lax.ppermute(block, axis, pairs_of(lax.axis_size(axis), k))  6.12 us
    ppermute x3, starting transfers between devices, to_origin(): lax.ppermute(block, axis, [(b, a) for a, b in pairs_of(lax.axis_size(axis...  4.45 us
    ppermute x3, waiting for transfers between devices, to_origin(): lax.ppermute(block, axis, [(b, a) for a, b in pairs_of(lax.axis_size(axis...  3.64 us
  transfers between devices with their start and end apart: 13, of which 7 were waited for; matrix products, arithmetic and copies ran while one was open for 0% of the time, Pallas kernels for 15%

profile of v7, /device:TPU:0, one launch (start us, length us, event | category | flops | bytes accessed | tf_op | source)
XLA Modules:
  0.0 32.3 jit_solution(850203120069198504)
XLA Ops:
  0.0 1.0 %shard_map.55 = (f32[6,8,512]{2,1,0:T(8,128)S(1)}, f32[6,8,512]{2,1,0:T(8,128)S(1)}, f32[6,8,512]{2,1,0:T(8,128)S(1)}, f32[6,8,512]{2,1,0:T(8,128)S(1)}) custom-call(f32[1,32,2,512]{3,2,1,0:T(2,128)} %refs_0_.1, s32[1,4,2,512]{3,2,1,0:T(2,128)} %refs_1_.1, s32[1,4,2,512]{3,2,1,0:T(2,128)} %refs_2_.2, s32[2,1,4,2,512]{4,3,2,1,0:T(2,128)} %refs_3_.2), custom_call_target="tpu_custom_call" | custom-call | bytes 196608 | tf_op jit(solution)/shard_map/pallas_call | solution.py:47
  1.0 4.1 %collective-permute-start = (f32[6,8,512]{2,1,0:T(8,128)S(1)}, f32[6,8,512]{2,1,0:T(8,128)S(1)}, u32[]{:S(2)}, u32[]{:S(2)}) collective-permute-start(f32[6,8,512]{2,1,0:T(8,128)S(1)} %get-tuple-element.26), channel_id=1, source_target_pairs={{0,8},{4,12},{8,0},{12,4},{1,9},{5,13},{9,1},{13,5},{2,10},{6,14},... | collective-permute-start | bytes 294920 | tf_op jit(solution)/shard_map/ppermute | solution.py:29
  5.1 1.6 %collective-permute-start.2 = (f32[6,8,512]{2,1,0:T(8,128)S(1)}, f32[6,8,512]{2,1,0:T(8,128)S(1)}, u32[]{:S(2)}, u32[]{:S(2)}) collective-permute-start(f32[6,8,512]{2,1,0:T(8,128)S(1)} %get-tuple-element.28), channel_id=1, source_target_pairs={{0,4},{4,0},{8,12},{12,8},{1,5},{5,1},{9,13},{13,9},{2,6},{6,2},{1... | collective-permute-start | bytes 294920 | tf_op jit(solution)/shard_map/ppermute | solution.py:29
  6.7 0.5 %shard_map.57.refs_2_ = bf16[2,256,2048]{2,1,0:T(8,128)(2,1)S(1)} custom-call(f32[6,8,512]{2,1,0:T(8,128)S(1)} %get-tuple-element.29.refs_0_), custom_call_target="tpu_custom_call" | custom-call | flops 83886080 | bytes 98304 | tf_op jit(solution)/shard_map/pallas_call | solution.py:47
  7.2 0.7 %collective-permute-done.3.refs_1_ = f32[1,2,8,512]{3,2,1,0:T(8,128)S(1)} collective-permute-done((f32[1,2,8,512]{3,2,1,0:T(8,128)S(1)}, f32[1,2,8,512]{3,2,1,0:T(8,128)S(1)}, u32[]{:S(2)}, u32[]{:S(2)}) %collective-permute-start.3) | collective-permute-done | bytes 32800 | tf_op jit(solution)/shard_map/ppermute | solution.py:29
  7.9 0.8 %shard_map.58 = (f32[4,2,8,512]{3,2,1,0:T(8,128)S(1)}, bf16[2,2048,256]{2,1,0:T(8,128)(2,1)S(1)}) custom-call(f32[6,8,512]{2,1,0:T(8,128)S(1)} %get-tuple-element.29.refs_0_, f32[1,2,8,512]{3,2,1,0:T(8,128)S(1)} %collective-permute-done.3.refs_1_, bf16[2,256,2048]{2,1,0:T(8,128)(2,1)S(1)} %shard_map.57.refs_2_), custom_call_target="tpu_custom_call" | custom-call | flops 335544320 | bytes 4325376 | tf_op jit(solution)/shard_map/pallas_call | solution.py:47
  8.7 1.3 %collective-permute-done.refs_0_ = f32[6,8,512]{2,1,0:T(8,128)S(1)} collective-permute-done((f32[6,8,512]{2,1,0:T(8,128)S(1)}, f32[6,8,512]{2,1,0:T(8,128)S(1)}, u32[]{:S(2)}, u32[]{:S(2)}) %collective-permute-start) | collective-permute-done | bytes 98336 | tf_op jit(solution)/shard_map/ppermute | solution.py:29
  10.0 0.4 %collective-permute-done.2.refs_1_.refs_0_ = f32[6,8,512]{2,1,0:T(8,128)S(1)} collective-permute-done((f32[6,8,512]{2,1,0:T(8,128)S(1)}, f32[6,8,512]{2,1,0:T(8,128)S(1)}, u32[]{:S(2)}, u32[]{:S(2)}) %collective-permute-start.2) | collective-permute-done | bytes 98336 | tf_op jit(solution)/shard_map/ppermute | solution.py:29
  10.4 0.5 %shard_map.61.refs_3_.refs_7_ = bf16[2,256,2048]{2,1,0:T(8,128)(2,1)S(1)} custom-call(f32[6,8,512]{2,1,0:T(8,128)S(1)} %collective-permute-done.refs_0_, f32[2,2,8,512]{3,2,1,0:T(8,128)S(1)} %shard_map.59.refs_1_), custom_call_target="tpu_custom_call" | custom-call | flops 83886080 | bytes 98304 | tf_op jit(solution)/shard_map/pallas_call | solution.py:47
  10.9 0.5 %shard_map.60.refs_2_.refs_4_.refs_7_ = bf16[2,256,2048]{2,1,0:T(8,128)(2,1)S(1)} custom-call(f32[6,8,512]{2,1,0:T(8,128)S(1)} %collective-permute-done.2.refs_1_.refs_0_, f32[2,2,8,512]{3,2,1,0:T(8,128)S(1)} %shard_map.59.refs_1_), custom_call_target="tpu_custom_call" | custom-call | flops 83886080 | bytes 98304 | tf_op jit(solution)/shard_map/pallas_call | solution.py:47
  11.3 2.5 %collective-permute-done.1.refs_0_.refs_1_ = f32[6,8,512]{2,1,0:T(8,128)S(1)} collective-permute-done((f32[6,8,512]{2,1,0:T(8,128)S(1)}, f32[6,8,512]{2,1,0:T(8,128)S(1)}, u32[]{:S(2)}, u32[]{:S(2)}) %collective-permute-start.1) | collective-permute-done | bytes 98336 | tf_op jit(solution)/shard_map/ppermute | solution.py:29
  13.8 0.5 %shard_map.64.refs_8_ = bf16[2,256,2048]{2,1,0:T(8,128)(2,1)S(1)} custom-call(f32[6,8,512]{2,1,0:T(8,128)S(1)} %collective-permute-done.1.refs_0_.refs_1_, f32[1,2,8,512]{3,2,1,0:T(8,128)S(1)} %shard_map.62.refs_5_.refs_1_), custom_call_target="tpu_custom_call" | custom-call | flops 83886080 | bytes 98304 | tf_op jit(solution)/shard_map/pallas_call | solution.py:47
  14.3 0.9 %shard_map.63 = (f32[4,2,8,512]{3,2,1,0:T(8,128)S(1)}, f32[4,2,8,512]{3,2,1,0:T(8,128)S(1)}) custom-call(f32[6,8,512]{2,1,0:T(8,128)S(1)} %collective-permute-done.refs_0_, f32[6,8,512]{2,1,0:T(8,128)S(1)} %collective-permute-done.2.refs_1_.refs_0_, f32[2,2,8,512]{3,2,1,0:T(8,128)S(1)} %collective-permute-done.5.refs_2_, ...), custom_call_target="tpu_custom_call" | custom-call | flops 671088640 | bytes 8650752 | tf_op jit(solution)/shard_map/pallas_call | solution.py:47
  15.3 2.2 %shard_map.65 = (f32[2,2,8,512]{3,2,1,0:T(8,128)S(1)}, f32[2,2,8,512]{3,2,1,0:T(8,128)S(1)}, f32[4,2,8,512]{3,2,1,0:T(8,128)S(1)}) custom-call(f32[6,8,512]{2,1,0:T(8,128)S(1)} %collective-permute-done.refs_0_, f32[6,8,512]{2,1,0:T(8,128)S(1)} %collective-permute-done.1.refs_0_.refs_1_, f32[1,2,8,512]{3,2,1,0:T(8,128)S(1)} %collective-permute-done.4.refs_2_, ...), custom_call_target="tpu_custom_call" | custom-call | flops 1006632960 | bytes 9142272 | tf_op jit(solution)/shard_map/pallas_call | solution.py:47
  17.5 0.6 %collective-permute-start.6 = (f32[2,2,8,512]{3,2,1,0:T(8,128)S(1)}, f32[2,2,8,512]{3,2,1,0:T(8,128)S(1)}, u32[]{:S(2)}, u32[]{:S(2)}) collective-permute-start(f32[2,2,8,512]{3,2,1,0:T(8,128)S(1)} %shard_map.66.refs_8_), channel_id=1, source_target_pairs={{0,1},{1,0},{2,3},{3,2},{4,5},{5,4},{6,7},{7,6},{8,9},{9,8},{10,11... | collective-permute-start | bytes 196616 | tf_op jit(solution)/shard_map/ppermute | solution.py:29
  18.1 1.3 %shard_map.67 = (f32[2,2,8,512]{3,2,1,0:T(8,128)S(1)}, f32[2,2,8,512]{3,2,1,0:T(8,128)S(1)}) custom-call(f32[6,8,512]{2,1,0:T(8,128)S(1)} %get-tuple-element.29.refs_0_, f32[6,8,512]{2,1,0:T(8,128)S(1)} %collective-permute-done.2.refs_1_.refs_0_, f32[4,8,2,512]{3,2,1,0:T(2,128)S(1)} %copy-done, f32[4,2,8,512]{3,2,1,0:T(8,128)S(1)} %get-tuple-element.35.refs_3_, ...), custom_call_target="tpu_custom_call" | custom-call | flops 671088640 | bytes 9109504 | tf_op jit(solution)/shard_map/pallas_call | solution.py:47
  19.6 1.5 %collective-permute-start.7 = (f32[2,2,8,256]{3,2,1,0:T(8,128)S(1)}, f32[2,2,8,256]{3,2,1,0:T(8,128)S(1)}, u32[]{:S(2)}, u32[]{:S(2)}) collective-permute-start(f32[2,2,8,256]{3,2,1,0:T(8,128)S(1)} %get-tuple-element.39), channel_id=1, source_target_pairs={{0,2},{2,0},{1,3},{3,1},{4,6},{6,4},{5,7},{7,5},{8,10},{10,8},{9,1... | collective-permute-start | bytes 98312 | tf_op jit(solution)/shard_map/ppermute | solution.py:29
  21.1 1.2 %collective-permute-start.11 = (f32[2,2,8,256]{3,2,1,0:T(8,128)S(1)}, f32[2,2,8,256]{3,2,1,0:T(8,128)S(1)}, u32[]{:S(2)}, u32[]{:S(2)}) collective-permute-start(f32[2,2,8,256]{3,2,1,0:T(8,128)S(1)} %get-tuple-element.44), channel_id=1, source_target_pairs={{0,2},{2,0},{1,3},{3,1},{4,6},{6,4},{5,7},{7,5},{8,10},{10,8},{9,1... | collective-permute-start | bytes 98312 | tf_op jit(solution)/shard_map/ppermute | solution.py:29
  22.4 1.2 %collective-permute-done.7.refs_1_ = f32[2,2,8,256]{3,2,1,0:T(8,128)S(1)} collective-permute-done((f32[2,2,8,256]{3,2,1,0:T(8,128)S(1)}, f32[2,2,8,256]{3,2,1,0:T(8,128)S(1)}, u32[]{:S(2)}, u32[]{:S(2)}) %collective-permute-start.7) | collective-permute-done | bytes 32800 | tf_op jit(solution)/shard_map/ppermute | solution.py:29
  23.5 3.5 %collective-permute-start.8 = (f32[2,8,256]{2,1,0:T(8,128)S(1)}, f32[2,8,256]{2,1,0:T(8,128)S(1)}, u32[]{:S(2)}, u32[]{:S(2)}) collective-permute-start(f32[2,8,256]{2,1,0:T(8,128)S(1)} %get-tuple-element.40), channel_id=1, source_target_pairs={{12,0},{8,4},{4,8},{0,12},{13,1},{9,5},{5,9},{1,13},{14,2},{10,6},... | collective-permute-start | bytes 49160 | tf_op jit(solution)/shard_map/ppermute | solution.py:33
  27.0 1.0 %collective-permute-start.12 = (f32[2,8,256]{2,1,0:T(8,128)S(1)}, f32[2,8,256]{2,1,0:T(8,128)S(1)}, u32[]{:S(2)}, u32[]{:S(2)}) collective-permute-start(f32[2,8,256]{2,1,0:T(8,128)S(1)} %get-tuple-element.46), channel_id=1, source_target_pairs={{4,0},{0,4},{12,8},{8,12},{5,1},{1,5},{13,9},{9,13},{6,2},{2,6},{1... | collective-permute-start | bytes 49160 | tf_op jit(solution)/shard_map/ppermute | solution.py:33
  28.0 1.1 %collective-permute-done.8.refs_0_ = f32[2,8,256]{2,1,0:T(8,128)S(1)} collective-permute-done((f32[2,8,256]{2,1,0:T(8,128)S(1)}, f32[2,8,256]{2,1,0:T(8,128)S(1)}, u32[]{:S(2)}, u32[]{:S(2)}) %collective-permute-start.8) | collective-permute-done | bytes 16416 | tf_op jit(solution)/shard_map/ppermute | solution.py:33
  29.1 2.6 %collective-permute-done.9.refs_1_ = f32[2,8,256]{2,1,0:T(8,128)S(1)} collective-permute-done((f32[2,8,256]{2,1,0:T(8,128)S(1)}, f32[2,8,256]{2,1,0:T(8,128)S(1)}, u32[]{:S(2)}, u32[]{:S(2)}) %collective-permute-start.9) | collective-permute-done | bytes 16416 | tf_op jit(solution)/shard_map/ppermute | solution.py:33
  31.6 0.7 %shard_map.74 = f32[1,32,2,256]{3,2,1,0:T(2,128)} custom-call(f32[2,2,8,256]{3,2,1,0:T(8,128)S(1)} %shard_map.70.refs_0_, f32[2,8,256]{2,1,0:T(8,128)S(1)} %get-tuple-element.45.refs_1_, f32[2,8,256]{2,1,0:T(8,128)S(1)} %collective-permute-done.12.refs_2_), custom_call_target="tpu_custom_call" | custom-call | bytes 65536 | tf_op jit(solution)/shard_map/pallas_call | solution.py:47
  (24 shorter events, 0.2 us)
Async XLA Ops:
  1.0 9.0 %collective-permute-start = (f32[6,8,512]{2,1,0:T(8,128)S(1)}, f32[6,8,512]{2,1,0:T(8,128)S(1)}, u32[]{:S(2)}, u32[]{:S(2)}) collective-permute-start(f32[6,8,512]{2,1,0:T(8,128)S(1)} %get-tuple-element.26), channel_id=1, source_target_pairs={{0,8},{4,12},{8,0},{12,4},{1,9},{5,13},{9,1},{13,5},{2,10},{6,14},... | collective-permute-start | bytes 294920 | tf_op jit(solution)/shard_map/ppermute | solution.py:29
  5.1 5.2 %collective-permute-start.2 = (f32[6,8,512]{2,1,0:T(8,128)S(1)}, f32[6,8,512]{2,1,0:T(8,128)S(1)}, u32[]{:S(2)}, u32[]{:S(2)}) collective-permute-start(f32[6,8,512]{2,1,0:T(8,128)S(1)} %get-tuple-element.28), channel_id=1, source_target_pairs={{0,4},{4,0},{8,12},{12,8},{1,5},{5,1},{9,13},{13,9},{2,6},{6,2},{1... | collective-permute-start | bytes 294920 | tf_op jit(solution)/shard_map/ppermute | solution.py:29
  6.7 1.2 %collective-permute-start.3 = (f32[1,2,8,512]{3,2,1,0:T(8,128)S(1)}, f32[1,2,8,512]{3,2,1,0:T(8,128)S(1)}, u32[]{:S(2)}, u32[]{:S(2)}) collective-permute-start(f32[1,2,8,512]{3,2,1,0:T(8,128)S(1)} %shard_map.56), channel_id=1, source_target_pairs={{0,1},{1,0},{2,3},{3,2},{4,5},{5,4},{6,7},{7,6},{8,9},{9,8},{10,11... | collective-permute-start | bytes 98312 | tf_op jit(solution)/shard_map/ppermute | solution.py:29
  6.7 7.1 %collective-permute-start.1 = (f32[6,8,512]{2,1,0:T(8,128)S(1)}, f32[6,8,512]{2,1,0:T(8,128)S(1)}, u32[]{:S(2)}, u32[]{:S(2)}) collective-permute-start(f32[6,8,512]{2,1,0:T(8,128)S(1)} %get-tuple-element.27), channel_id=1, source_target_pairs={{0,12},{4,8},{8,4},{12,0},{1,13},{5,9},{9,5},{13,1},{2,14},{6,10},... | collective-permute-start | bytes 294920 | tf_op jit(solution)/shard_map/ppermute | solution.py:29
  10.4 3.9 %collective-permute-start.5 = (f32[2,2,8,512]{3,2,1,0:T(8,128)S(1)}, f32[2,2,8,512]{3,2,1,0:T(8,128)S(1)}, u32[]{:S(2)}, u32[]{:S(2)}) collective-permute-start(f32[2,2,8,512]{3,2,1,0:T(8,128)S(1)} %shard_map.59.refs_1_), channel_id=1, source_target_pairs={{0,1},{1,0},{2,3},{3,2},{4,5},{5,4},{6,7},{7,6},{8,9},{9,8},{10,11... | collective-permute-start | bytes 196616 | tf_op jit(solution)/shard_map/ppermute | solution.py:29
  13.8 1.4 %collective-permute-start.4 = (f32[1,2,8,512]{3,2,1,0:T(8,128)S(1)}, f32[1,2,8,512]{3,2,1,0:T(8,128)S(1)}, u32[]{:S(2)}, u32[]{:S(2)}) collective-permute-start(f32[1,2,8,512]{3,2,1,0:T(8,128)S(1)} %shard_map.62.refs_5_.refs_1_), channel_id=1, source_target_pairs={{0,1},{1,0},{2,3},{3,2},{4,5},{5,4},{6,7},{7,6},{8,9},{9,8},{10,11... | collective-permute-start | bytes 98312 | tf_op jit(solution)/shard_map/ppermute | solution.py:29
  14.3 1.0 %copy-start = (f32[4,8,2,512]{3,2,1,0:T(2,128)S(1)}, f32[4,8,2,512]{3,2,1,0:T(2,128)}, u32[]{:S(2)}) copy-start(f32[4,8,2,512]{3,2,1,0:T(2,128)} %refs_2_.3) | copy-start | bytes 393220
  17.5 1.9 %collective-permute-start.6 = (f32[2,2,8,512]{3,2,1,0:T(8,128)S(1)}, f32[2,2,8,512]{3,2,1,0:T(8,128)S(1)}, u32[]{:S(2)}, u32[]{:S(2)}) collective-permute-start(f32[2,2,8,512]{3,2,1,0:T(8,128)S(1)} %shard_map.66.refs_8_), channel_id=1, source_target_pairs={{0,1},{1,0},{2,3},{3,2},{4,5},{5,4},{6,7},{7,6},{8,9},{9,8},{10,11... | collective-permute-start | bytes 196616 | tf_op jit(solution)/shard_map/ppermute | solution.py:29
  19.5 1.6 %collective-permute-start.10 = (f32[2,2,8,512]{3,2,1,0:T(8,128)S(1)}, f32[2,2,8,512]{3,2,1,0:T(8,128)S(1)}, u32[]{:S(2)}, u32[]{:S(2)}) collective-permute-start(f32[2,2,8,512]{3,2,1,0:T(8,128)S(1)} %shard_map.71), channel_id=1, source_target_pairs={{0,1},{1,0},{2,3},{3,2},{4,5},{5,4},{6,7},{7,6},{8,9},{9,8},{10,11... | collective-permute-start | bytes 196616 | tf_op jit(solution)/shard_map/ppermute | solution.py:29
  19.6 4.0 %collective-permute-start.7 = (f32[2,2,8,256]{3,2,1,0:T(8,128)S(1)}, f32[2,2,8,256]{3,2,1,0:T(8,128)S(1)}, u32[]{:S(2)}, u32[]{:S(2)}) collective-permute-start(f32[2,2,8,256]{3,2,1,0:T(8,128)S(1)} %get-tuple-element.39), channel_id=1, source_target_pairs={{0,2},{2,0},{1,3},{3,1},{4,6},{6,4},{5,7},{7,5},{8,10},{10,8},{9,1... | collective-permute-start | bytes 98312 | tf_op jit(solution)/shard_map/ppermute | solution.py:29
  21.1 5.9 %collective-permute-start.11 = (f32[2,2,8,256]{3,2,1,0:T(8,128)S(1)}, f32[2,2,8,256]{3,2,1,0:T(8,128)S(1)}, u32[]{:S(2)}, u32[]{:S(2)}) collective-permute-start(f32[2,2,8,256]{3,2,1,0:T(8,128)S(1)} %get-tuple-element.44), channel_id=1, source_target_pairs={{0,2},{2,0},{1,3},{3,1},{4,6},{6,4},{5,7},{7,5},{8,10},{10,8},{9,1... | collective-permute-start | bytes 98312 | tf_op jit(solution)/shard_map/ppermute | solution.py:29
  23.5 5.5 %collective-permute-start.8 = (f32[2,8,256]{2,1,0:T(8,128)S(1)}, f32[2,8,256]{2,1,0:T(8,128)S(1)}, u32[]{:S(2)}, u32[]{:S(2)}) collective-permute-start(f32[2,8,256]{2,1,0:T(8,128)S(1)} %get-tuple-element.40), channel_id=1, source_target_pairs={{12,0},{8,4},{4,8},{0,12},{13,1},{9,5},{5,9},{1,13},{14,2},{10,6},... | collective-permute-start | bytes 49160 | tf_op jit(solution)/shard_map/ppermute | solution.py:33
  27.0 4.6 %collective-permute-start.9 = (f32[2,8,256]{2,1,0:T(8,128)S(1)}, f32[2,8,256]{2,1,0:T(8,128)S(1)}, u32[]{:S(2)}, u32[]{:S(2)}) collective-permute-start(f32[2,8,256]{2,1,0:T(8,128)S(1)} %get-tuple-element.41), channel_id=1, source_target_pairs={{8,0},{12,4},{0,8},{4,12},{9,1},{13,5},{1,9},{5,13},{10,2},{14,6},... | collective-permute-start | bytes 49160 | tf_op jit(solution)/shard_map/ppermute | solution.py:33
  27.0 4.6 %collective-permute-start.12 = (f32[2,8,256]{2,1,0:T(8,128)S(1)}, f32[2,8,256]{2,1,0:T(8,128)S(1)}, u32[]{:S(2)}, u32[]{:S(2)}) collective-permute-start(f32[2,8,256]{2,1,0:T(8,128)S(1)} %get-tuple-element.46), channel_id=1, source_target_pairs={{4,0},{0,4},{12,8},{8,12},{5,1},{1,5},{13,9},{9,13},{6,2},{2,6},{1... | collective-permute-start | bytes 49160 | tf_op jit(solution)/shard_map/ppermute | solution.py:33
